TPU v7x, 128 devices: a whole 4x4x4 slice. The times are simulated.
128 devices in a mesh: shard: 32 (over x, y, core), rep: 4 (over z).
Axes of the slice: x: 4, y: 4, z: 4, core: 2. Of those that a mesh axis runs over, the one named last changes fastest.
Arguments:
- queries: bfloat16 [24576, 256], P(('shard', 'rep')), may hold values from -6 to 6
- item_owner: int32 [24576, 1], P(('shard', 'rep')), may hold values from 0 to 31; in each aligned block of 192 rows (0 to 191, 192 to 383, ...) at most 12 rows name the same one
- item_row: int32 [24576], P(('shard', 'rep')), may hold values from 0 to 2047
- log_freq: bfloat16 [24576], P(('shard', 'rep')), may hold values from -9 to -3
- table: float32 [65536, 256], P('shard'), may hold values from -6 to 6
- accum: float32 [65536, 256], P('shard'), may hold values from 0.001 to 0.1
- w_in: bfloat16 [256, 512], replicated, may hold values from -0.375 to 0.375
- w_out: bfloat16 [512, 256], replicated, may hold values from -0.25 to 0.25
Outputs:
- query_grad: float32 [24576, 256], P(('shard', 'rep'))
- table_new: float32 [65536, 256], P('shard')
- accum_new: float32 [65536, 256], P('shard')
- w_in_grad: float32 [256, 512], replicated
- w_out_grad: float32 [512, 256], replicated
Inputs may be any that keep to these rules, and one draw needn't show every extreme that they name: `item_owner`: among the pairs of one device no owner is named more than 12 times, a bound that some block reaches.
All inputs are finite; a program needn't handle non-finite values.
Results may differ from a plain program's by a relative error of at most 0.0039.
The roundings to bfloat16 on the way count: a program that leaves them out, or rounds other values in their place, can miss the bound.
Values may be sent and summed in bfloat16 or wider, within the bound.
No kernel may reach another device: no remote copies, remote signals or barrier semaphores. Data moves between devices by JAX's collectives and lax.ppermute only.
A program may use at most 128 MiB of HBM per device.

v0:
```python
import jax
import jax.numpy as jnp
from jax import lax
from jax.sharding import PartitionSpec as P

score_scale = 0.0625
learn_rate = 0.1


def local(queries, item_owner, item_row, log_freq, table, accum, w_in, w_out):
    pairs = queries.shape[0]
    width = queries.shape[1]
    owners = lax.axis_size("shard")
    capacity = max(2, 2 * pairs // owners)
    owner = item_owner[:, 0]
    onehot = (owner[:, None] == jnp.arange(owners, dtype=jnp.int32)[None, :]).astype(jnp.int32)
    before = jnp.cumsum(onehot, axis=0) - onehot
    slot = jnp.sum(before * onehot, axis=1)
    place = owner * capacity + slot
    request = (
        jnp.full((owners * capacity,), -1, jnp.int32)
        .at[place]
        .set(item_row)
        .reshape(owners, capacity)
    )
    asked = lax.all_to_all(request, "shard", split_axis=0, concat_axis=0, tiled=True)
    valid = asked >= 0
    picked = jnp.take(table, jnp.maximum(asked, 0), axis=0)
    picked = jnp.where(valid[..., None], picked, 0.0).astype(jnp.bfloat16)
    asked, fetched = (
        asked,
        lax.all_to_all(picked, "shard", split_axis=0, concat_axis=0, tiled=True),
    )
    emb = fetched.reshape(owners * capacity, width)[place]
    hidden = jax.nn.relu(jnp.dot(emb, w_in, preferred_element_type=jnp.float32)).astype(
        jnp.bfloat16
    )
    vec = (
        emb.astype(jnp.float32) + jnp.dot(hidden, w_out, preferred_element_type=jnp.float32)
    ).astype(jnp.bfloat16)
    all_vec, all_freq = (
        lax.all_gather(vec, ("shard", "rep"), axis=0, tiled=True),
        lax.all_gather(log_freq, ("shard", "rep"), axis=0, tiled=True),
    )
    total_pairs = all_vec.shape[0]
    start = lax.axis_index(("shard", "rep")) * pairs
    scores = (
        jnp.einsum("pe,be->pb", queries, all_vec, preferred_element_type=jnp.float32) * score_scale
    )
    scores = scores - all_freq.astype(jnp.float32)[None, :]
    top = jnp.max(scores, axis=1)
    lse = top + jnp.log(jnp.sum(jnp.exp(scores - top[:, None]), axis=1))
    own_rows = start + jnp.arange(pairs, dtype=jnp.int32)
    matches = own_rows[:, None] == jnp.arange(total_pairs, dtype=jnp.int32)[None, :]
    coef = (jnp.exp(scores - lse[:, None]) - matches.astype(jnp.float32)).astype(jnp.bfloat16)
    query_grad = jnp.dot(coef, all_vec, preferred_element_type=jnp.float32) * score_scale
    all_queries = lax.all_gather(queries, ("shard", "rep"), axis=0, tiled=True)
    all_lse = lax.all_gather(lse, ("shard", "rep"), axis=0, tiled=True)
    cross = (
        jnp.einsum("be,pe->bp", all_queries, vec, preferred_element_type=jnp.float32) * score_scale
    )
    cross = cross - log_freq.astype(jnp.float32)[None, :]
    back = (jnp.exp(cross - all_lse[:, None]) - matches.T.astype(jnp.float32)).astype(jnp.bfloat16)
    vec_grad = (
        jnp.einsum("bp,be->pe", back, all_queries, preferred_element_type=jnp.float32) * score_scale
    ).astype(jnp.bfloat16)
    active = (hidden > 0).astype(jnp.float32)
    hidden_grad = (
        jnp.einsum("pe,he->ph", vec_grad, w_out, preferred_element_type=jnp.float32) * active
    ).astype(jnp.bfloat16)
    emb_grad = vec_grad.astype(jnp.float32) + jnp.einsum(
        "ph,eh->pe", hidden_grad, w_in, preferred_element_type=jnp.float32
    )
    w_out_part = jnp.einsum("ph,pe->he", hidden, vec_grad, preferred_element_type=jnp.float32)
    w_in_part = jnp.einsum("pe,ph->eh", emb, hidden_grad, preferred_element_type=jnp.float32)
    w_in_grad, w_out_grad = lax.psum((w_in_part, w_out_part), ("shard", "rep"))
    outgoing = (
        jnp.zeros((owners * capacity, width), jnp.float32)
        .at[place]
        .set(emb_grad)
        .reshape(owners, capacity, width)
    )
    returned = lax.all_to_all(outgoing, "shard", split_axis=0, concat_axis=0, tiled=True)
    flat_ids = asked.reshape(-1)
    flat_vals = returned.reshape(-1, width)
    local_sum = jnp.zeros(table.shape, jnp.float32).at[jnp.maximum(flat_ids, 0)].add(flat_vals)
    row_grad = lax.psum(local_sum, "rep")
    accum_new = accum + row_grad * row_grad
    table_new = table - learn_rate * row_grad / jnp.sqrt(accum_new)
    return (query_grad, table_new, accum_new, w_in_grad, w_out_grad)


def solution(mesh):
    return jax.shard_map(
        local,
        mesh=mesh,
        in_specs=(
            P(("shard", "rep"), None),
            P(("shard", "rep"), None),
            P(("shard", "rep")),
            P(("shard", "rep")),
            P("shard", None),
            P("shard", None),
            P(),
            P(),
        ),
        out_specs=(P(("shard", "rep"), None), P("shard", None), P("shard", None), P(), P()),
        check_vma=False,
    )
```

profile of v0, /device:TPU:1, one launch (start us, length us, event | category | flops | bytes accessed | tf_op | source)
XLA Modules:
  0.0 596.5 jit_solution(13888864536576366947)
XLA Ops:
  7.2 0.0 copy-start
  7.2 0.7 iota_compare_fusion.2
  7.9 0.6 reduce-window.6
  8.5 0.2 slice_reduce_fusion
  8.7 0.1 bitcast_bitcast_fusion
  8.8 0.7 fusion.26
  9.5 0.7 compare_select_fusion
  10.2 1.3 scatter_custom_fusion
  11.6 0.1 all_to_all.12
  11.7 15.3 %all_to_all.19 = s32[32,1,12]{2,1,0:T(1,128)S(1)} all-to-all(s32[32,1,12]{2,1,0:T(1,128)S(1)} %bitcast.59), channel_id=1, replica_groups=mesh['shard'=32,'rep'=4] {'shard'}, dimensions={0} | all-to-all | bytes 3072 | tf_op jit(solution)/shard_map/all_to_all | solution.py:26
  27.0 0.1 copy.21
  27.1 0.1 copy.25
  27.2 0.1 reshape.100
  27.3 3.3 gather_fusion
  30.6 0.1 copy.24
  30.7 0.1 copy.22
  30.8 0.9 select_convert_fusion
  31.8 4.2 all-to-all-start.1
  35.9 0.0 all-gather.3.cloned.1.call-start
  36.0 9.0 %all-to-all-done.1 = bf16[32,12,256]{2,1,0:T(8,128)(2,1)S(1)} async-done(((bf16[32,12,256]{2,1,0:T(8,128)(2,1)}), bf16[32,12,256]{2,1,0:T(8,128)(2,1)S(1)}, u32[]{:S(2)}, u32[]{:S(2)}) %all-to-all-start.1) | async-done | bytes 196640 | tf_op jit(solution)/shard_map/all_to_all | solution.py:32
  45.1 1.0 gather_fusion.1
  46.1 1.2 fusion.13
  47.3 0.0 copy-done
  47.3 0.9 fusion.20
  48.1 0.0 all-gather.3.cloned.1.call-update
  48.1 0.0 all-gather.5.cloned.1.call-start
  48.2 0.7 all-gather.5.cloned.1.call-update
  48.9 0.0 all-reduce.10.cloned.1.call-start
  49.0 0.9 dynamic-update-slice
  49.8 67.0 %all-reduce.1 = bf16[24576]{0:T(1024)(128)(2,1)S(1)} all-reduce(bf16[24576]{0:T(1024)(128)(2,1)S(1)} %dynamic-update-slice), channel_id=1, replica_groups=mesh['shard'=32,'rep'=4] {'shard','rep'}, use_global_device_ids=true, to_apply=%add.1 | all-reduce | flops 24576 | bytes 98304
  116.8 4.4 all-gather.3.cloned.1.call-done
  121.2 15.3 %fusion.31 = (f32[192]{0:T(256)S(1)}, f32[24576,192]{0,1:T(8,128)}) fusion(f32[24576]{0:T(1024)S(1)} %convert_element_type.49, bf16[24576,256]{1,0:T(8,128)(2,1)} %all-gather.3.cloned.1.call-done, bf16[192,256]{1,0:T(8,128)(2,1)} %param.8), kind=kOutput, calls=%fused_computation.62 | convolution fusion | flops 2430074624 | bytes 31654656 | tf_op jit(solution)/shard_map/pe,be->pb/dot_general | solution.py:48
  136.5 0.0 copy-start.5
  136.5 0.0 copy-start.3
  136.5 9.1 %exponential_reduce_fusion = f32[192]{0:T(256)S(1)} fusion(f32[24576,192]{0,1:T(8,128)} %get-tuple-element.14, f32[192]{0:T(256)S(1)} %get-tuple-element.13), kind=kLoop, calls=%fused_computation.18 | loop fusion | flops 9436992 | bytes 18875904 | tf_op jit(solution)/shard_map/reduce_sum | solution.py:52
  145.6 0.1 fusion.30
  145.8 0.6 copy-done.4
  146.4 0.0 all-reduce.10.cloned.1.call-update
  146.4 0.2 all-reduce.8.cloned.1.call-start
  146.7 0.0 copy-done.5
  146.7 0.0 copy-start.2
  146.7 50.2 %all-gather.5.cloned.1.call-done = bf16[24576,256]{1,0:T(8,128)(2,1)} async-done(((bf16[192,256]{1,0:T(8,128)(2,1)}), bf16[24576,256]{1,0:T(8,128)(2,1)}) %all-gather.5.cloned.1.call-update) | async-done | bytes 12582928 | tf_op jit(solution)/shard_map/all_gather | solution.py:57
  196.9 142.8 %all-reduce.10.cloned.1.call-done = f32[24576]{0:T(1024)} async-done(((f32[24576]{0:T(1024)}), f32[24576]{0:T(1024)}) %all-reduce.10.cloned.1.call-update) | async-done | bytes 98320
  339.7 0.0 copy-done.3
  339.7 16.5 %fusion.19 = bf16[192,256]{1,0:T(8,128)(2,1)S(1)} fusion(bf16[24576,256]{1,0:T(8,128)(2,1)} %all-gather.5.cloned.1.call-done, bf16[192,256]{1,0:T(8,128)(2,1)S(1)} %copy-done.3, s32[192]{0:T(256)S(1)} %iota_add_fusion, f32[24576]{0:T(1024)} %all-reduce.10.cloned.1.call-done, f32[192]{0:T(256)S(1)} %convert_element_type.52), kind=kOutput, calls=%fused_computation.33 | convolution fusion | flops 4864966656 | bytes 12879360 | tf_op jit(solution)/shard_map/bp,be->pe/dot_general | solution.py:65
  356.2 0.2 fusion.14
  356.5 0.0 copy-done.2
  356.5 0.2 convolution_add_fusion
  356.7 1.3 scatter_custom_fusion.1
  358.1 17.0 %all_to_all.20 = f32[32,12,256]{2,1,0:T(8,128)S(1)} all-to-all(f32[32,12,256]{2,1,0:T(8,128)S(1)} %reshape.95), channel_id=1, replica_groups=mesh['shard'=32,'rep'=4] {'shard'}, dimensions={0} | all-to-all | bytes 786432 | tf_op jit(solution)/shard_map/all_to_all | solution.py:83
  375.1 4.0 scatter_custom_fusion.2
  379.2 0.0 all-reduce.8.cloned.1.call-update
  379.2 0.3 all-reduce.12.cloned.1.call-start
  379.5 0.0 copy-start.1
  379.5 15.9 %fusion.15 = f32[192,256]{1,0:T(8,128)} fusion(bf16[24576,256]{1,0:T(8,128)(2,1)} %all-gather.3.cloned.1.call-done, f32[24576,192]{0,1:T(8,128)} %get-tuple-element.14, s32[192]{0:T(256)S(1)} %iota_add_fusion, f32[192]{0:T(256)S(1)} %get-tuple-element.10), kind=kOutput, calls=%fused_computation.29 | convolution fusion | flops 2439561216 | bytes 31655424 | tf_op jit(solution)/shard_map/dot_general | solution.py:56
  395.4 1.0 fusion.32
  396.5 1.1 fusion.33
  397.5 0.0 all-reduce.12.cloned.1.call-update
  397.5 36.1 %all-reduce.8.cloned.1.call-done = f32[2048,256]{1,0:T(8,128)} async-done(((f32[2048,256]{1,0:T(8,128)}), f32[2048,256]{1,0:T(8,128)}) %all-reduce.8.cloned.1.call-update) | async-done | bytes 2097168 | tf_op jit(solution)/shard_map/psum | solution.py:87
  433.6 0.0 copy-done.1
  433.6 4.7 multiply_subtract_fusion
  438.3 148.0 %all-reduce.12.cloned.1.call-done = (f32[256,512]{1,0:T(8,128)}, f32[512,256]{1,0:T(8,128)}) async-done(((f32[256,512]{1,0:T(8,128)}, f32[512,256]{1,0:T(8,128)}), (f32[256,512]{1,0:T(8,128)}, f32[512,256]{1,0:T(8,128)})) %all-reduce.12.cloned.1.call-update) | async-done | bytes 1048592 | tf_op jit(solution)/shard_map/psum | solution.py:76
  586.3 1.9 copy.36
  588.1 1.9 copy.37
  (17 shorter events, 0.3 us)
Async XLA Ops:
  7.2 40.1 %copy-start = (bf16[512,256]{1,0:T(8,128)(2,1)S(1)}, bf16[512,256]{1,0:T(8,128)(2,1)}, u32[]{:S(2)}) copy-start(bf16[512,256]{1,0:T(8,128)(2,1)} %param.15) | copy-start | bytes 786436
  31.8 13.3 %all-to-all-start.1 = ((bf16[32,12,256]{2,1,0:T(8,128)(2,1)}), bf16[32,12,256]{2,1,0:T(8,128)(2,1)S(1)}, u32[]{:S(2)}, u32[]{:S(2)}) async-start(bf16[32,12,256]{2,1,0:T(8,128)(2,1)} %select_convert_fusion), calls=%async_computation.1 | async-start | bytes 524288 | tf_op jit(solution)/shard_map/all_to_all | solution.py:32
  35.9 85.3 %all-gather.3.cloned.1.call-start = ((), (), s32[]{:S(2)}) async-start(), calls=%async_computation.3 | async-start | bytes 12681216 | tf_op jit(solution)/shard_map/all_gather | solution.py:42
  48.1 148.8 %all-gather.5.cloned.1.call-start = ((), (), s32[]{:S(2)}) async-start(), calls=%async_computation.4 | async-start | bytes 12681216 | tf_op jit(solution)/shard_map/all_gather | solution.py:57
  48.9 290.8 %all-reduce.10.cloned.1.call-start = ((), (), s32[]{:S(2)}) async-start(), calls=%async_computation.6 | async-start | bytes 196608
  136.5 10.2 %copy-start.5 = (bf16[192]{0:T(256)(128)(2,1)S(1)}, bf16[192]{0:T(256)(128)(2,1)}, u32[]{:S(2)}) copy-start(bf16[192]{0:T(256)(128)(2,1)} %param.11) | copy-start | bytes 1156
  136.5 203.2 %copy-start.3 = (bf16[192,256]{1,0:T(8,128)(2,1)S(1)}, bf16[192,256]{1,0:T(8,128)(2,1)}, u32[]{:S(2)}) copy-start(bf16[192,256]{1,0:T(8,128)(2,1)} %fusion.20) | copy-start | bytes 294916
  145.8 0.6 copy-start.4
  146.4 287.2 %all-reduce.8.cloned.1.call-start = ((), (), s32[]{:S(2)}) async-start(), calls=%async_computation.5 | async-start | bytes 4194304 | tf_op jit(solution)/shard_map/psum | solution.py:87
  146.7 209.8 %copy-start.2 = (bf16[256,512]{1,0:T(8,128)(2,1)S(1)}, bf16[256,512]{1,0:T(8,128)(2,1)}, u32[]{:S(2)}) copy-start(bf16[256,512]{1,0:T(8,128)(2,1)} %param.14) | copy-start | bytes 786436
  379.2 207.1 %all-reduce.12.cloned.1.call-start = ((), (), s32[]{:S(2)}) async-start(), calls=%async_computation.7 | async-start | bytes 2097152 | tf_op jit(solution)/shard_map/psum | solution.py:76
  379.5 54.1 %copy-start.1 = (f32[2048,256]{1,0:T(8,128)S(1)}, f32[2048,256]{1,0:T(8,128)}, u32[]{:S(2)}) copy-start(f32[2048,256]{1,0:T(8,128)} %param.12) | copy-start | bytes 6291460
Sparse Core Ops, SparseCore 0:
  48.3 72.9 all-gather.2
  124.3 72.5 all-gather.4
  202.3 137.4 all-reduce.9
  379.3 54.2 all-reduce.7
  439.0 147.2 all-reduce.11
where the time goes:
time: 597 us
  waiting for transfers between devices  391 us (65%)
  blocking collectives  99.3 us (17%)
  matrix products  52.3 us (9%)
  other arithmetic  21.8 us (4%)
  between operations  14 us (2%)
  local copies, waits for them, and re-layouts  13.1 us (2%)
    psum x1, waiting for transfers between devices, local(): w_in_grad, w_out_grad = lax.psum((w_in_part, w_out_part), ('shard', 'rep'))  148 us
    unnamed x6, waiting for transfers between devices  144 us
    unnamed x1, blocking collectives  67 us
    all_gather x1, waiting for transfers between devices, local(): all_queries = lax.all_gather(queries, ('shard', 'rep'), axis=0, tiled=True)  50.2 us
    psum x1, waiting for transfers between devices, local(): row_grad = lax.psum(local_sum, 'rep')  36.1 us
    all_to_all x1, blocking collectives, local(): lax.all_to_all(outgoing, 'shard', split_axis=0, concat_axis=0, tiled=True)  17 us
    dot_general x1, matrix products, local(): jnp.einsum('bp,be->pe', back, all_queries, preferred_element_type=jnp.flo...  16.5 us
    dot_general x1, matrix products, local(): jnp.dot(coef, all_vec, preferred_element_type=jnp.float32) * score_scale  15.9 us
  transfers between devices with their start and end apart: 6, of which 6 were waited for; matrix products, arithmetic and copies ran while one was open for 8% of the time, Pallas kernels for 0%

commit v1 on v0

v1 whole, which is shorter than its diff:
```python
import jax
import jax.numpy as jnp
from jax import lax
from jax.experimental import pallas as pl
from jax.experimental.pallas import tpu as pltpu
from jax.sharding import Mesh, PartitionSpec as P

E = 256
H = 512
PAIRS = 192
ROWS = 2048
CAP = 12
SLOT = 16
OWNERS = 32
NA = 16
NB = 8
QS = NA * PAIRS
VS = NB * PAIRS
LIMIT = 40 << 20
score_scale = 0.0625
learn_rate = 0.1

SHARD = ("x", "y", "c")
ALL = ("x", "y", "c", "z")
CHIPS = ("x", "y", "z")
A = ("z", "x")

f32 = jnp.float32
bf16 = jnp.bfloat16
i32 = jnp.int32
VMEM = pltpu.MemorySpace.VMEM
NT = (((1,), (1,)), ((), ()))
TN = (((0,), (0,)), ((), ()))


def mm(a, b, dims=(((1,), (0,)), ((), ()))):
    return lax.dot_general(a, b, dims, preferred_element_type=f32)


def iota(shape, axis):
    return lax.broadcasted_iota(i32, shape, axis)


def call(kernel, out_shape, *, cost=(0, 0, 0), limit=None, **kw):
    return pl.pallas_call(
        kernel,
        out_shape=out_shape,
        compiler_params=pltpu.CompilerParams(vmem_limit_bytes=limit),
        cost_estimate=pl.CostEstimate(flops=cost[0], bytes_accessed=cost[1], transcendentals=cost[2]),
        **kw,
    )


def sds(shape, dtype):
    return jax.ShapeDtypeStruct(shape, dtype)


def column(lanes, rows):
    n = lanes.shape[1]
    eye = iota((rows, n), 0) == iota((rows, n), 1)
    return jnp.sum(jnp.where(eye, lanes, jnp.zeros((), lanes.dtype)), axis=1, keepdims=True)


def slots_kernel(pair_ref, req_ref, place_ref, pick_ref, ids_ref):
    owner = pair_ref[0:1, :]
    row = pair_ref[1:2, :]
    mine = owner == iota((OWNERS, 256), 0)
    onehot = mine.astype(f32).astype(bf16)
    earlier = (iota((256, 256), 0) < iota((256, 256), 1)).astype(f32).astype(bf16)
    before = mm(onehot, earlier)
    slot = jnp.sum(jnp.where(mine, before, 0.0), axis=0, keepdims=True).astype(i32)
    here = slot == iota((128, 256), 0)
    low = jnp.where(here, (row & 255).astype(f32), 0.0).astype(bf16)
    high = jnp.where(here, ((row >> 8) + 1).astype(f32), 0.0).astype(bf16)
    lo = mm(onehot, low, NT)
    hi = mm(onehot, high, NT) - 1.0
    req_ref[...] = jnp.where(hi < 0.0, -1, (hi * 256.0 + lo).astype(i32))
    ids_ref[:, 0:128] = hi
    ids_ref[:, 128:256] = lo
    place = jnp.where(owner < 0, -1, owner * SLOT + slot)
    place_ref[...] = place
    flat = jnp.where(owner < 0, -1, owner * CAP + slot).astype(f32)
    col = column(flat, PAIRS).astype(i32)
    pick_ref[...] = (col == iota((PAIRS, OWNERS * CAP), 1)).astype(f32).astype(bf16)


def tower_kernel(got_ref, pick_ref, w_in_ref, w_out_ref, freq_ref, emb_ref, hid_ref, pay_ref):
    emb = mm(pick_ref[...], got_ref[...]).astype(bf16)
    emb_ref[...] = emb
    hid = jnp.maximum(mm(emb, w_in_ref[...]), 0.0).astype(bf16)
    hid_ref[...] = hid
    vec = (emb.astype(f32) + mm(hid, w_out_ref[...])).astype(bf16)
    pay_ref[0:PAIRS, :] = vec
    pay_ref[PAIRS : PAIRS + 16, :] = freq_ref[...]


QB = 256


def load_vecs(vec_refs, vec, freq):
    for b in range(NB):
        at = slice(b * PAIRS, (b + 1) * PAIRS)
        line = vec_refs[b][PAIRS : PAIRS + 16, :].astype(f32)[0:1, :]
        freq[at, :] = jnp.broadcast_to(column(line, PAIRS), (PAIRS, 128))
        vec[at, :] = vec_refs[b][0:PAIRS, :]


def lanes(col, n):
    return jnp.concatenate([col] * (n // 128), axis=1)


def score_kernel(*refs):
    vec_refs, (q_ref, ml_ref, vec, freq, scores) = refs[:NB], refs[NB:]

    @pl.when(pl.program_id(0) == 0)
    def _():
        load_vecs(vec_refs, vec, freq)

    q = q_ref[...] * jnp.asarray(score_scale, bf16)
    top = None
    for b in range(NB):
        at = slice(b * PAIRS, (b + 1) * PAIRS)
        s = mm(vec[at, :], q, NT) - lanes(freq[at, :], QB)
        scores[at, :] = s
        t = jnp.max(s, axis=0, keepdims=True)
        top = t if top is None else jnp.maximum(top, t)
    total = jnp.zeros((1, QB), f32)
    for b in range(NB):
        at = slice(b * PAIRS, (b + 1) * PAIRS)
        total = total + jnp.sum(jnp.exp(scores[at, :] - top), axis=0, keepdims=True)
    ml_ref[0:1, :] = top
    ml_ref[1:2, :] = total


CB = 384


def grad_kernel(pos_ref, *refs):
    vec_refs, (all_ml_ref, q_ref, o_ref, same_ref, other_ref, vec, freq, turned, lse, coef) = refs[:NB], refs[NB:]
    step = pl.program_id(0)

    @pl.when(step == 0)
    def _():
        load_vecs(vec_refs, vec, freq)
        for k in range(0, VS, 256):
            turned[:, k : k + 256] = vec[k : k + 256, :].astype(f32).T.astype(bf16)
        top = all_ml_ref[0, 0:1, :]
        for a in range(1, NA):
            top = jnp.maximum(top, all_ml_ref[a, 0:1, :])
        total = jnp.zeros((1, QS), f32)
        for a in range(NA):
            total = total + jnp.exp(all_ml_ref[a, 0:1, :] - top) * all_ml_ref[a, 1:2, :]
        whole_lse = top + jnp.log(total)
        for k in range(QS // CB):
            lse[k, :, :] = jnp.broadcast_to(whole_lse[:, k * CB : (k + 1) * CB], (8, CB))
        same_ref[...] = jnp.zeros_like(same_ref)
        other_ref[...] = jnp.zeros_like(other_ref)

    q = q_ref[...]
    scaled = q * jnp.asarray(score_scale, bf16)
    norm = lse[step][0:1, :]
    first = pos_ref[0] * PAIRS - step * CB
    for b in range(NB):
        at = slice(b * PAIRS, (b + 1) * PAIRS)
        p = jnp.exp(mm(vec[at, :], scaled, NT) - lanes(freq[at, :], CB) - norm)
        if b == 0:
            p = jnp.where(iota((PAIRS, CB), 0) + first == iota((PAIRS, CB), 1), p - 1.0, p)
        coef[at, :] = p.astype(bf16)
    o_ref[...] = mm(turned[...], coef[...]).T.astype(bf16)
    for b in range(NB):
        at = slice(b * PAIRS, (b + 1) * PAIRS)
        ref = (same_ref, other_ref)[b // 4]
        ref[b % 4] += mm(coef[at, :], q)


def back_kernel(*refs):
    parts, (emb_ref, hid_ref, w_out_ref, place_ref, ids_ref, out_ref) = refs[:4], refs[4:]
    total = parts[0][...]
    for part in parts[1:]:
        total = total + part[...]
    grad = (total * score_scale).astype(bf16)
    hid = hid_ref[...]
    hg = jnp.where(hid.astype(f32) > 0.0, mm(grad, w_out_ref[...], NT), 0.0).astype(bf16)
    scatter = (iota((OWNERS * SLOT, PAIRS), 0) == place_ref[:, 0:PAIRS]).astype(f32).astype(bf16)
    slots = mm(scatter, grad).reshape(OWNERS, SLOT, E)
    ids = ids_ref[...].reshape(OWNERS, 1, E)
    slots = jnp.where(iota((OWNERS, SLOT, E), 1) == CAP, ids, slots).astype(bf16).reshape(16, 2, SLOT, E)
    w_out_part = mm(hid, grad, TN)
    w_in_part = mm(emb_ref[...], hg, TN)
    pieces = []
    for part in (w_out_part, w_in_part):
        n = part.shape[0] // 8
        tiles = [part[:, k : k + 128].reshape(n, 1, 8, 128) for k in range(0, part.shape[1], 128)]
        pieces.append(jnp.concatenate(tiles, axis=1).reshape(16, 4, SLOT, 128).astype(bf16))
    for z in range(4):
        out_ref[:, :, z, :, 0:E] = slots
        for c in range(2):
            out_ref[:, c, z, :, E : E + 128] = pieces[c][:, z]


TB = 256


def update_kernel(ids_ref, got_ref, table_ref, accum_ref, w_in_ref, w_out_ref, table_out, accum_out):
    base = pl.program_id(0) * TB
    onehot = (ids_ref[...] == iota((TB, 128 * SLOT), 0) + base).astype(f32).astype(bf16)
    vals = got_ref[:, :, 0:E].reshape(128 * SLOT, E)
    vg = mm(onehot, vals)
    high = vg.astype(bf16)
    low = (vg - high.astype(f32)).astype(bf16)
    table = table_ref[...]
    hid = jnp.maximum(mm(table.astype(bf16), w_in_ref[...]), 0.0).astype(bf16).astype(f32)
    back = mm(high, w_out_ref[...], NT) + mm(low, w_out_ref[...], NT)
    hg = jnp.where(hid > 0.0, back, 0.0).astype(bf16)
    g = vg + mm(hg, w_in_ref[...], NT)
    acc = accum_ref[...] + g * g
    accum_out[...] = acc
    table_out[...] = table - learn_rate * g / jnp.sqrt(acc)


def a2a(x, axes):
    return lax.all_to_all(x, axes, split_axis=0, concat_axis=0, tiled=True)


def shift(x, axis, k):
    n = 2 if axis == "c" else 4
    return lax.ppermute(x, axis, [(i, (i + k) % n) for i in range(n)])


def whole(n):
    return [pl.BlockSpec(memory_space=VMEM)] * n


def const(*shape):
    return pl.BlockSpec(shape, lambda *_: (0,) * len(shape))


def local(queries, item_owner, item_row, log_freq, table, accum, w_in, w_out):
    all_q = lax.all_gather(queries, A, axis=0, tiled=True)
    here = lax.axis_index(A).astype(i32)
    here_x = lax.axis_index("x").astype(i32)
    here_z = lax.axis_index("z").astype(i32)

    pair = jnp.stack(
        [
            jnp.pad(item_owner[:, 0], (0, 256 - PAIRS), constant_values=-1),
            jnp.pad(item_row, (0, 256 - PAIRS)),
        ]
    )
    req, place, pick, ids = call(
        slots_kernel,
        (
            sds((OWNERS, 128), i32),
            sds((1, 256), i32),
            sds((PAIRS, OWNERS * CAP), bf16),
            sds((OWNERS, E), f32),
        ),
        in_specs=whole(1),
        out_specs=tuple(whole(4)),
    )(pair)
    asked = a2a(req.reshape(OWNERS, 1, 128), SHARD)
    wanted = jnp.maximum(asked[:, 0, :CAP].reshape(OWNERS * CAP), 0)
    picked = table.at[wanted].get(mode="promise_in_bounds").astype(bf16)
    got = a2a(picked.reshape(OWNERS, CAP, E), SHARD).reshape(OWNERS * CAP, E)
    freq_row = jnp.pad(log_freq.reshape(1, PAIRS), ((0, 15), (0, 256 - PAIRS)))
    emb, hid, pay = call(
        tower_kernel,
        (sds((PAIRS, E), bf16), sds((PAIRS, H), bf16), sds((PAIRS + 16, E), bf16)),
        in_specs=whole(5),
        out_specs=tuple(whole(3)),
    )(got, pick, w_in, w_out, freq_row)
    vecs = [pay] + [shift(pay, "y", k) for k in range(1, 4)]
    vecs = vecs + [shift(v, "c", 1) for v in vecs]

    ml = call(
        score_kernel,
        sds((2, QS), f32),
        cost=(2 * VS * QS * E, VS * QS * 2, VS * QS),
        limit=LIMIT,
        grid=(QS // QB,),
        in_specs=[const(PAIRS + 16, E)] * NB + [pl.BlockSpec((QB, E), lambda i: (i, 0))],
        out_specs=pl.BlockSpec((2, QB), lambda i: (0, i)),
        scratch_shapes=[pltpu.VMEM((VS, E), bf16), pltpu.VMEM((VS, 128), f32), pltpu.VMEM((VS, QB), f32)],
    )(*vecs, all_q)
    all_ml = a2a(jnp.broadcast_to(ml[None], (NA, 2, QS)), A)

    per = QS // 4 // CB
    o, same, other = call(
        grad_kernel,
        (sds((QS, E), bf16), sds((4, PAIRS, E), f32), sds((4, PAIRS, E), f32)),
        cost=(6 * VS * QS * E, VS * QS * 2, VS * QS),
        limit=LIMIT,
        grid_spec=pltpu.PrefetchScalarGridSpec(
            num_scalar_prefetch=1,
            grid=(QS // CB,),
            in_specs=[const(PAIRS + 16, E)] * NB
            + [const(NA, 2, QS), pl.BlockSpec((CB, E), lambda i, pos: (i, 0))],
            out_specs=(
                pl.BlockSpec((CB, E), lambda i, pos: (((i // per - pos[1] + 4) % 4) * per + i % per, 0)),
                const(4, PAIRS, E),
                const(4, PAIRS, E),
            ),
            scratch_shapes=[
                pltpu.VMEM((VS, E), bf16),
                pltpu.VMEM((VS, 128), f32),
                pltpu.VMEM((E, VS), bf16),
                pltpu.VMEM((QS // CB, 8, CB), f32),
                pltpu.VMEM((VS, CB), bf16),
            ],
        ),
    )(jnp.stack([here, here_z]), *vecs, all_ml, all_q)

    from_core = shift(other, "c", 1)
    sums = [same[k] + from_core[k] for k in range(4)]
    parts = [sums[0]] + [shift(sums[k], "y", 4 - k) for k in range(1, 4)]
    out = call(
        back_kernel,
        sds((16, 2, 4, SLOT, E + 128), bf16),
        limit=LIMIT,
        in_specs=whole(9),
        out_specs=whole(1)[0],
    )(*parts, emb, hid, w_out, place, ids)
    back = a2a(out.reshape(128, SLOT, E + 128), ALL)

    slab = QS // 4
    slabs = [o[:slab]] + [shift(o[k * slab : (k + 1) * slab], "z", k) for k in range(1, 4)]

    def toward(k):
        at = ((here_x + k) % 4) * PAIRS
        return sum(lax.dynamic_slice(v, (at, 0), (PAIRS, E)).astype(f32) for v in slabs)

    query_grad = toward(0)
    for k in range(1, 4):
        query_grad = query_grad + shift(toward(k), "x", k)
    query_grad = query_grad * score_scale

    w_sum = jnp.sum(back[:, :, E:].astype(f32), axis=0)
    w_mine = a2a(jnp.broadcast_to(w_sum[None], (64, SLOT, 128)), CHIPS)
    w_other = shift(w_mine, "c", 1)
    zero = lax.axis_index("c") == 0

    def tiles(x, rows, cols):
        return x.reshape(rows // 8, cols // 128, 8, 128).transpose(0, 2, 1, 3).reshape(rows, cols)

    w_out_grad = tiles(jnp.where(zero, w_mine, w_other), H, E)
    w_in_grad = tiles(jnp.where(zero, w_other, w_mine), E, H)

    hi = back[:, CAP, 0:CAP].astype(i32)
    lo = back[:, CAP, 128 : 128 + CAP].astype(i32)
    row_ids = jnp.where(hi < 0, -1, hi * 256 + lo)
    row_ids = jnp.pad(row_ids, ((0, 0), (0, SLOT - CAP)), constant_values=-1).reshape(1, 128 * SLOT)
    table_new, accum_new = call(
        update_kernel,
        (sds((ROWS, E), f32), sds((ROWS, E), f32)),
        cost=(4 * ROWS * 2048 * E, 4 * ROWS * E * 4, 0),
        limit=LIMIT,
        grid=(ROWS // TB,),
        in_specs=[
            const(1, 128 * SLOT),
            const(128, SLOT, E + 128),
            pl.BlockSpec((TB, E), lambda i: (i, 0)),
            pl.BlockSpec((TB, E), lambda i: (i, 0)),
            const(E, H),
            const(H, E),
        ],
        out_specs=(
            pl.BlockSpec((TB, E), lambda i: (i, 0)),
            pl.BlockSpec((TB, E), lambda i: (i, 0)),
        ),
    )(row_ids, back, table, accum, w_in, w_out)
    return query_grad, table_new, accum_new, w_in_grad, w_out_grad


def solution(mesh):
    fine = Mesh(mesh.devices.reshape(4, 4, 2, 4), ALL)
    return jax.shard_map(
        local,
        mesh=fine,
        in_specs=(
            P(ALL, None),
            P(ALL, None),
            P(ALL),
            P(ALL),
            P(SHARD, None),
            P(SHARD, None),
            P(),
            P(),
        ),
        out_specs=(P(ALL, None), P(SHARD, None), P(SHARD, None), P(), P()),
        check_vma=False,
    )
```

time: 597 us -> 210 us (0.35)
  waiting for transfers between devices: 391 us -> 67.6 us
  blocking collectives: 99.3 us -> 15.5 us
  matrix products: 52.3 us -> 0 us
  starting transfers between devices: 4.78 us -> 47.7 us
  Pallas kernels: 0 us -> 39.1 us
  other arithmetic: 21.8 us -> 6.44 us
    psum x2 -> x0, waiting for transfers between devices: 184 us -> none  [the longest x1 148 us: local(): w_in_grad, w_out_grad = lax.psum((w_in_part, w_out_part), ('shard', 'rep'))]
    unnamed x6 -> x1, waiting for transfers between devices: 144 us -> 0.68 us
    unnamed x1 -> x0, blocking collectives: 67 us -> none
    all_gather x2 -> x1, waiting for transfers between devices: 54.6 us -> 0.01 us  [local(): all_q = lax.all_gather(queries, A, axis=0, tiled=True)]
    dot_general x9 -> x0, matrix products: 52.3 us -> none  [the longest x1 16.5 us: local(): jnp.einsum('bp,be->pe', back, all_queries, preferred_element_type=jnp.flo...]
    pallas_call x0 -> x6, Pallas kernels: none -> 39.1 us  [the longest x1 13.4 us: local(): call(grad_kernel, (sds((QS, E), bf16), sds((4, PAIRS, E), f32), sds((4, P...]
    ppermute x0 -> x18, waiting for transfers between devices: none -> 29.1 us  [shift(): return lax.ppermute(x, axis, [(i, (i + k) % n) for i in range(n)])]
    all_to_all x1 -> x4, waiting for transfers between devices: 9.04 us -> 37.9 us  [a2a(): return lax.all_to_all(x, axes, split_axis=0, concat_axis=0, tiled=True)]
  transfers between devices with their start and end apart: 6 -> 23, of which waited for: 6 -> 14; matrix products, arithmetic and copies ran while one was open for 8% -> 7% of each run, Pallas kernels for 0% -> 7%
where the time goes in v1:
time: 210 us; the launch traced here: 209 us
  waiting for transfers between devices  67.6 us (32%)
  starting transfers between devices  47.7 us (23%)
  Pallas kernels  39.1 us (19%)
  local copies, waits for them, and re-layouts  18.5 us (9%)
  blocking collectives  15.5 us (7%)
  between operations  14.3 us (7%)
  other arithmetic  6.44 us (3%)
    all_to_all x4, waiting for transfers between devices, a2a(): return lax.all_to_all(x, axes, split_axis=0, concat_axis=0, tiled=True)  37.9 us
    ppermute x18, waiting for transfers between devices, shift(): return lax.ppermute(x, axis, [(i, (i + k) % n) for i in range(n)])  29.1 us
    all_to_all x4, starting transfers between devices, a2a(): return lax.all_to_all(x, axes, split_axis=0, concat_axis=0, tiled=True)  26.2 us
    ppermute x18, starting transfers between devices, shift(): return lax.ppermute(x, axis, [(i, (i + k) % n) for i in range(n)])  21.5 us
    all_to_all x1, blocking collectives, a2a(): return lax.all_to_all(x, axes, split_axis=0, concat_axis=0, tiled=True)  15.5 us
    pallas_call x1, Pallas kernels, local(): call(grad_kernel, (sds((QS, E), bf16), sds((4, PAIRS, E), f32), sds((4, P...  13.4 us
    pallas_call x1, Pallas kernels, local(): call(update_kernel, (sds((ROWS, E), f32), sds((ROWS, E), f32)), cost=(4 *...  10.6 us
    pallas_call x1, Pallas kernels, local(): call(score_kernel, sds((2, QS), f32), cost=(2 * VS * QS * E, VS * QS * 2,...  9.48 us
  transfers between devices with their start and end apart: 23, of which 14 were waited for; matrix products, arithmetic and copies ran while one was open for 7% of the time, Pallas kernels for 7%

profile of v1, /device:TPU:1, one launch (start us, length us, event | category | flops | bytes accessed | tf_op | source)
XLA Modules:
  0.0 209.2 jit_solution(12399553691656061617)
XLA Ops:
  7.2 0.7 all-gather.2.cloned.1.call-update
  7.9 0.7 pad.16
  8.6 0.7 pad.15
  9.3 0.6 pad_add_fusion.pair_ref
  9.9 1.6 shard_map.119
  11.5 15.5 %all_to_all.25 = s32[32,1,128]{2,1,0:T(1,128)S(1)} all-to-all(s32[32,1,128]{2,1,0:T(1,128)} %bitcast.31), channel_id=1, replica_groups=mesh['x'=4,'y'=4,'c'=2,'z'=4] {'x','y','c'}, dimensions={0} | all-to-all | bytes 32768 | tf_op jit(solution)/shard_map/all_to_all | solution.py:222
  27.0 0.1 reshape.78
  27.1 3.3 %gather_fusion = bf16[384,256]{1,0:T(8,128)(2,1)S(1)} fusion(f32[2048,256]{1,0:T(8,128)} %table_ref.1, s32[1024]{0:T(1024)S(1)} %pad_clamp_fusion), kind=kCustom, calls=%fused_computation | custom fusion | bytes 394752 | tf_op jit(solution)/shard_map/gather | solution.py:263
  30.4 0.7 convert_element_type.69
  31.2 4.2 %all-to-all-start.1 = ((bf16[32,12,256]{2,1,0:T(8,128)(2,1)}), bf16[32,12,256]{2,1,0:T(8,128)(2,1)S(1)}, u32[]{:S(2)}, u32[]{:S(2)}) async-start(bf16[32,12,256]{2,1,0:T(8,128)(2,1)} %convert_element_type.69), calls=%async_computation.1 | async-start | bytes 524288 | tf_op jit(solution)/shard_map/all_to_all | solution.py:222
  35.4 0.6 pad.17.freq_ref
  36.0 8.5 %all-to-all-done.1 = bf16[32,12,256]{2,1,0:T(8,128)(2,1)S(1)} async-done(((bf16[32,12,256]{2,1,0:T(8,128)(2,1)}), bf16[32,12,256]{2,1,0:T(8,128)(2,1)S(1)}, u32[]{:S(2)}, u32[]{:S(2)}) %all-to-all-start.1) | async-done | bytes 196640 | tf_op jit(solution)/shard_map/all_to_all | solution.py:222
  44.4 0.7 reshape.68.got_ref
  45.2 2.3 %shard_map.120 = (bf16[192,256]{1,0:T(8,128)(2,1)}, bf16[192,512]{1,0:T(8,128)(2,1)}, bf16[208,256]{1,0:T(8,128)(2,1)}) custom-call(bf16[384,256]{1,0:T(8,128)(2,1)} %reshape.68.got_ref, bf16[192,384]{1,0:T(8,128)(2,1)} %get-tuple-element.18.pick_ref, bf16[256,512]{1,0:T(8,128)(2,1)} %w_in_ref.3, bf16[512,256]{1,0:T(8,128)(2,1)} %w_out_ref.3, ...), custom_call_target="tpu_custom_call" | custom-call | tf_op jit(solution)/shard_map/pallas_call | solution.py:266
  47.5 0.2 collective-permute-start
  47.7 1.9 collective-permute-start.1
  49.7 0.5 collective-permute-start.2
  50.2 1.4 collective-permute-start.3
  51.6 2.1 %collective-permute-done.refs_1_ = bf16[208,256]{1,0:T(8,128)(2,1)S(1)} collective-permute-done((bf16[208,256]{1,0:T(8,128)(2,1)}, bf16[208,256]{1,0:T(8,128)(2,1)S(1)}, u32[]{:S(2)}, u32[]{:S(2)}) %collective-permute-start) | collective-permute-done | bytes 106528 | tf_op jit(solution)/shard_map/ppermute | solution.py:227
  53.8 2.8 %collective-permute-start.4 = (bf16[208,256]{1,0:T(8,128)(2,1)S(1)}, bf16[208,256]{1,0:T(8,128)(2,1)S(1)}, u32[]{:S(2)}, u32[]{:S(2)}) collective-permute-start(bf16[208,256]{1,0:T(8,128)(2,1)S(1)} %collective-permute-done.refs_1_), channel_id=1, source_target_pairs={{0,4},{4,0},{1,5},{5,1},{2,6},{6,2},{3,7},{7,3},{8,12},{12,8},{9,1... | collective-permute-start | bytes 319496 | tf_op jit(solution)/shard_map/ppermute | solution.py:227
  56.6 0.6 collective-permute-start.6
  57.2 0.3 collective-permute-done.4.refs_5_
  57.6 0.4 collective-permute-done.5.refs_6_
  57.9 0.3 collective-permute-done.6.refs_7_
  58.2 1.4 copy-done.8
  59.6 0.9 copy-done.10
  60.5 9.5 %shard_map.121 = f32[2,3072]{1,0:T(2,128)S(1)} custom-call(bf16[208,256]{1,0:T(8,128)(2,1)S(1)} %copy-done.10, bf16[208,256]{1,0:T(8,128)(2,1)S(1)} %collective-permute-done.refs_1_, bf16[208,256]{1,0:T(8,128)(2,1)S(1)} %collective-permute-done.1.refs_2_, bf16[208,256]{1,0:T(8,128)(2,1)S(1)} %collective-permute-done.2.refs_3_, ...), custom_call_target="tpu_custom_call" | custom-call | flops 2415919104 | bytes 9437184 | tf_op jit(solution)/shard_map/pallas_call | solution.py:275
  70.0 0.8 broadcast_in_dim.7
  70.9 5.9 %all-to-all-start.2 = ((f32[16,2,3072]{2,1,0:T(2,128)}), f32[16,2,3072]{2,1,0:T(2,128)S(1)}, u32[]{:S(2)}, u32[]{:S(2)}) async-start(f32[16,2,3072]{2,1,0:T(2,128)} %broadcast_in_dim.7), calls=%async_computation.2 | async-start | bytes 786432 | tf_op jit(solution)/shard_map/all_to_all | solution.py:222
  76.9 9.4 %all-to-all-done.2.refs_8_ = f32[16,2,3072]{2,1,0:T(2,128)S(1)} async-done(((f32[16,2,3072]{2,1,0:T(2,128)}), f32[16,2,3072]{2,1,0:T(2,128)S(1)}, u32[]{:S(2)}, u32[]{:S(2)}) %all-to-all-start.2) | async-done | bytes 393248 | tf_op jit(solution)/shard_map/all_to_all | solution.py:222
  86.3 1.4 copy-done.9
  87.7 0.9 copy-done.13
  88.6 0.9 copy-done.15
  89.5 13.4 %shard_map.122 = (bf16[3072,256]{1,0:T(8,128)(2,1)S(1)}, f32[4,192,256]{2,1,0:T(8,128)S(1)}, f32[4,192,256]{2,1,0:T(8,128)S(1)}) custom-call(s32[2]{0:T(128)S(1)} %pad_add_fusion.1.pos_ref, bf16[208,256]{1,0:T(8,128)(2,1)S(1)} %copy-done.11, bf16[208,256]{1,0:T(8,128)(2,1)S(1)} %collective-permute-done.refs_1_, ...), custom_call_target="tpu_custom_call" | custom-call | flops 7247757312 | bytes 9437184 | tf_op jit(solution)/shard_map/pallas_call | solution.py:288
  103.0 1.6 collective-permute-start.13
  104.6 1.9 collective-permute-done.13
  106.6 2.2 %collective-permute-start.14 = (f32[192,256]{1,0:T(8,128)S(1)}, f32[192,256]{1,0:T(8,128)S(1)}, u32[]{:S(2)}, u32[]{:S(2)}) collective-permute-start(f32[192,256]{1,0:T(8,128)S(1)} %get-tuple-element.31), channel_id=1, source_target_pairs={{0,24},{8,0},{16,8},{24,16},{1,25},{9,1},{17,9},{25,17},{2,26},{10... | collective-permute-start | bytes 589832 | tf_op jit(solution)/shard_map/ppermute | solution.py:227
  108.8 0.7 collective-permute-start.16
  109.5 3.6 %collective-permute-done.14.refs_1_ = f32[192,256]{1,0:T(8,128)S(1)} collective-permute-done((f32[192,256]{1,0:T(8,128)S(1)}, f32[192,256]{1,0:T(8,128)S(1)}, u32[]{:S(2)}, u32[]{:S(2)}) %collective-permute-start.14) | collective-permute-done | bytes 196640 | tf_op jit(solution)/shard_map/ppermute | solution.py:227
  113.1 3.1 %collective-permute-done.15.refs_2_ = f32[192,256]{1,0:T(8,128)S(1)} collective-permute-done((f32[192,256]{1,0:T(8,128)S(1)}, f32[192,256]{1,0:T(8,128)S(1)}, u32[]{:S(2)}, u32[]{:S(2)}) %collective-permute-start.15) | collective-permute-done | bytes 196640 | tf_op jit(solution)/shard_map/ppermute | solution.py:227
  116.2 4.5 %collective-permute-done.16.refs_3_ = f32[192,256]{1,0:T(8,128)S(1)} collective-permute-done((f32[192,256]{1,0:T(8,128)S(1)}, f32[192,256]{1,0:T(8,128)S(1)}, u32[]{:S(2)}, u32[]{:S(2)}) %collective-permute-start.16) | collective-permute-done | bytes 196640 | tf_op jit(solution)/shard_map/ppermute | solution.py:227
  120.8 1.6 shard_map.123
  122.4 4.2 %all-to-all-start.3 = ((bf16[128,16,384]{2,1,0:T(8,128)(2,1)}), bf16[128,16,384]{2,1,0:T(8,128)(2,1)S(1)}, u32[]{:S(2)}, u32[]{:S(2)}) async-start(bf16[128,16,384]{2,1,0:T(8,128)(2,1)} %bitcast.11), calls=%async_computation.3 | async-start | bytes 3145728 | tf_op jit(solution)/shard_map/all_to_all | solution.py:222
  126.6 1.2 fusion.6
  127.8 3.4 %collective-permute-start.9 = (bf16[768,256]{1,0:T(8,128)(2,1)}, bf16[768,256]{1,0:T(8,128)(2,1)}, u32[]{:S(2)}, u32[]{:S(2)}) collective-permute-start(bf16[768,256]{1,0:T(8,128)(2,1)} %get-tuple-element.37), channel_id=1, source_target_pairs={{0,3},{1,0},{2,1},{3,2},{4,7},{5,4},{6,5},{7,6},{8,11},{9,8},{10,9... | collective-permute-start | bytes 1179656 | tf_op jit(solution)/shard_map/ppermute | solution.py:227
  131.2 0.8 collective-permute-start.7
  132.1 19.9 %all-to-all-done.3.got_ref = bf16[128,16,384]{2,1,0:T(8,128)(2,1)S(1)} async-done(((bf16[128,16,384]{2,1,0:T(8,128)(2,1)}), bf16[128,16,384]{2,1,0:T(8,128)(2,1)S(1)}, u32[]{:S(2)}, u32[]{:S(2)}) %all-to-all-start.3) | async-done | bytes 1572896 | tf_op jit(solution)/shard_map/all_to_all | solution.py:222
  152.0 0.1 convert_reduce_fusion
  152.1 0.8 broadcast_in_dim.9
  152.9 11.8 %all-to-all-start.4 = ((f32[64,16,128]{2,1,0:T(8,128)}), f32[64,16,128]{2,1,0:T(8,128)S(1)}, u32[]{:S(2)}, u32[]{:S(2)}) async-start(f32[64,16,128]{2,1,0:T(8,128)} %broadcast_in_dim.9), calls=%async_computation.4 | async-start | bytes 1048576 | tf_op jit(solution)/shard_map/all_to_all | solution.py:222
  164.8 1.6 collective-permute-done.7
  166.4 2.2 %convert_add_fusion.2 = (f32[192,256]{1,0:T(8,128)S(1)}, f32[192,256]{1,0:T(8,128)}, f32[192,256]{1,0:T(8,128)}) fusion(bf16[768,256]{1,0:T(8,128)(2,1)} %collective-permute-done.9, s32[]{:T(128)S(6)} %select_n.66, bf16[768,256]{1,0:T(8,128)(2,1)} %collective-permute-done.8, bf16[768,256]{1,0:T(8,128)(2,1)} %collective-permute-done.7, ...), kind=kLoop, calls=%fused_computation.16 | loop fusion | flops 1032192 | bytes 1769484 | tf_op jit(solution)/shard_map/add | solution.py:330
  168.6 3.1 %collective-permute-start.12 = (f32[192,256]{1,0:T(8,128)}, f32[192,256]{1,0:T(8,128)}, u32[]{:S(2)}, u32[]{:S(2)}) collective-permute-start(f32[192,256]{1,0:T(8,128)} %get-tuple-element.34), channel_id=1, source_target_pairs={{0,96},{32,0},{64,32},{96,64},{1,97},{33,1},{65,33},{97,65},{2,98}... | collective-permute-start | bytes 589832 | tf_op jit(solution)/shard_map/ppermute | solution.py:227
  171.7 0.8 collective-permute-start.11
  172.5 0.9 collective-permute-start.10
  173.4 6.6 %collective-permute-done.12 = f32[192,256]{1,0:T(8,128)} collective-permute-done((f32[192,256]{1,0:T(8,128)}, f32[192,256]{1,0:T(8,128)}, u32[]{:S(2)}, u32[]{:S(2)}) %collective-permute-start.12) | collective-permute-done | bytes 196640 | tf_op jit(solution)/shard_map/ppermute | solution.py:227
  180.0 4.6 %collective-permute-done.10 = f32[192,256]{1,0:T(8,128)} collective-permute-done((f32[192,256]{1,0:T(8,128)S(1)}, f32[192,256]{1,0:T(8,128)}, u32[]{:S(2)}, u32[]{:S(2)}) %collective-permute-start.10) | collective-permute-done | bytes 196640 | tf_op jit(solution)/shard_map/ppermute | solution.py:227
  184.6 2.0 add_multiply_fusion
  186.6 0.5 collective-permute-start.17
  187.1 0.2 compare_select_fusion
  187.5 1.6 copy-done
  189.1 1.6 copy-done.7
  190.7 10.6 %shard_map.124 = (f32[2048,256]{1,0:T(8,128)}, f32[2048,256]{1,0:T(8,128)}) custom-call(s32[1,2048]{1,0:T(1,128)S(1)} %reshape.71.ids_ref, bf16[128,16,384]{2,1,0:T(8,128)(2,1)S(1)} %all-to-all-done.3.got_ref, f32[2048,256]{1,0:T(8,128)S(1)} %copy-done, f32[2048,256]{1,0:T(8,128)S(1)} %copy-done.7, bf16[256,512]{1,0:T(8,128)(2,1)S(1)} %copy-done.2, ...), custom_call_target="tpu_custom_call" | custom-call | flops 4294967296 | bytes 8388608 | tf_op jit(solution)/shard_map/pallas_call | solution.py:352
  201.3 1.0 select_bitcast_fusion
  (49 shorter events, 0.5 us)
Async XLA Ops:
  7.2 28.2 %copy-start.17 = (bf16[192]{0:T(256)(128)(2,1)S(1)}, bf16[192]{0:T(256)(128)(2,1)}, u32[]{:S(2)}) copy-start(bf16[192]{0:T(256)(128)(2,1)} %param.11) | copy-start | bytes 1156
  7.2 51.0 %all-gather.2.cloned.1.call-start = ((), (), s32[]{:S(2)}) async-start(), calls=%async_computation.5 | async-start | bytes 1671168 | tf_op jit(solution)/shard_map/all_gather | solution.py:239
  31.2 13.3 %all-to-all-start.1 = ((bf16[32,12,256]{2,1,0:T(8,128)(2,1)}), bf16[32,12,256]{2,1,0:T(8,128)(2,1)S(1)}, u32[]{:S(2)}, u32[]{:S(2)}) async-start(bf16[32,12,256]{2,1,0:T(8,128)(2,1)} %convert_element_type.69), calls=%async_computation.1 | async-start | bytes 524288 | tf_op jit(solution)/shard_map/all_to_all | solution.py:222
  47.5 6.3 %collective-permute-start = (bf16[208,256]{1,0:T(8,128)(2,1)}, bf16[208,256]{1,0:T(8,128)(2,1)S(1)}, u32[]{:S(2)}, u32[]{:S(2)}) collective-permute-start(bf16[208,256]{1,0:T(8,128)(2,1)} %get-tuple-element.19.refs_0_), channel_id=1, source_target_pairs={{0,8},{8,16},{16,24},{24,0},{1,9},{9,17},{17,25},{25,1},{2,10},{10... | collective-permute-start | bytes 319496 | tf_op jit(solution)/shard_map/ppermute | solution.py:227
  47.7 8.9 %collective-permute-start.1 = (bf16[208,256]{1,0:T(8,128)(2,1)}, bf16[208,256]{1,0:T(8,128)(2,1)S(1)}, u32[]{:S(2)}, u32[]{:S(2)}) collective-permute-start(bf16[208,256]{1,0:T(8,128)(2,1)} %get-tuple-element.19.refs_0_), channel_id=1, source_target_pairs={{0,16},{8,24},{16,0},{24,8},{1,17},{9,25},{17,1},{25,9},{2,18},{10... | collective-permute-start | bytes 319496 | tf_op jit(solution)/shard_map/ppermute | solution.py:227
  49.7 7.0 %collective-permute-start.2 = (bf16[208,256]{1,0:T(8,128)(2,1)}, bf16[208,256]{1,0:T(8,128)(2,1)S(1)}, u32[]{:S(2)}, u32[]{:S(2)}) collective-permute-start(bf16[208,256]{1,0:T(8,128)(2,1)} %get-tuple-element.19.refs_0_), channel_id=1, source_target_pairs={{0,24},{8,0},{16,8},{24,16},{1,25},{9,1},{17,9},{25,17},{2,26},{10... | collective-permute-start | bytes 319496 | tf_op jit(solution)/shard_map/ppermute | solution.py:227
  50.2 7.0 %collective-permute-start.3 = (bf16[208,256]{1,0:T(8,128)(2,1)}, bf16[208,256]{1,0:T(8,128)(2,1)S(1)}, u32[]{:S(2)}, u32[]{:S(2)}) collective-permute-start(bf16[208,256]{1,0:T(8,128)(2,1)} %get-tuple-element.19.refs_0_), channel_id=1, source_target_pairs={{0,4},{4,0},{1,5},{5,1},{2,6},{6,2},{3,7},{7,3},{8,12},{12,8},{9,1... | collective-permute-start | bytes 319496 | tf_op jit(solution)/shard_map/ppermute | solution.py:227
  53.8 3.8 %collective-permute-start.4 = (bf16[208,256]{1,0:T(8,128)(2,1)S(1)}, bf16[208,256]{1,0:T(8,128)(2,1)S(1)}, u32[]{:S(2)}, u32[]{:S(2)}) collective-permute-start(bf16[208,256]{1,0:T(8,128)(2,1)S(1)} %collective-permute-done.refs_1_), channel_id=1, source_target_pairs={{0,4},{4,0},{1,5},{5,1},{2,6},{6,2},{3,7},{7,3},{8,12},{12,8},{9,1... | collective-permute-start | bytes 319496 | tf_op jit(solution)/shard_map/ppermute | solution.py:227
  56.6 1.3 collective-permute-start.5
  56.6 1.6 collective-permute-start.6
  57.9 12.1 %copy-start.12 = (bf16[208,256]{1,0:T(8,128)(2,1)}, bf16[208,256]{1,0:T(8,128)(2,1)S(1)}, u32[]{:S(2)}) copy-start(bf16[208,256]{1,0:T(8,128)(2,1)S(1)} %collective-permute-done.5.refs_6_) | copy-start | bytes 319492
  58.2 11.9 %copy-start.14 = (bf16[208,256]{1,0:T(8,128)(2,1)}, bf16[208,256]{1,0:T(8,128)(2,1)S(1)}, u32[]{:S(2)}) copy-start(bf16[208,256]{1,0:T(8,128)(2,1)S(1)} %collective-permute-done.6.refs_7_) | copy-start | bytes 319492
  58.2 1.4 copy-start.8
  59.6 0.9 copy-start.10
  60.5 25.8 %copy-start.11 = (bf16[208,256]{1,0:T(8,128)(2,1)S(1)}, bf16[208,256]{1,0:T(8,128)(2,1)}, u32[]{:S(2)}) copy-start(bf16[208,256]{1,0:T(8,128)(2,1)} %get-tuple-element.19.refs_0_) | copy-start | bytes 319492
  70.9 15.4 %all-to-all-start.2 = ((f32[16,2,3072]{2,1,0:T(2,128)}), f32[16,2,3072]{2,1,0:T(2,128)S(1)}, u32[]{:S(2)}, u32[]{:S(2)}) async-start(f32[16,2,3072]{2,1,0:T(2,128)} %broadcast_in_dim.7), calls=%async_computation.2 | async-start | bytes 786432 | tf_op jit(solution)/shard_map/all_to_all | solution.py:222
  86.3 1.4 copy-start.9
  87.7 0.9 copy-start.13
  88.6 0.9 copy-start.15
  103.0 17.7 %copy-start.1 = (bf16[512,256]{1,0:T(8,128)(2,1)S(1)}, bf16[512,256]{1,0:T(8,128)(2,1)}, u32[]{:S(2)}) copy-start(bf16[512,256]{1,0:T(8,128)(2,1)} %w_out_ref.3) | copy-start | bytes 786436
  103.0 17.7 %copy-start.3 = (bf16[192,512]{1,0:T(8,128)(2,1)S(1)}, bf16[192,512]{1,0:T(8,128)(2,1)}, u32[]{:S(2)}) copy-start(bf16[192,512]{1,0:T(8,128)(2,1)} %get-tuple-element.24.refs_5_) | copy-start | bytes 589828
  103.0 17.7 %copy-start.4 = (bf16[192,256]{1,0:T(8,128)(2,1)S(1)}, bf16[192,256]{1,0:T(8,128)(2,1)}, u32[]{:S(2)}) copy-start(bf16[192,256]{1,0:T(8,128)(2,1)} %get-tuple-element.23.refs_4_) | copy-start | bytes 294916
  103.0 17.7 %copy-start.5 = (f32[32,256]{1,0:T(8,128)S(1)}, f32[32,256]{1,0:T(8,128)}, u32[]{:S(2)}) copy-start(f32[32,256]{1,0:T(8,128)} %get-tuple-element.26.refs_8_) | copy-start | bytes 98308
  103.0 17.7 %copy-start.6 = (s32[1,256]{1,0:T(1,128)S(1)}, s32[1,256]{1,0:T(1,128)}, u32[]{:S(2)}) copy-start(s32[1,256]{1,0:T(1,128)} %get-tuple-element.25.refs_7_) | copy-start | bytes 3076
  103.0 3.5 %collective-permute-start.13 = (f32[4,192,256]{2,1,0:T(8,128)S(1)}, f32[4,192,256]{2,1,0:T(8,128)S(1)}, u32[]{:S(2)}, u32[]{:S(2)}) collective-permute-start(f32[4,192,256]{2,1,0:T(8,128)S(1)} %get-tuple-element.22), channel_id=1, source_target_pairs={{0,4},{4,0},{1,5},{5,1},{2,6},{6,2},{3,7},{7,3},{8,12},{12,8},{9,1... | collective-permute-start | bytes 2359304 | tf_op jit(solution)/shard_map/ppermute | solution.py:227
  106.6 6.5 %collective-permute-start.14 = (f32[192,256]{1,0:T(8,128)S(1)}, f32[192,256]{1,0:T(8,128)S(1)}, u32[]{:S(2)}, u32[]{:S(2)}) collective-permute-start(f32[192,256]{1,0:T(8,128)S(1)} %get-tuple-element.31), channel_id=1, source_target_pairs={{0,24},{8,0},{16,8},{24,16},{1,25},{9,1},{17,9},{25,17},{2,26},{10... | collective-permute-start | bytes 589832 | tf_op jit(solution)/shard_map/ppermute | solution.py:227
  108.8 7.4 %collective-permute-start.15 = (f32[192,256]{1,0:T(8,128)S(1)}, f32[192,256]{1,0:T(8,128)S(1)}, u32[]{:S(2)}, u32[]{:S(2)}) collective-permute-start(f32[192,256]{1,0:T(8,128)S(1)} %get-tuple-element.30), channel_id=1, source_target_pairs={{0,16},{8,24},{16,0},{24,8},{1,17},{9,25},{17,1},{25,9},{2,18},{10... | collective-permute-start | bytes 589832 | tf_op jit(solution)/shard_map/ppermute | solution.py:227
  108.8 11.9 %collective-permute-start.16 = (f32[192,256]{1,0:T(8,128)S(1)}, f32[192,256]{1,0:T(8,128)S(1)}, u32[]{:S(2)}, u32[]{:S(2)}) collective-permute-start(f32[192,256]{1,0:T(8,128)S(1)} %get-tuple-element.29), channel_id=1, source_target_pairs={{0,8},{8,16},{16,24},{24,0},{1,9},{9,17},{17,25},{25,1},{2,10},{10... | collective-permute-start | bytes 589832 | tf_op jit(solution)/shard_map/ppermute | solution.py:227
  122.4 29.6 %all-to-all-start.3 = ((bf16[128,16,384]{2,1,0:T(8,128)(2,1)}), bf16[128,16,384]{2,1,0:T(8,128)(2,1)S(1)}, u32[]{:S(2)}, u32[]{:S(2)}) async-start(bf16[128,16,384]{2,1,0:T(8,128)(2,1)} %bitcast.11), calls=%async_computation.3 | async-start | bytes 3145728 | tf_op jit(solution)/shard_map/all_to_all | solution.py:222
  127.8 38.7 %copy-start.16 = (bf16[768,256]{1,0:T(8,128)(2,1)S(1)}, bf16[768,256]{1,0:T(8,128)(2,1)}, u32[]{:S(2)}) copy-start(bf16[768,256]{1,0:T(8,128)(2,1)} %get-tuple-element.36) | copy-start | bytes 1179652
  127.8 37.0 %collective-permute-start.9 = (bf16[768,256]{1,0:T(8,128)(2,1)}, bf16[768,256]{1,0:T(8,128)(2,1)}, u32[]{:S(2)}, u32[]{:S(2)}) collective-permute-start(bf16[768,256]{1,0:T(8,128)(2,1)} %get-tuple-element.37), channel_id=1, source_target_pairs={{0,3},{1,0},{2,1},{3,2},{4,7},{5,4},{6,5},{7,6},{8,11},{9,8},{10,9... | collective-permute-start | bytes 1179656 | tf_op jit(solution)/shard_map/ppermute | solution.py:227
  131.2 33.6 %collective-permute-start.8 = (bf16[768,256]{1,0:T(8,128)(2,1)}, bf16[768,256]{1,0:T(8,128)(2,1)}, u32[]{:S(2)}, u32[]{:S(2)}) collective-permute-start(bf16[768,256]{1,0:T(8,128)(2,1)} %get-tuple-element.38), channel_id=1, source_target_pairs={{0,2},{1,3},{2,0},{3,1},{4,6},{5,7},{6,4},{7,5},{8,10},{9,11},{10,... | collective-permute-start | bytes 1179656 | tf_op jit(solution)/shard_map/ppermute | solution.py:227
  131.2 35.2 %collective-permute-start.7 = (bf16[768,256]{1,0:T(8,128)(2,1)}, bf16[768,256]{1,0:T(8,128)(2,1)}, u32[]{:S(2)}, u32[]{:S(2)}) collective-permute-start(bf16[768,256]{1,0:T(8,128)(2,1)} %get-tuple-element.39), channel_id=1, source_target_pairs={{0,1},{1,2},{2,3},{3,0},{4,5},{5,6},{6,7},{7,4},{8,9},{9,10},{10,1... | collective-permute-start | bytes 1179656 | tf_op jit(solution)/shard_map/ppermute | solution.py:227
  152.9 33.7 %all-to-all-start.4 = ((f32[64,16,128]{2,1,0:T(8,128)}), f32[64,16,128]{2,1,0:T(8,128)S(1)}, u32[]{:S(2)}, u32[]{:S(2)}) async-start(f32[64,16,128]{2,1,0:T(8,128)} %broadcast_in_dim.9), calls=%async_computation.4 | async-start | bytes 1048576 | tf_op jit(solution)/shard_map/all_to_all | solution.py:222
  166.4 21.0 %copy-start.2 = (bf16[256,512]{1,0:T(8,128)(2,1)S(1)}, bf16[256,512]{1,0:T(8,128)(2,1)}, u32[]{:S(2)}) copy-start(bf16[256,512]{1,0:T(8,128)(2,1)} %w_in_ref.3) | copy-start | bytes 786436
  168.6 11.4 %collective-permute-start.12 = (f32[192,256]{1,0:T(8,128)}, f32[192,256]{1,0:T(8,128)}, u32[]{:S(2)}, u32[]{:S(2)}) collective-permute-start(f32[192,256]{1,0:T(8,128)} %get-tuple-element.34), channel_id=1, source_target_pairs={{0,96},{32,0},{64,32},{96,64},{1,97},{33,1},{65,33},{97,65},{2,98}... | collective-permute-start | bytes 589832 | tf_op jit(solution)/shard_map/ppermute | solution.py:227
  171.7 8.3 %collective-permute-start.11 = (f32[192,256]{1,0:T(8,128)}, f32[192,256]{1,0:T(8,128)}, u32[]{:S(2)}, u32[]{:S(2)}) collective-permute-start(f32[192,256]{1,0:T(8,128)} %get-tuple-element.35), channel_id=1, source_target_pairs={{0,64},{32,96},{64,0},{96,32},{1,65},{33,97},{65,1},{97,33},{2,66}... | collective-permute-start | bytes 589832 | tf_op jit(solution)/shard_map/ppermute | solution.py:227
  172.5 12.1 %collective-permute-start.10 = (f32[192,256]{1,0:T(8,128)S(1)}, f32[192,256]{1,0:T(8,128)}, u32[]{:S(2)}, u32[]{:S(2)}) collective-permute-start(f32[192,256]{1,0:T(8,128)S(1)} %get-tuple-element.33), channel_id=1, source_target_pairs={{0,32},{32,64},{64,96},{96,0},{1,33},{33,65},{65,97},{97,1},{2,34}... | collective-permute-start | bytes 589832 | tf_op jit(solution)/shard_map/ppermute | solution.py:227
  186.6 14.7 %collective-permute-start.17 = (f32[64,16,128]{2,1,0:T(8,128)S(1)}, f32[64,16,128]{2,1,0:T(8,128)S(1)}, u32[]{:S(2)}, u32[]{:S(2)}) collective-permute-start(f32[64,16,128]{2,1,0:T(8,128)S(1)} %all-to-all-done.4), channel_id=1, source_target_pairs={{0,4},{4,0},{1,5},{5,1},{2,6},{6,2},{3,7},{7,3},{8,12},{12,8},{9,1... | collective-permute-start | bytes 1572872 | tf_op jit(solution)/shard_map/ppermute | solution.py:227
  187.5 1.6 copy-start
  189.1 1.6 copy-start.7
Sparse Core Ops, SparseCore 0:
  10.1 46.3 all-gather.1

commit v2 on v1

--- a/solution.py
+++ b/solution.py
@@ -16,14 +16,15 @@
 NB = 8
 QS = NA * PAIRS
 VS = NB * PAIRS
-LIMIT = 40 << 20
+LIMIT = 58 << 20
+SMALL = 24 << 20
 score_scale = 0.0625
 learn_rate = 0.1
 
 SHARD = ("x", "y", "c")
 ALL = ("x", "y", "c", "z")
 CHIPS = ("x", "y", "z")
-A = ("z", "x")
+A = ("x", "z")
 
 f32 = jnp.float32
 bf16 = jnp.bfloat16
@@ -61,9 +62,12 @@
     return jnp.sum(jnp.where(eye, lanes, jnp.zeros((), lanes.dtype)), axis=1, keepdims=True)
 
 
-def slots_kernel(pair_ref, req_ref, place_ref, pick_ref, ids_ref):
-    owner = pair_ref[0:1, :]
-    row = pair_ref[1:2, :]
+def slots_kernel(owner_ref, row_ref, req_ref, place_ref, pick_ref, ids_ref, pair):
+    pair[...] = jnp.full((8, 256), -1, i32)
+    pair[0:1, 0:PAIRS] = owner_ref[...]
+    pair[1:2, 0:PAIRS] = row_ref[...]
+    owner = pair[0:1, :]
+    row = pair[1:2, :]
     mine = owner == iota((OWNERS, 256), 0)
     onehot = mine.astype(f32).astype(bf16)
     earlier = (iota((256, 256), 0) < iota((256, 256), 1)).astype(f32).astype(bf16)
@@ -84,7 +88,8 @@
     pick_ref[...] = (col == iota((PAIRS, OWNERS * CAP), 1)).astype(f32).astype(bf16)
 
 
-def tower_kernel(got_ref, pick_ref, w_in_ref, w_out_ref, freq_ref, emb_ref, hid_ref, pay_ref):
+def tower_kernel(got_ref, pick_ref, w_in_ref, w_out_ref, freq_ref, *refs):
+    emb_ref, hid_ref, pay_ref = refs[-3:]
     emb = mm(pick_ref[...], got_ref[...]).astype(bf16)
     emb_ref[...] = emb
     hid = jnp.maximum(mm(emb, w_in_ref[...]), 0.0).astype(bf16)
@@ -94,7 +99,8 @@
     pay_ref[PAIRS : PAIRS + 16, :] = freq_ref[...]
 
 
-QB = 256
+QB = 768
+VB = 384
 
 
 def load_vecs(vec_refs, vec, freq):
@@ -105,12 +111,12 @@
         vec[at, :] = vec_refs[b][0:PAIRS, :]
 
 
-def lanes(col, n):
-    return jnp.concatenate([col] * (n // 128), axis=1)
+def lanes(col):
+    return jnp.concatenate([col] * (QB // 128), axis=1)
 
 
 def score_kernel(*refs):
-    vec_refs, (q_ref, ml_ref, vec, freq, scores) = refs[:NB], refs[NB:]
+    vec_refs, (q_ref, lse_ref, vec, freq, scores) = refs[:NB], refs[NB:]
 
     @pl.when(pl.program_id(0) == 0)
     def _():
@@ -118,63 +124,100 @@
 
     q = q_ref[...] * jnp.asarray(score_scale, bf16)
     top = None
-    for b in range(NB):
-        at = slice(b * PAIRS, (b + 1) * PAIRS)
-        s = mm(vec[at, :], q, NT) - lanes(freq[at, :], QB)
+    for b in range(0, VS, VB):
+        at = slice(b, b + VB)
+        s = mm(vec[at, :], q, NT) - lanes(freq[at, :])
         scores[at, :] = s
-        t = jnp.max(s, axis=0, keepdims=True)
+        t = jnp.max(s.reshape(VB // 8, 8, QB), axis=0)
         top = t if top is None else jnp.maximum(top, t)
-    total = jnp.zeros((1, QB), f32)
-    for b in range(NB):
-        at = slice(b * PAIRS, (b + 1) * PAIRS)
-        total = total + jnp.sum(jnp.exp(scores[at, :] - top), axis=0, keepdims=True)
-    ml_ref[0:1, :] = top
-    ml_ref[1:2, :] = total
-
-
-CB = 384
-
-
-def grad_kernel(pos_ref, *refs):
-    vec_refs, (all_ml_ref, q_ref, o_ref, same_ref, other_ref, vec, freq, turned, lse, coef) = refs[:NB], refs[NB:]
-    step = pl.program_id(0)
-
-    @pl.when(step == 0)
+    top = jnp.max(top, axis=0, keepdims=True)
+    total = jnp.zeros((8, QB), f32)
+    for b in range(0, VS, VB):
+        e = jnp.exp(scores[b : b + VB, :] - top)
+        total = total + jnp.sum(e.reshape(VB // 8, 8, QB), axis=0)
+    part = top + jnp.log(jnp.sum(total, axis=0, keepdims=True))
+    for k in range(QB // 128):
+        row = jnp.broadcast_to(part[:, k * 128 : (k + 1) * 128].reshape(1, 1, 128), (NA, 1, 128))
+        lse_ref[:, pl.ds(pl.program_id(0) * (QB // 128) + k, 1), :] = row
+
+
+def is_pair(pos_ref):
+    first = pos_ref[0] * PAIRS - pl.program_id(0) * QB
+    return iota((PAIRS, QB), 0) + first == iota((PAIRS, QB), 1)
+
+
+def query_lanes(rows_ref, *index):
+    n = QB // 128
+    at = pl.program_id(0) * n
+    return jnp.concatenate([rows_ref[(*index, pl.ds(at + i, 1), slice(None))] for i in range(n)], axis=1)
+
+
+def query_kernel(pos_ref, *refs):
+    vec_refs, (part_ref, q_ref, o_ref, vec, freq, turned, weight) = refs[:NB], refs[NB:]
+
+    @pl.when(pl.program_id(0) == 0)
     def _():
         load_vecs(vec_refs, vec, freq)
         for k in range(0, VS, 256):
             turned[:, k : k + 256] = vec[k : k + 256, :].astype(f32).T.astype(bf16)
-        top = all_ml_ref[0, 0:1, :]
+
+    q = q_ref[...] * jnp.asarray(score_scale, bf16)
+    norm = query_lanes(part_ref, 0).reshape(1, QB)
+    for b in range(0, VS, VB):
+        at = slice(b, b + VB)
+        p = jnp.exp(mm(vec[at, :], q, NT) - lanes(freq[at, :]) - norm)
+        if b == 0:
+            p = jnp.concatenate([jnp.where(is_pair(pos_ref), 0.0, p[:PAIRS]), p[PAIRS:]], axis=0)
+        weight[at, :] = p.astype(bf16)
+    o_ref[...] = mm(turned[...], weight[...]).T.astype(bf16)
+
+
+def vec_kernel(pos_ref, vec, freq, parts_ref, q_ref, unread_ref, same_ref, other_ref, lse, coef):
+    @pl.when(pl.program_id(0) == 0)
+    def _():
+        top = parts_ref[0]
         for a in range(1, NA):
-            top = jnp.maximum(top, all_ml_ref[a, 0:1, :])
-        total = jnp.zeros((1, QS), f32)
-        for a in range(NA):
-            total = total + jnp.exp(all_ml_ref[a, 0:1, :] - top) * all_ml_ref[a, 1:2, :]
-        whole_lse = top + jnp.log(total)
-        for k in range(QS // CB):
-            lse[k, :, :] = jnp.broadcast_to(whole_lse[:, k * CB : (k + 1) * CB], (8, CB))
+            top = jnp.maximum(top, parts_ref[a])
+        total = jnp.exp(parts_ref[0] - top)
+        for a in range(1, NA):
+            total = total + jnp.exp(parts_ref[a] - top)
+        lse[...] = top + jnp.log(total)
         same_ref[...] = jnp.zeros_like(same_ref)
         other_ref[...] = jnp.zeros_like(other_ref)
 
     q = q_ref[...]
     scaled = q * jnp.asarray(score_scale, bf16)
-    norm = lse[step][0:1, :]
-    first = pos_ref[0] * PAIRS - step * CB
-    for b in range(NB):
-        at = slice(b * PAIRS, (b + 1) * PAIRS)
-        p = jnp.exp(mm(vec[at, :], scaled, NT) - lanes(freq[at, :], CB) - norm)
+    norm = query_lanes(lse)
+    for b in range(0, VS, VB):
+        at = slice(b, b + VB)
+        p = jnp.exp(mm(vec[at, :], scaled, NT) - lanes(freq[at, :]) - norm)
         if b == 0:
-            p = jnp.where(iota((PAIRS, CB), 0) + first == iota((PAIRS, CB), 1), p - 1.0, p)
+            p = jnp.concatenate([jnp.where(is_pair(pos_ref), p[:PAIRS] - 1.0, p[:PAIRS]), p[PAIRS:]], axis=0)
         coef[at, :] = p.astype(bf16)
-    o_ref[...] = mm(turned[...], coef[...]).T.astype(bf16)
-    for b in range(NB):
-        at = slice(b * PAIRS, (b + 1) * PAIRS)
+    for b in range(0, NB, 2):
+        g = mm(coef[b * PAIRS : (b + 2) * PAIRS, :], q)
         ref = (same_ref, other_ref)[b // 4]
-        ref[b % 4] += mm(coef[at, :], q)
+        ref[b % 4] += g[:PAIRS]
+        ref[b % 4 + 1] += g[PAIRS:]
+
+
+def combine_kernel(got_ref, parts_ref, q_ref, pay_ref, out_ref):
+    parts = parts_ref[...]
+    top = jnp.max(parts, axis=0, keepdims=True)
+    lse = top + jnp.log(jnp.sum(jnp.exp(parts - top), axis=0, keepdims=True))
+    shares = jnp.exp(parts - lse)
+    q = q_ref[...].astype(f32)
+    vec = pay_ref[0:PAIRS, :].astype(f32)
+    line = pay_ref[PAIRS : PAIRS + 16, :].astype(f32)[0:1, :]
+    own = jnp.sum(q * vec, axis=1, keepdims=True) * score_scale - column(line, PAIRS) - column(lse, PAIRS)
+    total = (jnp.exp(own) - 1.0).astype(bf16).astype(f32) * vec
+    for a in range(NA):
+        total = total + got_ref[a].astype(f32) * column(shares[a : a + 1], PAIRS)
+    out_ref[...] = total * score_scale
 
 
 def back_kernel(*refs):
-    parts, (emb_ref, hid_ref, w_out_ref, place_ref, ids_ref, out_ref) = refs[:4], refs[4:]
+    parts, (emb_ref, hid_ref, w_out_ref, place_ref, ids_ref), out_ref = refs[:4], refs[4:9], refs[-1]
     total = parts[0][...]
     for part in parts[1:]:
         total = total + part[...]
@@ -198,7 +241,7 @@
             out_ref[:, c, z, :, E : E + 128] = pieces[c][:, z]
 
 
-TB = 256
+TB = 512
 
 
 def update_kernel(ids_ref, got_ref, table_ref, accum_ref, w_in_ref, w_out_ref, table_out, accum_out):
@@ -231,22 +274,27 @@
     return [pl.BlockSpec(memory_space=VMEM)] * n
 
 
+def unread(n):
+    return [pl.BlockSpec(memory_space=pl.ANY)] * n
+
+
+def after(x, *others):
+    return pl.pallas_call(
+        lambda *refs: None,
+        out_shape=sds(x.shape, x.dtype),
+        in_specs=unread(1 + len(others)),
+        out_specs=unread(1)[0],
+        input_output_aliases={0: 0},
+    )(x, *others)
+
+
 def const(*shape):
     return pl.BlockSpec(shape, lambda *_: (0,) * len(shape))
 
 
 def local(queries, item_owner, item_row, log_freq, table, accum, w_in, w_out):
-    all_q = lax.all_gather(queries, A, axis=0, tiled=True)
-    here = lax.axis_index(A).astype(i32)
     here_x = lax.axis_index("x").astype(i32)
     here_z = lax.axis_index("z").astype(i32)
-
-    pair = jnp.stack(
-        [
-            jnp.pad(item_owner[:, 0], (0, 256 - PAIRS), constant_values=-1),
-            jnp.pad(item_row, (0, 256 - PAIRS)),
-        ]
-    )
     req, place, pick, ids = call(
         slots_kernel,
         (
@@ -255,10 +303,20 @@
             sds((PAIRS, OWNERS * CAP), bf16),
             sds((OWNERS, E), f32),
         ),
-        in_specs=whole(1),
+        in_specs=whole(2),
         out_specs=tuple(whole(4)),
-    )(pair)
+        scratch_shapes=[pltpu.VMEM((8, 256), i32)],
+    )(item_owner.reshape(1, PAIRS), item_row.reshape(1, PAIRS))
     asked = a2a(req.reshape(OWNERS, 1, 128), SHARD)
+    early = after(queries, req)
+    slab = jnp.zeros((QB, E), bf16)
+    for k in range(4):
+        block = shift(early, "z", 4 - k) if k else queries
+        slab = lax.dynamic_update_slice(slab, block, ((here_z + k) % 4 * PAIRS, 0))
+    slabs = [slab] + [shift(slab, "x", 4 - k) for k in range(1, 4)]
+    all_q = jnp.zeros((QS, E), bf16)
+    for k in range(4):
+        all_q = lax.dynamic_update_slice(all_q, slabs[k], ((here_x + k) % 4 * QB, 0))
     wanted = jnp.maximum(asked[:, 0, :CAP].reshape(OWNERS * CAP), 0)
     picked = table.at[wanted].get(mode="promise_in_bounds").astype(bf16)
     got = a2a(picked.reshape(OWNERS, CAP, E), SHARD).reshape(OWNERS * CAP, E)
@@ -266,49 +324,58 @@
     emb, hid, pay = call(
         tower_kernel,
         (sds((PAIRS, E), bf16), sds((PAIRS, H), bf16), sds((PAIRS + 16, E), bf16)),
-        in_specs=whole(5),
+        in_specs=whole(5) + unread(2),
         out_specs=tuple(whole(3)),
-    )(got, pick, w_in, w_out, freq_row)
+    )(got, pick, w_in, w_out, freq_row, slabs[1], slabs[3])
     vecs = [pay] + [shift(pay, "y", k) for k in range(1, 4)]
     vecs = vecs + [shift(v, "c", 1) for v in vecs]
 
-    ml = call(
+    part_lse = call(
         score_kernel,
-        sds((2, QS), f32),
+        sds((NA, QS // 128, 128), f32),
         cost=(2 * VS * QS * E, VS * QS * 2, VS * QS),
         limit=LIMIT,
         grid=(QS // QB,),
         in_specs=[const(PAIRS + 16, E)] * NB + [pl.BlockSpec((QB, E), lambda i: (i, 0))],
-        out_specs=pl.BlockSpec((2, QB), lambda i: (0, i)),
+        out_specs=const(NA, QS // 128, 128),
         scratch_shapes=[pltpu.VMEM((VS, E), bf16), pltpu.VMEM((VS, 128), f32), pltpu.VMEM((VS, QB), f32)],
     )(*vecs, all_q)
-    all_ml = a2a(jnp.broadcast_to(ml[None], (NA, 2, QS)), A)
-
-    per = QS // 4 // CB
-    o, same, other = call(
-        grad_kernel,
-        (sds((QS, E), bf16), sds((4, PAIRS, E), f32), sds((4, PAIRS, E), f32)),
-        cost=(6 * VS * QS * E, VS * QS * 2, VS * QS),
+    all_lse = a2a(part_lse, A)
+    here = here_x * 4 + here_z
+    o, vec_all, freq_all = call(
+        query_kernel,
+        (sds((QS, E), bf16), sds((VS, E), bf16), sds((VS, 128), f32)),
+        cost=(4 * VS * QS * E, VS * QS, VS * QS),
         limit=LIMIT,
         grid_spec=pltpu.PrefetchScalarGridSpec(
             num_scalar_prefetch=1,
-            grid=(QS // CB,),
+            grid=(QS // QB,),
             in_specs=[const(PAIRS + 16, E)] * NB
-            + [const(NA, 2, QS), pl.BlockSpec((CB, E), lambda i, pos: (i, 0))],
-            out_specs=(
-                pl.BlockSpec((CB, E), lambda i, pos: (((i // per - pos[1] + 4) % 4) * per + i % per, 0)),
-                const(4, PAIRS, E),
-                const(4, PAIRS, E),
-            ),
-            scratch_shapes=[
-                pltpu.VMEM((VS, E), bf16),
-                pltpu.VMEM((VS, 128), f32),
-                pltpu.VMEM((E, VS), bf16),
-                pltpu.VMEM((QS // CB, 8, CB), f32),
-                pltpu.VMEM((VS, CB), bf16),
+            + [const(NA, QS // 128, 128), pl.BlockSpec((QB, E), lambda i, pos: (i, 0))],
+            out_specs=(pl.BlockSpec((QB, E), lambda i, pos: (i, 0)), const(VS, E), const(VS, 128)),
+            scratch_shapes=[pltpu.VMEM((E, VS), bf16), pltpu.VMEM((VS, QB), bf16)],
+        ),
+    )(here.reshape(1), *vecs, part_lse, all_q)
+    same, other = call(
+        vec_kernel,
+        (sds((4, PAIRS, E), f32), sds((4, PAIRS, E), f32)),
+        cost=(4 * VS * QS * E, VS * QS, VS * QS),
+        limit=LIMIT,
+        grid_spec=pltpu.PrefetchScalarGridSpec(
+            num_scalar_prefetch=1,
+            grid=(QS // QB,),
+            in_specs=[
+                const(VS, E),
+                const(VS, 128),
+                const(NA, QS // 128, 128),
+                pl.BlockSpec((QB, E), lambda i, pos: (i, 0)),
+                unread(1)[0],
             ],
+            out_specs=(const(4, PAIRS, E), const(4, PAIRS, E)),
+            scratch_shapes=[pltpu.VMEM((QS // 128, 128), f32), pltpu.VMEM((VS, QB), bf16)],
         ),
-    )(jnp.stack([here, here_z]), *vecs, all_ml, all_q)
+    )(here.reshape(1), vec_all, freq_all, all_lse, all_q, o)
+    o_got = a2a(o.reshape(NA, PAIRS, E), A)
 
     from_core = shift(other, "c", 1)
     sums = [same[k] + from_core[k] for k in range(4)]
@@ -316,35 +383,23 @@
     out = call(
         back_kernel,
         sds((16, 2, 4, SLOT, E + 128), bf16),
-        limit=LIMIT,
-        in_specs=whole(9),
+        limit=SMALL,
+        in_specs=whole(9) + unread(1),
         out_specs=whole(1)[0],
-    )(*parts, emb, hid, w_out, place, ids)
+    )(*parts, emb, hid, w_out, place, ids, o_got)
     back = a2a(out.reshape(128, SLOT, E + 128), ALL)
 
-    slab = QS // 4
-    slabs = [o[:slab]] + [shift(o[k * slab : (k + 1) * slab], "z", k) for k in range(1, 4)]
-
-    def toward(k):
-        at = ((here_x + k) % 4) * PAIRS
-        return sum(lax.dynamic_slice(v, (at, 0), (PAIRS, E)).astype(f32) for v in slabs)
-
-    query_grad = toward(0)
-    for k in range(1, 4):
-        query_grad = query_grad + shift(toward(k), "x", k)
-    query_grad = query_grad * score_scale
+    own = lax.dynamic_slice(all_lse.reshape(NA, QS), (0, here * PAIRS), (NA, PAIRS))
+    query_grad = call(
+        combine_kernel,
+        sds((PAIRS, E), f32),
+        limit=SMALL,
+        in_specs=whole(4),
+        out_specs=whole(1)[0],
+    )(o_got, jnp.pad(own, ((0, 0), (0, 256 - PAIRS))), queries, pay)
 
     w_sum = jnp.sum(back[:, :, E:].astype(f32), axis=0)
     w_mine = a2a(jnp.broadcast_to(w_sum[None], (64, SLOT, 128)), CHIPS)
-    w_other = shift(w_mine, "c", 1)
-    zero = lax.axis_index("c") == 0
-
-    def tiles(x, rows, cols):
-        return x.reshape(rows // 8, cols // 128, 8, 128).transpose(0, 2, 1, 3).reshape(rows, cols)
-
-    w_out_grad = tiles(jnp.where(zero, w_mine, w_other), H, E)
-    w_in_grad = tiles(jnp.where(zero, w_other, w_mine), E, H)
-
     hi = back[:, CAP, 0:CAP].astype(i32)
     lo = back[:, CAP, 128 : 128 + CAP].astype(i32)
     row_ids = jnp.where(hi < 0, -1, hi * 256 + lo)
@@ -368,6 +423,16 @@
             pl.BlockSpec((TB, E), lambda i: (i, 0)),
         ),
     )(row_ids, back, table, accum, w_in, w_out)
+    w_mine = after(w_mine, table_new)
+    w_other = shift(w_mine, "c", 1)
+    zero = lax.axis_index("c") == 0
+
+    def tiles(x, rows, cols):
+        return x.reshape(rows // 8, cols // 128, 8, 128).transpose(0, 2, 1, 3).reshape(rows, cols)
+
+    w_out_grad = tiles(jnp.where(zero, w_mine, w_other), H, E)
+    w_in_grad = tiles(jnp.where(zero, w_other, w_mine), E, H)
+
     return query_grad, table_new, accum_new, w_in_grad, w_out_grad
 
 

time: 210 us -> 179 us (0.85)
  waiting for transfers between devices: 67.6 us -> 27.3 us
  blocking collectives: 15.5 us -> 35.2 us
  between operations: 14.3 us -> 1.14 us
  Pallas kernels: 39.1 us -> 44.5 us
  starting transfers between devices: 47.7 us -> 50.9 us
  local copies, waits for them, and re-layouts: 18.5 us -> 15.6 us
  other arithmetic: 6.44 us -> 3.83 us
    all_to_all x4 -> x5, waiting for transfers between devices: 37.9 us -> 12.8 us  [a2a(): return lax.all_to_all(x, axes, split_axis=0, concat_axis=0, tiled=True)]
    all_to_all x1, blocking collectives: 15.5 us -> 35.2 us  [a2a(): return lax.all_to_all(x, axes, split_axis=0, concat_axis=0, tiled=True)]
    ppermute x18, waiting for transfers between devices: 29.1 us -> 14.5 us  [shift(): return lax.ppermute(x, axis, [(i, (i + k) % n) for i in range(n)])]
    pallas_call x3 -> x7, Pallas kernels: 24.5 us -> 29 us  [the longest x1 9.41 us: local(): call(query_kernel, (sds((QS, E), bf16), sds((VS, E), bf16), sds((VS, 128)...]
    all_to_all x4 -> x5, starting transfers between devices: 26.2 us -> 29.1 us  [a2a(): return lax.all_to_all(x, axes, split_axis=0, concat_axis=0, tiled=True)]
    unnamed x36 -> x50, local copies, waits for them, and re-layouts: 8.77 us -> 6.34 us
    add x1 -> x0, other arithmetic: 2.18 us -> none  [toward(): sum((lax.dynamic_slice(v, (at, 0), (PAIRS, E)).astype(f32) for v in slabs))]
  transfers between devices with their start and end apart: 23 -> 23, of which waited for: 14 -> 9; matrix products, arithmetic and copies ran while one was open for 7% -> 6% of each run, Pallas kernels for 7% -> 19%
where the time goes in v2:
time: 179 us; the launch traced here: 178 us
  starting transfers between devices  50.9 us (28%)
  Pallas kernels  44.5 us (25%)
  blocking collectives  35.2 us (20%)
  waiting for transfers between devices  27.3 us (15%)
  local copies, waits for them, and re-layouts  15.6 us (9%)
  other arithmetic  3.83 us (2%)
    all_to_all x1, blocking collectives, a2a(): return lax.all_to_all(x, axes, split_axis=0, concat_axis=0, tiled=True)  35.2 us
    all_to_all x5, starting transfers between devices, a2a(): return lax.all_to_all(x, axes, split_axis=0, concat_axis=0, tiled=True)  29.1 us
    ppermute x18, starting transfers between devices, shift(): return lax.ppermute(x, axis, [(i, (i + k) % n) for i in range(n)])  21.8 us
    ppermute x18, waiting for transfers between devices, shift(): return lax.ppermute(x, axis, [(i, (i + k) % n) for i in range(n)])  14.5 us
    all_to_all x5, waiting for transfers between devices, a2a(): return lax.all_to_all(x, axes, split_axis=0, concat_axis=0, tiled=True)  12.8 us
    pallas_call x1, Pallas kernels, local(): call(update_kernel, (sds((ROWS, E), f32), sds((ROWS, E), f32)), cost=(4 *...  11.5 us
    pallas_call x1, Pallas kernels, local(): call(query_kernel, (sds((QS, E), bf16), sds((VS, E), bf16), sds((VS, 128)...  9.41 us
    pallas_call x1, Pallas kernels, local(): call(score_kernel, sds((NA, QS // 128, 128), f32), cost=(2 * VS * QS * E,...  8.94 us
  transfers between devices with their start and end apart: 23, of which 9 were waited for; matrix products, arithmetic and copies ran while one was open for 6% of the time, Pallas kernels for 19%

profile of v2, /device:TPU:1, one launch (start us, length us, event | category | flops | bytes accessed | tf_op | source)
XLA Modules:
  0.0 178.4 jit_solution(3909755193907489518)
XLA Ops:
  0.6 1.5 copy.20.refs_0_
  2.2 1.7 shard_map.119
  3.8 2.5 %collective-permute-start.2 = (bf16[192,256]{1,0:T(8,128)(2,1)}, bf16[192,256]{1,0:T(8,128)(2,1)S(1)}, u32[]{:S(2)}, u32[]{:S(2)}) collective-permute-start(bf16[192,256]{1,0:T(8,128)(2,1)} %shard_map.120), channel_id=1, source_target_pairs={{0,1},{1,2},{2,3},{3,0},{4,5},{5,6},{6,7},{7,4},{8,9},{9,10},{10,1... | collective-permute-start | bytes 294920 | tf_op jit(solution)/shard_map/ppermute | solution.py:270
  6.3 3.3 %collective-permute-start.1 = (bf16[192,256]{1,0:T(8,128)(2,1)}, bf16[192,256]{1,0:T(8,128)(2,1)S(1)}, u32[]{:S(2)}, u32[]{:S(2)}) collective-permute-start(bf16[192,256]{1,0:T(8,128)(2,1)} %shard_map.120), channel_id=1, source_target_pairs={{0,2},{1,3},{2,0},{3,1},{4,6},{5,7},{6,4},{7,5},{8,10},{9,11},{10,... | collective-permute-start | bytes 294920 | tf_op jit(solution)/shard_map/ppermute | solution.py:270
  9.6 0.7 collective-permute-start
  10.3 8.6 %all-to-all-start = ((s32[32,1,128]{2,1,0:T(1,128)}), s32[32,1,128]{2,1,0:T(1,128)S(1)}, u32[]{:S(2)}, u32[]{:S(2)}) async-start(s32[32,1,128]{2,1,0:T(1,128)} %bitcast.38), calls=%async_computation | async-start | bytes 32768 | tf_op jit(solution)/shard_map/all_to_all | solution.py:265
  19.0 0.9 constant_dynamic-update-slice_fusion.7
  20.1 1.5 collective-permute-start.4
  21.5 1.3 collective-permute-start.3
  22.8 3.0 %all-to-all-done = s32[32,1,128]{2,1,0:T(1,128)S(1)} async-done(((s32[32,1,128]{2,1,0:T(1,128)}), s32[32,1,128]{2,1,0:T(1,128)S(1)}, u32[]{:S(2)}, u32[]{:S(2)}) %all-to-all-start) | async-done | bytes 16416 | tf_op jit(solution)/shard_map/all_to_all | solution.py:265
  25.9 0.1 reshape.98
  26.0 1.0 collective-permute-start.12
  27.0 3.3 %gather_fusion = bf16[384,256]{1,0:T(8,128)(2,1)S(1)} fusion(f32[2048,256]{1,0:T(8,128)} %table_ref.1, s32[1024]{0:T(1024)S(1)} %pad_clamp_fusion), kind=kCustom, calls=%fused_computation | custom fusion | bytes 394752 | tf_op jit(solution)/shard_map/gather | solution.py:321
  30.3 0.7 convert_element_type.23
  31.0 5.3 %all-to-all-start.1 = ((bf16[32,12,256]{2,1,0:T(8,128)(2,1)}), bf16[32,12,256]{2,1,0:T(8,128)(2,1)S(1)}, u32[]{:S(2)}, u32[]{:S(2)}) async-start(bf16[32,12,256]{2,1,0:T(8,128)(2,1)} %convert_element_type.23), calls=%async_computation.1 | async-start | bytes 524288 | tf_op jit(solution)/shard_map/all_to_all | solution.py:265
  36.4 0.6 pad.12.freq_ref
  37.0 0.1 broadcast_in_dim.18
  37.1 9.8 %all-to-all-done.1 = bf16[32,12,256]{2,1,0:T(8,128)(2,1)S(1)} async-done(((bf16[32,12,256]{2,1,0:T(8,128)(2,1)}), bf16[32,12,256]{2,1,0:T(8,128)(2,1)S(1)}, u32[]{:S(2)}, u32[]{:S(2)}) %all-to-all-start.1) | async-done | bytes 196640 | tf_op jit(solution)/shard_map/all_to_all | solution.py:265
  46.9 0.7 reshape.86.got_ref
  47.7 0.7 copy-done.11
  48.4 0.1 copy-done.13
  48.5 2.3 %shard_map.121 = (bf16[192,256]{1,0:T(8,128)(2,1)}, bf16[192,512]{1,0:T(8,128)(2,1)}, bf16[208,256]{1,0:T(8,128)(2,1)}) custom-call(bf16[384,256]{1,0:T(8,128)(2,1)} %reshape.86.got_ref, bf16[192,384]{1,0:T(8,128)(2,1)} %get-tuple-element.20.pick_ref, bf16[256,512]{1,0:T(8,128)(2,1)} %w_in_ref.3, bf16[512,256]{1,0:T(8,128)(2,1)} %w_out_ref.3, ...), custom_call_target="tpu_custom_call" | custom-call | tf_op jit(solution)/shard_map/pallas_call | solution.py:324
  50.9 0.6 collective-permute-start.8
  51.5 0.4 collective-permute-start.7
  51.9 1.7 collective-permute-start.6
  53.6 1.0 constant_dynamic-update-slice_fusion.2
  54.6 1.6 collective-permute-done.7.refs_3_
  56.3 1.2 collective-permute-start.11
  57.5 2.2 %collective-permute-start.10 = (bf16[208,256]{1,0:T(8,128)(2,1)S(1)}, bf16[208,256]{1,0:T(8,128)(2,1)S(1)}, u32[]{:S(2)}, u32[]{:S(2)}) collective-permute-start(bf16[208,256]{1,0:T(8,128)(2,1)S(1)} %collective-permute-done.6.refs_2_), channel_id=1, source_target_pairs={{0,4},{4,0},{1,5},{5,1},{2,6},{6,2},{3,7},{7,3},{8,12},{12,8},{9,1... | collective-permute-start | bytes 319496 | tf_op jit(solution)/shard_map/ppermute | solution.py:270
  59.6 0.8 collective-permute-done.5.refs_1_
  60.5 0.8 collective-permute-start.9
  61.4 0.8 collective-permute-done.9.refs_5_
  62.2 0.2 copy-done.10
  62.5 0.6 copy-done.22
  63.2 8.9 %shard_map.122.refs_8_ = f32[16,24,128]{2,1,0:T(8,128)} custom-call(bf16[208,256]{1,0:T(8,128)(2,1)} %get-tuple-element.21.refs_0_.pay_ref, bf16[208,256]{1,0:T(8,128)(2,1)} %copy-done.19, bf16[208,256]{1,0:T(8,128)(2,1)} %copy-done.18, bf16[208,256]{1,0:T(8,128)(2,1)} %copy-done.17, bf16[208,256]{1,0:T(8,128)(2,1)} %copy-done.16, ...), custom_call_target="tpu_custom_call" | custom-call | flops 2415919104 | bytes 9437184 | tf_op jit(solution)/shard_map/pallas_call | solution.py:333
  72.1 4.0 %all-to-all-start.3 = ((f32[16,24,128]{2,1,0:T(8,128)}), f32[16,24,128]{2,1,0:T(8,128)S(1)}, u32[]{:S(2)}, u32[]{:S(2)}) async-start(f32[16,24,128]{2,1,0:T(8,128)} %shard_map.122.refs_8_), calls=%async_computation.3 | async-start | bytes 393216 | tf_op jit(solution)/shard_map/all_to_all | solution.py:265
  76.1 9.4 %shard_map.123 = (bf16[3072,256]{1,0:T(8,128)(2,1)}, bf16[1536,256]{1,0:T(8,128)(2,1)}, f32[1536,128]{1,0:T(8,128)}) custom-call(s32[1]{0:T(128)} %bitcast.pos_ref, bf16[208,256]{1,0:T(8,128)(2,1)} %get-tuple-element.21.refs_0_.pay_ref, bf16[208,256]{1,0:T(8,128)(2,1)} %copy-done.19, bf16[208,256]{1,0:T(8,128)(2,1)} %copy-done.18, ...), custom_call_target="tpu_custom_call" | custom-call | flops 4831838208 | bytes 4718592 | tf_op jit(solution)/shard_map/pallas_call | solution.py:345
  85.5 0.7 copy-done.14
  86.2 6.7 %all-to-all-start.2 = ((bf16[16,192,256]{2,1,0:T(8,128)(2,1)}), bf16[16,192,256]{2,1,0:T(8,128)(2,1)S(1)}, u32[]{:S(2)}, u32[]{:S(2)}) async-start(bf16[16,192,256]{2,1,0:T(8,128)(2,1)} %bitcast.33), calls=%async_computation.2 | async-start | bytes 3145728 | tf_op jit(solution)/shard_map/all_to_all | solution.py:265
  92.9 8.9 %shard_map.125 = (f32[4,192,256]{2,1,0:T(8,128)}, f32[4,192,256]{2,1,0:T(8,128)}) custom-call(s32[1]{0:T(128)} %bitcast.pos_ref, bf16[1536,256]{1,0:T(8,128)(2,1)} %get-tuple-element.23.vec, f32[1536,128]{1,0:T(8,128)} %get-tuple-element.24.freq, f32[16,24,128]{2,1,0:T(8,128)} %copy-done.14, bf16[3072,256]{1,0:T(8,128)(2,1)} %copy-done.10, ...), custom_call_target="tpu_custom_call" | custom-call | flops 4831838208 | bytes 4718592 | tf_op jit(solution)/shard_map/pallas_call | solution.py:359
  101.8 1.0 collective-permute-start.13
  102.8 2.1 %collective-permute-done.13 = f32[4,192,256]{2,1,0:T(8,128)S(1)} collective-permute-done((f32[4,192,256]{2,1,0:T(8,128)}, f32[4,192,256]{2,1,0:T(8,128)S(1)}, u32[]{:S(2)}, u32[]{:S(2)}) %collective-permute-start.13) | collective-permute-done | bytes 786464 | tf_op jit(solution)/shard_map/ppermute | solution.py:270
  104.9 1.3 fusion
  106.2 0.1 collective-permute-start.16
  106.3 1.6 collective-permute-start.15
  107.9 1.3 collective-permute-start.14
  109.2 8.6 %collective-permute-done.16.refs_3_ = f32[192,256]{1,0:T(8,128)S(1)} collective-permute-done((f32[192,256]{1,0:T(8,128)S(1)}, f32[192,256]{1,0:T(8,128)S(1)}, u32[]{:S(2)}, u32[]{:S(2)}) %collective-permute-start.16) | collective-permute-done | bytes 196640 | tf_op jit(solution)/shard_map/ppermute | solution.py:270
  117.8 0.3 collective-permute-done.14.refs_1_
  118.2 0.5 shard_map.126
  118.7 35.2 %all_to_all.30.got_ref = bf16[128,16,384]{2,1,0:T(8,128)(2,1)S(1)} all-to-all(bf16[128,16,384]{2,1,0:T(8,128)(2,1)S(1)} %bitcast.32), channel_id=1, replica_groups=mesh['x'=4,'y'=4,'c'=2,'z'=4] {'x','y','c','z'}, dimensions={0} | all-to-all | bytes 3145728 | tf_op jit(solution)/shard_map/all_to_all | solution.py:265
  153.9 1.2 copy-done.9
  155.0 0.1 convert_reduce_fusion
  155.2 0.8 broadcast_in_dim.20
  156.0 4.6 %all-to-all-start.5 = ((f32[64,16,128]{2,1,0:T(8,128)}), f32[64,16,128]{2,1,0:T(8,128)S(1)}, u32[]{:S(2)}, u32[]{:S(2)}) async-start(f32[64,16,128]{2,1,0:T(8,128)} %broadcast_in_dim.20), calls=%async_computation.5 | async-start | bytes 1048576 | tf_op jit(solution)/shard_map/all_to_all | solution.py:265
  160.6 1.3 compare_select_fusion
  161.9 0.7 reshape.91.ids_ref
  162.6 11.5 %shard_map.127 = (f32[2048,256]{1,0:T(8,128)}, f32[2048,256]{1,0:T(8,128)}) custom-call(s32[1,2048]{1,0:T(1,128)} %reshape.91.ids_ref, bf16[128,16,384]{2,1,0:T(8,128)(2,1)} %copy-done.9, f32[2048,256]{1,0:T(8,128)} %table_ref.1, f32[2048,256]{1,0:T(8,128)} %accum_ref.1, bf16[256,512]{1,0:T(8,128)(2,1)} %w_in_ref.3, bf16[512,256]{1,0:T(8,128)(2,1)} %w_out_ref.3), custom_call_target="tpu_custom_call" | custom-call | flops 4294967296 | bytes 8388608 | tf_op jit(solution)/shard_map/pallas_call | solution.py:407
  174.1 0.8 copy-done.7
  174.9 0.6 collective-permute-start.17
  175.6 0.3 copy-done.15
  175.9 0.1 constant_dynamic-slice_fusion
  176.0 1.3 shard_map.124
  177.3 0.1 collective-permute-done.17
  177.3 1.0 select_bitcast_fusion
  (70 shorter events, 0.5 us)
Async XLA Ops:
  3.8 16.2 %collective-permute-start.2 = (bf16[192,256]{1,0:T(8,128)(2,1)}, bf16[192,256]{1,0:T(8,128)(2,1)S(1)}, u32[]{:S(2)}, u32[]{:S(2)}) collective-permute-start(bf16[192,256]{1,0:T(8,128)(2,1)} %shard_map.120), channel_id=1, source_target_pairs={{0,1},{1,2},{2,3},{3,0},{4,5},{5,6},{6,7},{7,4},{8,9},{9,10},{10,1... | collective-permute-start | bytes 294920 | tf_op jit(solution)/shard_map/ppermute | solution.py:270
  6.3 13.7 %collective-permute-start.1 = (bf16[192,256]{1,0:T(8,128)(2,1)}, bf16[192,256]{1,0:T(8,128)(2,1)S(1)}, u32[]{:S(2)}, u32[]{:S(2)}) collective-permute-start(bf16[192,256]{1,0:T(8,128)(2,1)} %shard_map.120), channel_id=1, source_target_pairs={{0,2},{1,3},{2,0},{3,1},{4,6},{5,7},{6,4},{7,5},{8,10},{9,11},{10,... | collective-permute-start | bytes 294920 | tf_op jit(solution)/shard_map/ppermute | solution.py:270
  9.6 10.3 %collective-permute-start = (bf16[192,256]{1,0:T(8,128)(2,1)}, bf16[192,256]{1,0:T(8,128)(2,1)S(1)}, u32[]{:S(2)}, u32[]{:S(2)}) collective-permute-start(bf16[192,256]{1,0:T(8,128)(2,1)} %shard_map.120), channel_id=1, source_target_pairs={{0,3},{1,0},{2,1},{3,2},{4,7},{5,4},{6,5},{7,6},{8,11},{9,8},{10,9... | collective-permute-start | bytes 294920 | tf_op jit(solution)/shard_map/ppermute | solution.py:270
  10.3 15.5 %all-to-all-start = ((s32[32,1,128]{2,1,0:T(1,128)}), s32[32,1,128]{2,1,0:T(1,128)S(1)}, u32[]{:S(2)}, u32[]{:S(2)}) async-start(s32[32,1,128]{2,1,0:T(1,128)} %bitcast.38), calls=%async_computation | async-start | bytes 32768 | tf_op jit(solution)/shard_map/all_to_all | solution.py:265
  20.0 16.3 %copy-start.23 = (bf16[192]{0:T(256)(128)(2,1)S(1)}, bf16[192]{0:T(256)(128)(2,1)}, u32[]{:S(2)}) copy-start(bf16[192]{0:T(256)(128)(2,1)} %param.11) | copy-start | bytes 1156
  20.1 27.6 %collective-permute-start.4 = (bf16[768,256]{1,0:T(8,128)(2,1)S(1)}, bf16[768,256]{1,0:T(8,128)(2,1)S(1)}, u32[]{:S(2)}, u32[]{:S(2)}) collective-permute-start(bf16[768,256]{1,0:T(8,128)(2,1)S(1)} %constant_dynamic-update-slice_fusion.4), channel_id=1, source_target_pairs={{0,32},{32,64},{64,96},{96,0},{1,33},{33,65},{65,97},{97,1},{2,34}... | collective-permute-start | bytes 1179656 | tf_op jit(solution)/shard_map/ppermute | solution.py:270
  21.5 26.1 %collective-permute-start.3 = (bf16[768,256]{1,0:T(8,128)(2,1)S(1)}, bf16[768,256]{1,0:T(8,128)(2,1)S(1)}, u32[]{:S(2)}, u32[]{:S(2)}) collective-permute-start(bf16[768,256]{1,0:T(8,128)(2,1)S(1)} %constant_dynamic-update-slice_fusion.4), channel_id=1, source_target_pairs={{0,96},{32,0},{64,32},{96,64},{1,97},{33,1},{65,33},{97,65},{2,98}... | collective-permute-start | bytes 1179656 | tf_op jit(solution)/shard_map/ppermute | solution.py:270
  26.0 28.6 %collective-permute-start.12 = (bf16[768,256]{1,0:T(8,128)(2,1)S(1)}, bf16[768,256]{1,0:T(8,128)(2,1)S(1)}, u32[]{:S(2)}, u32[]{:S(2)}) collective-permute-start(bf16[768,256]{1,0:T(8,128)(2,1)S(1)} %constant_dynamic-update-slice_fusion.4), channel_id=1, source_target_pairs={{0,64},{32,96},{64,0},{96,32},{1,65},{33,97},{65,1},{97,33},{2,66}... | collective-permute-start | bytes 1179656 | tf_op jit(solution)/shard_map/ppermute | solution.py:270
  31.0 15.9 %all-to-all-start.1 = ((bf16[32,12,256]{2,1,0:T(8,128)(2,1)}), bf16[32,12,256]{2,1,0:T(8,128)(2,1)S(1)}, u32[]{:S(2)}, u32[]{:S(2)}) async-start(bf16[32,12,256]{2,1,0:T(8,128)(2,1)} %convert_element_type.23), calls=%async_computation.1 | async-start | bytes 524288 | tf_op jit(solution)/shard_map/all_to_all | solution.py:265
  47.6 0.7 copy-start.11
  47.6 0.9 copy-start.13
  50.9 10.4 %copy-start.12 = (bf16[768,256]{1,0:T(8,128)(2,1)S(1)}, bf16[768,256]{1,0:T(8,128)(2,1)}, u32[]{:S(2)}) copy-start(bf16[768,256]{1,0:T(8,128)(2,1)} %copy-done.11) | copy-start | bytes 1179652
  50.9 10.5 %collective-permute-start.8 = (bf16[208,256]{1,0:T(8,128)(2,1)}, bf16[208,256]{1,0:T(8,128)(2,1)S(1)}, u32[]{:S(2)}, u32[]{:S(2)}) collective-permute-start(bf16[208,256]{1,0:T(8,128)(2,1)} %get-tuple-element.21.refs_0_.pay_ref), channel_id=1, source_target_pairs={{0,4},{4,0},{1,5},{5,1},{2,6},{6,2},{3,7},{7,3},{8,12},{12,8},{9,1... | collective-permute-start | bytes 319496 | tf_op jit(solution)/shard_map/ppermute | solution.py:270
  51.5 4.8 %collective-permute-start.7 = (bf16[208,256]{1,0:T(8,128)(2,1)}, bf16[208,256]{1,0:T(8,128)(2,1)S(1)}, u32[]{:S(2)}, u32[]{:S(2)}) collective-permute-start(bf16[208,256]{1,0:T(8,128)(2,1)} %get-tuple-element.21.refs_0_.pay_ref), channel_id=1, source_target_pairs={{0,24},{8,0},{16,8},{24,16},{1,25},{9,1},{17,9},{25,17},{2,26},{10... | collective-permute-start | bytes 319496 | tf_op jit(solution)/shard_map/ppermute | solution.py:270
  51.9 5.6 %collective-permute-start.6 = (bf16[208,256]{1,0:T(8,128)(2,1)}, bf16[208,256]{1,0:T(8,128)(2,1)S(1)}, u32[]{:S(2)}, u32[]{:S(2)}) collective-permute-start(bf16[208,256]{1,0:T(8,128)(2,1)} %get-tuple-element.21.refs_0_.pay_ref), channel_id=1, source_target_pairs={{0,16},{8,24},{16,0},{24,8},{1,17},{9,25},{17,1},{25,9},{2,18},{10... | collective-permute-start | bytes 319496 | tf_op jit(solution)/shard_map/ppermute | solution.py:270
  53.6 6.9 %collective-permute-start.5 = (bf16[208,256]{1,0:T(8,128)(2,1)}, bf16[208,256]{1,0:T(8,128)(2,1)S(1)}, u32[]{:S(2)}, u32[]{:S(2)}) collective-permute-start(bf16[208,256]{1,0:T(8,128)(2,1)} %get-tuple-element.21.refs_0_.pay_ref), channel_id=1, source_target_pairs={{0,8},{8,16},{16,24},{24,0},{1,9},{9,17},{17,25},{25,1},{2,10},{10... | collective-permute-start | bytes 319496 | tf_op jit(solution)/shard_map/ppermute | solution.py:270
  56.3 5.9 %copy-start.17 = (bf16[208,256]{1,0:T(8,128)(2,1)}, bf16[208,256]{1,0:T(8,128)(2,1)S(1)}, u32[]{:S(2)}) copy-start(bf16[208,256]{1,0:T(8,128)(2,1)S(1)} %collective-permute-done.7.refs_3_) | copy-start | bytes 319492
  56.3 5.0 %collective-permute-start.11 = (bf16[208,256]{1,0:T(8,128)(2,1)S(1)}, bf16[208,256]{1,0:T(8,128)(2,1)S(1)}, u32[]{:S(2)}, u32[]{:S(2)}) collective-permute-start(bf16[208,256]{1,0:T(8,128)(2,1)S(1)} %collective-permute-done.7.refs_3_), channel_id=1, source_target_pairs={{0,4},{4,0},{1,5},{5,1},{2,6},{6,2},{3,7},{7,3},{8,12},{12,8},{9,1... | collective-permute-start | bytes 319496 | tf_op jit(solution)/shard_map/ppermute | solution.py:270
  57.5 4.7 %copy-start.18 = (bf16[208,256]{1,0:T(8,128)(2,1)}, bf16[208,256]{1,0:T(8,128)(2,1)S(1)}, u32[]{:S(2)}) copy-start(bf16[208,256]{1,0:T(8,128)(2,1)S(1)} %collective-permute-done.6.refs_2_) | copy-start | bytes 319492
  57.5 3.9 %collective-permute-start.10 = (bf16[208,256]{1,0:T(8,128)(2,1)S(1)}, bf16[208,256]{1,0:T(8,128)(2,1)S(1)}, u32[]{:S(2)}, u32[]{:S(2)}) collective-permute-start(bf16[208,256]{1,0:T(8,128)(2,1)S(1)} %collective-permute-done.6.refs_2_), channel_id=1, source_target_pairs={{0,4},{4,0},{1,5},{5,1},{2,6},{6,2},{3,7},{7,3},{8,12},{12,8},{9,1... | collective-permute-start | bytes 319496 | tf_op jit(solution)/shard_map/ppermute | solution.py:270
  60.5 1.8 copy-start.19
  60.5 1.8 collective-permute-start.9
  61.3 1.1 copy-start.10
  61.3 1.1 copy-start.16
  61.3 1.1 copy-start.20
  61.4 1.2 copy-start.21
  62.5 0.6 copy-start.22
  72.1 13.4 %all-to-all-start.3 = ((f32[16,24,128]{2,1,0:T(8,128)}), f32[16,24,128]{2,1,0:T(8,128)S(1)}, u32[]{:S(2)}, u32[]{:S(2)}) async-start(f32[16,24,128]{2,1,0:T(8,128)} %shard_map.122.refs_8_), calls=%async_computation.3 | async-start | bytes 393216 | tf_op jit(solution)/shard_map/all_to_all | solution.py:265
  85.5 0.7 copy-start.14
  86.2 32.0 %all-to-all-start.2 = ((bf16[16,192,256]{2,1,0:T(8,128)(2,1)}), bf16[16,192,256]{2,1,0:T(8,128)(2,1)S(1)}, u32[]{:S(2)}, u32[]{:S(2)}) async-start(bf16[16,192,256]{2,1,0:T(8,128)(2,1)} %bitcast.33), calls=%async_computation.2 | async-start | bytes 3145728 | tf_op jit(solution)/shard_map/all_to_all | solution.py:265
  101.7 16.5 %copy-start = (bf16[512,256]{1,0:T(8,128)(2,1)S(1)}, bf16[512,256]{1,0:T(8,128)(2,1)}, u32[]{:S(2)}) copy-start(bf16[512,256]{1,0:T(8,128)(2,1)} %w_out_ref.3) | copy-start | bytes 786436
  101.7 16.5 %copy-start.2 = (bf16[192,512]{1,0:T(8,128)(2,1)S(1)}, bf16[192,512]{1,0:T(8,128)(2,1)}, u32[]{:S(2)}) copy-start(bf16[192,512]{1,0:T(8,128)(2,1)} %get-tuple-element.28.refs_5_) | copy-start | bytes 589828
  101.7 16.5 %copy-start.4 = (bf16[192,256]{1,0:T(8,128)(2,1)S(1)}, bf16[192,256]{1,0:T(8,128)(2,1)}, u32[]{:S(2)}) copy-start(bf16[192,256]{1,0:T(8,128)(2,1)} %get-tuple-element.27.refs_4_) | copy-start | bytes 294916
  101.7 16.5 %copy-start.5 = (f32[32,256]{1,0:T(8,128)S(1)}, f32[32,256]{1,0:T(8,128)}, u32[]{:S(2)}) copy-start(f32[32,256]{1,0:T(8,128)} %get-tuple-element.30.refs_8_) | copy-start | bytes 98308
  101.8 16.5 %copy-start.6 = (s32[1,256]{1,0:T(1,128)S(1)}, s32[1,256]{1,0:T(1,128)}, u32[]{:S(2)}) copy-start(s32[1,256]{1,0:T(1,128)} %get-tuple-element.29.refs_7_) | copy-start | bytes 3076
  101.8 3.1 %collective-permute-start.13 = (f32[4,192,256]{2,1,0:T(8,128)}, f32[4,192,256]{2,1,0:T(8,128)S(1)}, u32[]{:S(2)}, u32[]{:S(2)}) collective-permute-start(f32[4,192,256]{2,1,0:T(8,128)} %get-tuple-element.26), channel_id=1, source_target_pairs={{0,4},{4,0},{1,5},{5,1},{2,6},{6,2},{3,7},{7,3},{8,12},{12,8},{9,1... | collective-permute-start | bytes 2359304 | tf_op jit(solution)/shard_map/ppermute | solution.py:270
  106.2 11.6 %collective-permute-start.16 = (f32[192,256]{1,0:T(8,128)S(1)}, f32[192,256]{1,0:T(8,128)S(1)}, u32[]{:S(2)}, u32[]{:S(2)}) collective-permute-start(f32[192,256]{1,0:T(8,128)S(1)} %get-tuple-element.33), channel_id=1, source_target_pairs={{0,8},{8,16},{16,24},{24,0},{1,9},{9,17},{17,25},{25,1},{2,10},{10... | collective-permute-start | bytes 589832 | tf_op jit(solution)/shard_map/ppermute | solution.py:270
  106.3 11.5 %collective-permute-start.15 = (f32[192,256]{1,0:T(8,128)S(1)}, f32[192,256]{1,0:T(8,128)S(1)}, u32[]{:S(2)}, u32[]{:S(2)}) collective-permute-start(f32[192,256]{1,0:T(8,128)S(1)} %get-tuple-element.34), channel_id=1, source_target_pairs={{0,16},{8,24},{16,0},{24,8},{1,17},{9,25},{17,1},{25,9},{2,18},{10... | collective-permute-start | bytes 589832 | tf_op jit(solution)/shard_map/ppermute | solution.py:270
  107.9 10.3 %collective-permute-start.14 = (f32[192,256]{1,0:T(8,128)S(1)}, f32[192,256]{1,0:T(8,128)S(1)}, u32[]{:S(2)}, u32[]{:S(2)}) collective-permute-start(f32[192,256]{1,0:T(8,128)S(1)} %get-tuple-element.35), channel_id=1, source_target_pairs={{0,24},{8,0},{16,8},{24,16},{1,25},{9,1},{17,9},{25,17},{2,26},{10... | collective-permute-start | bytes 589832 | tf_op jit(solution)/shard_map/ppermute | solution.py:270
  153.9 1.2 copy-start.9
  156.0 18.1 %all-to-all-start.5 = ((f32[64,16,128]{2,1,0:T(8,128)}), f32[64,16,128]{2,1,0:T(8,128)S(1)}, u32[]{:S(2)}, u32[]{:S(2)}) async-start(f32[64,16,128]{2,1,0:T(8,128)} %broadcast_in_dim.20), calls=%async_computation.5 | async-start | bytes 1048576 | tf_op jit(solution)/shard_map/all_to_all | solution.py:265
  174.1 0.8 copy-start.7
  174.9 0.9 copy-start.15
  174.9 1.1 copy-start.1
  174.9 1.1 copy-start.3
  174.9 2.4 %copy-start.8 = (f32[64,16,128]{2,1,0:T(8,128)S(1)}, f32[64,16,128]{2,1,0:T(8,128)}, u32[]{:S(2)}) copy-start(f32[64,16,128]{2,1,0:T(8,128)} %shard_map.128) | copy-start | bytes 1572868
  174.9 2.4 %collective-permute-start.17 = (f32[64,16,128]{2,1,0:T(8,128)}, f32[64,16,128]{2,1,0:T(8,128)S(1)}, u32[]{:S(2)}, u32[]{:S(2)}) collective-permute-start(f32[64,16,128]{2,1,0:T(8,128)} %shard_map.128), channel_id=1, source_target_pairs={{0,4},{4,0},{1,5},{5,1},{2,6},{6,2},{3,7},{7,3},{8,12},{12,8},{9,1... | collective-permute-start | bytes 1572872 | tf_op jit(solution)/shard_map/ppermute | solution.py:270

commit v3 on v2

--- a/solution.py
+++ b/solution.py
@@ -23,8 +23,7 @@
 
 SHARD = ("x", "y", "c")
 ALL = ("x", "y", "c", "z")
-CHIPS = ("x", "y", "z")
-A = ("x", "z")
+A = ("z", "x")
 
 f32 = jnp.float32
 bf16 = jnp.bfloat16
@@ -111,34 +110,40 @@
         vec[at, :] = vec_refs[b][0:PAIRS, :]
 
 
-def lanes(col):
-    return jnp.concatenate([col] * (QB // 128), axis=1)
+def lanes(col, n=QB):
+    return jnp.concatenate([col] * (n // 128), axis=1)
+
+
+PB = 512
 
 
 def score_kernel(*refs):
-    vec_refs, (q_ref, lse_ref, vec, freq, scores) = refs[:NB], refs[NB:]
-
-    @pl.when(pl.program_id(0) == 0)
-    def _():
-        load_vecs(vec_refs, vec, freq)
-
-    q = q_ref[...] * jnp.asarray(score_scale, bf16)
-    top = None
-    for b in range(0, VS, VB):
-        at = slice(b, b + VB)
-        s = mm(vec[at, :], q, NT) - lanes(freq[at, :])
-        scores[at, :] = s
-        t = jnp.max(s.reshape(VB // 8, 8, QB), axis=0)
-        top = t if top is None else jnp.maximum(top, t)
-    top = jnp.max(top, axis=0, keepdims=True)
-    total = jnp.zeros((8, QB), f32)
-    for b in range(0, VS, VB):
-        e = jnp.exp(scores[b : b + VB, :] - top)
-        total = total + jnp.sum(e.reshape(VB // 8, 8, QB), axis=0)
-    part = top + jnp.log(jnp.sum(total, axis=0, keepdims=True))
-    for k in range(QB // 128):
-        row = jnp.broadcast_to(part[:, k * 128 : (k + 1) * 128].reshape(1, 1, 128), (NA, 1, 128))
-        lse_ref[:, pl.ds(pl.program_id(0) * (QB // 128) + k, 1), :] = row
+    vec_refs, (q_ref, lse_ref, vec, freq, *scores) = refs[:NB], refs[NB:]
+    load_vecs(vec_refs, vec, freq)
+    tops = []
+    for j in range(QS // PB + 1):
+        top, total = None, jnp.zeros((8, PB), f32)
+        if j < QS // PB:
+            q = q_ref[j * PB : (j + 1) * PB, :] * jnp.asarray(score_scale, bf16)
+        for b in range(0, VS, VB):
+            at = slice(b, b + VB)
+            if j < QS // PB:
+                s = mm(vec[at, :], q, NT) - lanes(freq[at, :], PB)
+                scores[j % 2][at, :] = s
+                t = jnp.max(s.reshape(VB // 8, 8, PB), axis=0)
+                top = t if top is None else jnp.maximum(top, t)
+            if j > 0:
+                e = jnp.exp(scores[(j - 1) % 2][at, :] - tops[j - 1])
+                total = total + jnp.sum(e.reshape(VB // 8, 8, PB), axis=0)
+        if j < QS // PB:
+            tops.append(jnp.max(top, axis=0, keepdims=True))
+        if j > 0:
+            part = tops[j - 1] + jnp.log(jnp.sum(total, axis=0, keepdims=True))
+            n = PB // 128
+            for k in range(n):
+                row = part[:, k * 128 : (k + 1) * 128].reshape(1, 1, 128)
+                at = (j - 1) * n + k
+                lse_ref[:, at : at + 1, :] = jnp.broadcast_to(row, (NA, 1, 128))
 
 
 def is_pair(pos_ref):
@@ -244,7 +249,12 @@
 TB = 512
 
 
-def update_kernel(ids_ref, got_ref, table_ref, accum_ref, w_in_ref, w_out_ref, table_out, accum_out):
+def active_kernel(table_ref, w_in_ref, active_ref):
+    hid = jnp.maximum(mm(table_ref[...].astype(bf16), w_in_ref[...]), 0.0).astype(bf16)
+    active_ref[...] = (hid.astype(f32) > 0.0).astype(f32).astype(bf16)
+
+
+def update_kernel(ids_ref, got_ref, table_ref, accum_ref, active_ref, w_in_ref, w_out_ref, table_out, accum_out):
     base = pl.program_id(0) * TB
     onehot = (ids_ref[...] == iota((TB, 128 * SLOT), 0) + base).astype(f32).astype(bf16)
     vals = got_ref[:, :, 0:E].reshape(128 * SLOT, E)
@@ -252,9 +262,8 @@
     high = vg.astype(bf16)
     low = (vg - high.astype(f32)).astype(bf16)
     table = table_ref[...]
-    hid = jnp.maximum(mm(table.astype(bf16), w_in_ref[...]), 0.0).astype(bf16).astype(f32)
     back = mm(high, w_out_ref[...], NT) + mm(low, w_out_ref[...], NT)
-    hg = jnp.where(hid > 0.0, back, 0.0).astype(bf16)
+    hg = jnp.where(active_ref[...].astype(f32) > 0.0, back, 0.0).astype(bf16)
     g = vg + mm(hg, w_in_ref[...], NT)
     acc = accum_ref[...] + g * g
     accum_out[...] = acc
@@ -279,13 +288,7 @@
 
 
 def after(x, *others):
-    return pl.pallas_call(
-        lambda *refs: None,
-        out_shape=sds(x.shape, x.dtype),
-        in_specs=unread(1 + len(others)),
-        out_specs=unread(1)[0],
-        input_output_aliases={0: 0},
-    )(x, *others)
+    return lax.optimization_barrier((x, *others))[0]
 
 
 def const(*shape):
@@ -308,15 +311,14 @@
         scratch_shapes=[pltpu.VMEM((8, 256), i32)],
     )(item_owner.reshape(1, PAIRS), item_row.reshape(1, PAIRS))
     asked = a2a(req.reshape(OWNERS, 1, 128), SHARD)
-    early = after(queries, req)
     slab = jnp.zeros((QB, E), bf16)
     for k in range(4):
-        block = shift(early, "z", 4 - k) if k else queries
-        slab = lax.dynamic_update_slice(slab, block, ((here_z + k) % 4 * PAIRS, 0))
-    slabs = [slab] + [shift(slab, "x", 4 - k) for k in range(1, 4)]
+        block = shift(queries, "x", 4 - k) if k else queries
+        slab = lax.dynamic_update_slice(slab, block, ((here_x + k) % 4 * PAIRS, 0))
+    slabs = [slab] + [shift(slab, "z", 4 - k) for k in range(1, 4)]
     all_q = jnp.zeros((QS, E), bf16)
     for k in range(4):
-        all_q = lax.dynamic_update_slice(all_q, slabs[k], ((here_x + k) % 4 * QB, 0))
+        all_q = lax.dynamic_update_slice(all_q, slabs[k], ((here_z + k) % 4 * QB, 0))
     wanted = jnp.maximum(asked[:, 0, :CAP].reshape(OWNERS * CAP), 0)
     picked = table.at[wanted].get(mode="promise_in_bounds").astype(bf16)
     got = a2a(picked.reshape(OWNERS, CAP, E), SHARD).reshape(OWNERS * CAP, E)
@@ -324,9 +326,9 @@
     emb, hid, pay = call(
         tower_kernel,
         (sds((PAIRS, E), bf16), sds((PAIRS, H), bf16), sds((PAIRS + 16, E), bf16)),
-        in_specs=whole(5) + unread(2),
+        in_specs=whole(5) + unread(1),
         out_specs=tuple(whole(3)),
-    )(got, pick, w_in, w_out, freq_row, slabs[1], slabs[3])
+    )(got, pick, w_in, w_out, freq_row, slab)
     vecs = [pay] + [shift(pay, "y", k) for k in range(1, 4)]
     vecs = vecs + [shift(v, "c", 1) for v in vecs]
 
@@ -335,13 +337,12 @@
         sds((NA, QS // 128, 128), f32),
         cost=(2 * VS * QS * E, VS * QS * 2, VS * QS),
         limit=LIMIT,
-        grid=(QS // QB,),
-        in_specs=[const(PAIRS + 16, E)] * NB + [pl.BlockSpec((QB, E), lambda i: (i, 0))],
-        out_specs=const(NA, QS // 128, 128),
-        scratch_shapes=[pltpu.VMEM((VS, E), bf16), pltpu.VMEM((VS, 128), f32), pltpu.VMEM((VS, QB), f32)],
+        in_specs=whole(NB + 1),
+        out_specs=whole(1)[0],
+        scratch_shapes=[pltpu.VMEM((VS, E), bf16), pltpu.VMEM((VS, 128), f32)] + [pltpu.VMEM((VS, PB), f32)] * 2,
     )(*vecs, all_q)
     all_lse = a2a(part_lse, A)
-    here = here_x * 4 + here_z
+    here = here_z * 4 + here_x
     o, vec_all, freq_all = call(
         query_kernel,
         (sds((QS, E), bf16), sds((VS, E), bf16), sds((VS, 128), f32)),
@@ -398,8 +399,18 @@
         out_specs=whole(1)[0],
     )(o_got, jnp.pad(own, ((0, 0), (0, 256 - PAIRS))), queries, pay)
 
+    active = call(
+        active_kernel,
+        sds((ROWS, H), bf16),
+        cost=(2 * ROWS * E * H, ROWS * (E * 4 + H * 2), 0),
+        limit=SMALL,
+        grid=(ROWS // TB,),
+        in_specs=[pl.BlockSpec((TB, E), lambda i: (i, 0)), const(E, H)],
+        out_specs=pl.BlockSpec((TB, H), lambda i: (i, 0)),
+    )(table, w_in)
     w_sum = jnp.sum(back[:, :, E:].astype(f32), axis=0)
-    w_mine = a2a(jnp.broadcast_to(w_sum[None], (64, SLOT, 128)), CHIPS)
+    w_sum = after(jnp.broadcast_to(w_sum.astype(bf16)[None], (128, SLOT, 128)), query_grad, active)
+    w_all = a2a(w_sum, ALL).reshape(16, 2, 4, SLOT, 128).astype(f32)
     hi = back[:, CAP, 0:CAP].astype(i32)
     lo = back[:, CAP, 128 : 128 + CAP].astype(i32)
     row_ids = jnp.where(hi < 0, -1, hi * 256 + lo)
@@ -415,6 +426,7 @@
             const(128, SLOT, E + 128),
             pl.BlockSpec((TB, E), lambda i: (i, 0)),
             pl.BlockSpec((TB, E), lambda i: (i, 0)),
+            pl.BlockSpec((TB, H), lambda i: (i, 0)),
             const(E, H),
             const(H, E),
         ],
@@ -422,17 +434,13 @@
             pl.BlockSpec((TB, E), lambda i: (i, 0)),
             pl.BlockSpec((TB, E), lambda i: (i, 0)),
         ),
-    )(row_ids, back, table, accum, w_in, w_out)
-    w_mine = after(w_mine, table_new)
-    w_other = shift(w_mine, "c", 1)
-    zero = lax.axis_index("c") == 0
+    )(row_ids, back, table, accum, active, w_in, w_out)
 
     def tiles(x, rows, cols):
         return x.reshape(rows // 8, cols // 128, 8, 128).transpose(0, 2, 1, 3).reshape(rows, cols)
 
-    w_out_grad = tiles(jnp.where(zero, w_mine, w_other), H, E)
-    w_in_grad = tiles(jnp.where(zero, w_other, w_mine), E, H)
-
+    w_out_grad = tiles(w_all[:, 0], H, E)
+    w_in_grad = tiles(w_all[:, 1], E, H)
     return query_grad, table_new, accum_new, w_in_grad, w_out_grad
 
 

time: 179 us -> 170 us (0.950)
  blocking collectives: 35.2 us -> 0 us
  waiting for transfers between devices: 27.3 us -> 48.5 us
  starting transfers between devices: 50.9 us -> 57.3 us
  other arithmetic: 3.83 us -> 1.76 us
    all_to_all x1 -> x0, blocking collectives: 35.2 us -> none  [a2a(): return lax.all_to_all(x, axes, split_axis=0, concat_axis=0, tiled=True)]
    all_to_all x5 -> x6, waiting for transfers between devices: 12.8 us -> 30.8 us  [a2a(): return lax.all_to_all(x, axes, split_axis=0, concat_axis=0, tiled=True)]
    all_to_all x5 -> x6, starting transfers between devices: 29.1 us -> 34.2 us  [a2a(): return lax.all_to_all(x, axes, split_axis=0, concat_axis=0, tiled=True)]
    ppermute x18 -> x17, waiting for transfers between devices: 14.5 us -> 17.8 us  [shift(): return lax.ppermute(x, axis, [(i, (i + k) % n) for i in range(n)])]
    unnamed x50 -> x47, local copies, waits for them, and re-layouts: 6.34 us -> 4.6 us
    ppermute x18 -> x17, starting transfers between devices: 21.8 us -> 23.1 us  [shift(): return lax.ppermute(x, axis, [(i, (i + k) % n) for i in range(n)])]
  transfers between devices with their start and end apart: 23 -> 23, of which waited for: 9 -> 13; matrix products, arithmetic and copies ran while one was open for 6% -> 5% of each run, Pallas kernels for 19% -> 21%
where the time goes in v3:
time: 170 us; the launch traced here: 169 us
  starting transfers between devices  57.3 us (34%)
  waiting for transfers between devices  48.5 us (29%)
  Pallas kernels  46.1 us (27%)
  local copies, waits for them, and re-layouts  14.2 us (8%)
  other arithmetic  1.76 us (1%)
    all_to_all x6, starting transfers between devices, a2a(): return lax.all_to_all(x, axes, split_axis=0, concat_axis=0, tiled=True)  34.2 us
    all_to_all x6, waiting for transfers between devices, a2a(): return lax.all_to_all(x, axes, split_axis=0, concat_axis=0, tiled=True)  30.8 us
    ppermute x17, starting transfers between devices, shift(): return lax.ppermute(x, axis, [(i, (i + k) % n) for i in range(n)])  23.1 us
    ppermute x17, waiting for transfers between devices, shift(): return lax.ppermute(x, axis, [(i, (i + k) % n) for i in range(n)])  17.8 us
    pallas_call x1, Pallas kernels, local(): call(update_kernel, (sds((ROWS, E), f32), sds((ROWS, E), f32)), cost=(4 *...  11.3 us
    pallas_call x1, Pallas kernels, local(): call(query_kernel, (sds((QS, E), bf16), sds((VS, E), bf16), sds((VS, 128)...  9.41 us
    pallas_call x1, Pallas kernels, local(): call(vec_kernel, (sds((4, PAIRS, E), f32), sds((4, PAIRS, E), f32)), cost...  8.88 us
    pallas_call x1, Pallas kernels, local(): call(score_kernel, sds((NA, QS // 128, 128), f32), cost=(2 * VS * QS * E,...  8.25 us
  transfers between devices with their start and end apart: 23, of which 13 were waited for; matrix products, arithmetic and copies ran while one was open for 5% of the time, Pallas kernels for 21%

profile of v3, /device:TPU:1, one launch (start us, length us, event | category | flops | bytes accessed | tf_op | source)
XLA Modules:
  0.0 168.9 jit_solution(4796435139798171574)
XLA Ops:
  0.6 3.4 %collective-permute-start = (bf16[192,256]{1,0:T(8,128)(2,1)}, bf16[192,256]{1,0:T(8,128)(2,1)S(1)}, u32[]{:S(2)}, u32[]{:S(2)}) collective-permute-start(bf16[192,256]{1,0:T(8,128)(2,1)} %q_ref.1), channel_id=1, source_target_pairs={{0,96},{32,0},{64,32},{96,64},{1,97},{33,1},{65,33},{97,65},{2,98}... | collective-permute-start | bytes 294920 | tf_op jit(solution)/shard_map/ppermute | solution.py:279
  4.0 0.5 collective-permute-start.1
  4.5 0.6 collective-permute-start.2
  5.1 1.7 shard_map.119
  6.8 7.9 %all-to-all-start = ((s32[32,1,128]{2,1,0:T(1,128)}), s32[32,1,128]{2,1,0:T(1,128)S(1)}, u32[]{:S(2)}, u32[]{:S(2)}) async-start(s32[32,1,128]{2,1,0:T(1,128)} %bitcast.40), calls=%async_computation | async-start | bytes 32768 | tf_op jit(solution)/shard_map/all_to_all | solution.py:274
  14.8 0.9 constant_dynamic-update-slice_fusion.7
  15.9 3.8 %collective-permute-start.10 = (bf16[768,256]{1,0:T(8,128)(2,1)S(1)}, bf16[768,256]{1,0:T(8,128)(2,1)S(1)}, u32[]{:S(2)}, u32[]{:S(2)}) collective-permute-start(bf16[768,256]{1,0:T(8,128)(2,1)S(1)} %constant_dynamic-update-slice_fusion.4.refs_0_), channel_id=1, source_target_pairs={{0,3},{1,0},{2,1},{3,2},{4,7},{5,4},{6,5},{7,6},{8,11},{9,8},{10,9... | collective-permute-start | bytes 1179656 | tf_op jit(solution)/shard_map/ppermute | solution.py:279
  19.7 1.9 %all-to-all-done = s32[32,1,128]{2,1,0:T(1,128)S(1)} async-done(((s32[32,1,128]{2,1,0:T(1,128)}), s32[32,1,128]{2,1,0:T(1,128)S(1)}, u32[]{:S(2)}, u32[]{:S(2)}) %all-to-all-start) | async-done | bytes 16416 | tf_op jit(solution)/shard_map/all_to_all | solution.py:274
  21.6 0.1 fusion.5
  21.7 0.1 reshape.94
  21.8 3.7 %collective-permute-start.11 = (bf16[768,256]{1,0:T(8,128)(2,1)S(1)}, bf16[768,256]{1,0:T(8,128)(2,1)S(1)}, u32[]{:S(2)}, u32[]{:S(2)}) collective-permute-start(bf16[768,256]{1,0:T(8,128)(2,1)S(1)} %constant_dynamic-update-slice_fusion.4.refs_0_), channel_id=1, source_target_pairs={{0,2},{1,3},{2,0},{3,1},{4,6},{5,7},{6,4},{7,5},{8,10},{9,11},{10,... | collective-permute-start | bytes 1179656 | tf_op jit(solution)/shard_map/ppermute | solution.py:279
  25.4 3.3 %gather_fusion = bf16[384,256]{1,0:T(8,128)(2,1)S(1)} fusion(f32[2048,256]{1,0:T(8,128)} %table_ref.3, s32[1024]{0:T(1024)S(1)} %pad_clamp_fusion), kind=kCustom, calls=%fused_computation | custom fusion | bytes 394752 | tf_op jit(solution)/shard_map/gather | solution.py:323
  28.7 0.7 convert_element_type.28
  29.5 4.5 %all-to-all-start.1 = ((bf16[32,12,256]{2,1,0:T(8,128)(2,1)}), bf16[32,12,256]{2,1,0:T(8,128)(2,1)S(1)}, u32[]{:S(2)}, u32[]{:S(2)}) async-start(bf16[32,12,256]{2,1,0:T(8,128)(2,1)} %convert_element_type.28), calls=%async_computation.1 | async-start | bytes 524288 | tf_op jit(solution)/shard_map/all_to_all | solution.py:274
  33.9 0.8 collective-permute-start.12
  34.7 0.6 pad.12.freq_ref
  35.3 0.1 broadcast_in_dim.18
  35.5 7.5 %all-to-all-done.1 = bf16[32,12,256]{2,1,0:T(8,128)(2,1)S(1)} async-done(((bf16[32,12,256]{2,1,0:T(8,128)(2,1)}), bf16[32,12,256]{2,1,0:T(8,128)(2,1)S(1)}, u32[]{:S(2)}, u32[]{:S(2)}) %all-to-all-start.1) | async-done | bytes 196640 | tf_op jit(solution)/shard_map/all_to_all | solution.py:274
  43.0 0.7 reshape.83.got_ref
  43.7 2.4 %shard_map.120 = (bf16[192,256]{1,0:T(8,128)(2,1)}, bf16[192,512]{1,0:T(8,128)(2,1)}, bf16[208,256]{1,0:T(8,128)(2,1)}) custom-call(bf16[384,256]{1,0:T(8,128)(2,1)} %reshape.83.got_ref, bf16[192,384]{1,0:T(8,128)(2,1)} %get-tuple-element.21.pick_ref, bf16[256,512]{1,0:T(8,128)(2,1)} %w_in_ref.5, bf16[512,256]{1,0:T(8,128)(2,1)} %w_out_ref.3, ...), custom_call_target="tpu_custom_call" | custom-call | tf_op jit(solution)/shard_map/pallas_call | solution.py:326
  46.1 0.2 collective-permute-start.3
  46.3 1.9 %collective-permute-start.4 = (bf16[208,256]{1,0:T(8,128)(2,1)}, bf16[208,256]{1,0:T(8,128)(2,1)S(1)}, u32[]{:S(2)}, u32[]{:S(2)}) collective-permute-start(bf16[208,256]{1,0:T(8,128)(2,1)} %get-tuple-element.22.refs_0_.pay_ref), channel_id=1, source_target_pairs={{0,16},{8,24},{16,0},{24,8},{1,17},{9,25},{17,1},{25,9},{2,18},{10... | collective-permute-start | bytes 319496 | tf_op jit(solution)/shard_map/ppermute | solution.py:279
  48.3 0.5 collective-permute-start.5
  48.8 3.4 %collective-permute-done.3.refs_1_ = bf16[208,256]{1,0:T(8,128)(2,1)S(1)} collective-permute-done((bf16[208,256]{1,0:T(8,128)(2,1)}, bf16[208,256]{1,0:T(8,128)(2,1)S(1)}, u32[]{:S(2)}, u32[]{:S(2)}) %collective-permute-start.3) | collective-permute-done | bytes 106528 | tf_op jit(solution)/shard_map/ppermute | solution.py:279
  52.2 3.0 %collective-permute-start.6 = (bf16[208,256]{1,0:T(8,128)(2,1)}, bf16[208,256]{1,0:T(8,128)(2,1)S(1)}, u32[]{:S(2)}, u32[]{:S(2)}) collective-permute-start(bf16[208,256]{1,0:T(8,128)(2,1)} %get-tuple-element.22.refs_0_.pay_ref), channel_id=1, source_target_pairs={{0,4},{4,0},{1,5},{5,1},{2,6},{6,2},{3,7},{7,3},{8,12},{12,8},{9,1... | collective-permute-start | bytes 319496 | tf_op jit(solution)/shard_map/ppermute | solution.py:279
  55.2 0.1 collective-permute-start.7
  55.3 0.5 collective-permute-start.8
  55.8 0.3 collective-permute-start.9
  56.2 0.2 collective-permute-done.6.refs_4_
  56.4 0.2 collective-permute-done.7.refs_5_
  56.5 0.3 collective-permute-done.8.refs_6_
  56.8 0.4 collective-permute-done.9.refs_7_
  57.2 0.2 copy-done.12
  57.4 0.6 copy-done.21
  58.1 8.2 %shard_map.121.refs_8_ = f32[16,24,128]{2,1,0:T(8,128)} custom-call(bf16[208,256]{1,0:T(8,128)(2,1)} %get-tuple-element.22.refs_0_.pay_ref, bf16[208,256]{1,0:T(8,128)(2,1)} %copy-done.15, bf16[208,256]{1,0:T(8,128)(2,1)} %copy-done.16, bf16[208,256]{1,0:T(8,128)(2,1)} %copy-done.17, bf16[208,256]{1,0:T(8,128)(2,1)} %copy-done.18, ...), custom_call_target="tpu_custom_call" | custom-call | flops 2415919104 | bytes 9437184 | tf_op jit(solution)/shard_map/pallas_call | solution.py:335
  66.3 3.5 %all-to-all-start.3 = ((f32[16,24,128]{2,1,0:T(8,128)}), f32[16,24,128]{2,1,0:T(8,128)S(1)}, u32[]{:S(2)}, u32[]{:S(2)}) async-start(f32[16,24,128]{2,1,0:T(8,128)} %shard_map.121.refs_8_), calls=%async_computation.3 | async-start | bytes 393216 | tf_op jit(solution)/shard_map/all_to_all | solution.py:274
  69.8 9.4 %shard_map.122 = (bf16[3072,256]{1,0:T(8,128)(2,1)}, bf16[1536,256]{1,0:T(8,128)(2,1)}, f32[1536,128]{1,0:T(8,128)}) custom-call(s32[1]{0:T(128)} %bitcast.pos_ref, bf16[208,256]{1,0:T(8,128)(2,1)} %get-tuple-element.22.refs_0_.pay_ref, bf16[208,256]{1,0:T(8,128)(2,1)} %copy-done.15, bf16[208,256]{1,0:T(8,128)(2,1)} %copy-done.16, ...), custom_call_target="tpu_custom_call" | custom-call | flops 4831838208 | bytes 4718592 | tf_op jit(solution)/shard_map/pallas_call | solution.py:346
  79.3 0.7 copy-done.13
  79.9 6.6 %all-to-all-start.2 = ((bf16[16,192,256]{2,1,0:T(8,128)(2,1)}), bf16[16,192,256]{2,1,0:T(8,128)(2,1)S(1)}, u32[]{:S(2)}, u32[]{:S(2)}) async-start(bf16[16,192,256]{2,1,0:T(8,128)(2,1)} %bitcast.34), calls=%async_computation.2 | async-start | bytes 3145728 | tf_op jit(solution)/shard_map/all_to_all | solution.py:274
  86.5 8.9 %shard_map.124 = (f32[4,192,256]{2,1,0:T(8,128)}, f32[4,192,256]{2,1,0:T(8,128)}) custom-call(s32[1]{0:T(128)} %bitcast.pos_ref, bf16[1536,256]{1,0:T(8,128)(2,1)} %get-tuple-element.24.vec, f32[1536,128]{1,0:T(8,128)} %get-tuple-element.25.freq, f32[16,24,128]{2,1,0:T(8,128)} %copy-done.13, bf16[3072,256]{1,0:T(8,128)(2,1)} %copy-done.12, ...), custom_call_target="tpu_custom_call" | custom-call | flops 4831838208 | bytes 4718592 | tf_op jit(solution)/shard_map/pallas_call | solution.py:360
  95.4 1.0 collective-permute-start.13
  96.4 2.1 %collective-permute-done.13 = f32[4,192,256]{2,1,0:T(8,128)S(1)} collective-permute-done((f32[4,192,256]{2,1,0:T(8,128)}, f32[4,192,256]{2,1,0:T(8,128)S(1)}, u32[]{:S(2)}, u32[]{:S(2)}) %collective-permute-start.13) | collective-permute-done | bytes 786464 | tf_op jit(solution)/shard_map/ppermute | solution.py:279
  98.6 1.3 fusion
  99.9 2.1 %collective-permute-start.14 = (f32[192,256]{1,0:T(8,128)S(1)}, f32[192,256]{1,0:T(8,128)S(1)}, u32[]{:S(2)}, u32[]{:S(2)}) collective-permute-start(f32[192,256]{1,0:T(8,128)S(1)} %get-tuple-element.37), channel_id=1, source_target_pairs={{0,24},{8,0},{16,8},{24,16},{1,25},{9,1},{17,9},{25,17},{2,26},{10... | collective-permute-start | bytes 589832 | tf_op jit(solution)/shard_map/ppermute | solution.py:279
  102.0 0.7 collective-permute-start.16
  102.7 3.6 %collective-permute-done.14.refs_1_ = f32[192,256]{1,0:T(8,128)S(1)} collective-permute-done((f32[192,256]{1,0:T(8,128)S(1)}, f32[192,256]{1,0:T(8,128)S(1)}, u32[]{:S(2)}, u32[]{:S(2)}) %collective-permute-start.14) | collective-permute-done | bytes 196640 | tf_op jit(solution)/shard_map/ppermute | solution.py:279
  106.3 3.1 %collective-permute-done.15.refs_2_ = f32[192,256]{1,0:T(8,128)S(1)} collective-permute-done((f32[192,256]{1,0:T(8,128)S(1)}, f32[192,256]{1,0:T(8,128)S(1)}, u32[]{:S(2)}, u32[]{:S(2)}) %collective-permute-start.15) | collective-permute-done | bytes 196640 | tf_op jit(solution)/shard_map/ppermute | solution.py:279
  109.4 4.5 %collective-permute-done.16.refs_3_ = f32[192,256]{1,0:T(8,128)S(1)} collective-permute-done((f32[192,256]{1,0:T(8,128)S(1)}, f32[192,256]{1,0:T(8,128)S(1)}, u32[]{:S(2)}, u32[]{:S(2)}) %collective-permute-start.16) | collective-permute-done | bytes 196640 | tf_op jit(solution)/shard_map/ppermute | solution.py:279
  114.0 1.6 shard_map.125
  115.6 7.9 %all-to-all-start.4 = ((bf16[128,16,384]{2,1,0:T(8,128)(2,1)}), bf16[128,16,384]{2,1,0:T(8,128)(2,1)S(1)}, u32[]{:S(2)}, u32[]{:S(2)}) async-start(bf16[128,16,384]{2,1,0:T(8,128)(2,1)} %bitcast.10), calls=%async_computation.4 | async-start | bytes 3145728 | tf_op jit(solution)/shard_map/all_to_all | solution.py:274
  123.5 1.6 copy-done
  125.1 1.4 shard_map.126.active_ref
  126.5 1.3 copy-done.1
  127.8 0.1 constant_dynamic-slice_fusion
  127.9 1.3 shard_map.123
  129.2 19.4 %all-to-all-done.4.got_ref = bf16[128,16,384]{2,1,0:T(8,128)(2,1)S(1)} async-done(((bf16[128,16,384]{2,1,0:T(8,128)(2,1)}), bf16[128,16,384]{2,1,0:T(8,128)(2,1)S(1)}, u32[]{:S(2)}, u32[]{:S(2)}) %all-to-all-start.4) | async-done | bytes 1572896 | tf_op jit(solution)/shard_map/all_to_all | solution.py:274
  148.7 0.1 slice_reduce_fusion
  148.8 1.0 broadcast_in_dim.20
  149.8 3.8 %all-to-all-start.5 = ((bf16[128,16,128]{2,1,0:T(8,128)(2,1)}), bf16[128,16,128]{2,1,0:T(8,128)(2,1)S(1)}, u32[]{:S(2)}, u32[]{:S(2)}) async-start(bf16[128,16,128]{2,1,0:T(8,128)(2,1)} %broadcast_in_dim.20), calls=%async_computation.5 | async-start | bytes 1048576 | tf_op jit(solution)/shard_map/all_to_all | solution.py:274
  153.7 0.2 compare_select_fusion
  153.9 0.7 reshape.88.ids_ref
  154.6 11.3 %shard_map.127 = (f32[2048,256]{1,0:T(8,128)}, f32[2048,256]{1,0:T(8,128)}) custom-call(s32[1,2048]{1,0:T(1,128)} %reshape.88.ids_ref, bf16[128,16,384]{2,1,0:T(8,128)(2,1)} %copy-done.11, f32[2048,256]{1,0:T(8,128)} %table_ref.3, f32[2048,256]{1,0:T(8,128)} %accum_ref.1, bf16[2048,512]{1,0:T(8,128)(2,1)} %copy-done.1, bf16[256,512]{1,0:T(8,128)(2,1)} %w_in_ref.5, ...), custom_call_target="tpu_custom_call" | custom-call | flops 4294967296 | bytes 8388608 | tf_op jit(solution)/shard_map/pallas_call | solution.py:418
  165.9 1.9 %all-to-all-done.5 = bf16[128,16,128]{2,1,0:T(8,128)(2,1)S(1)} async-done(((bf16[128,16,128]{2,1,0:T(8,128)(2,1)}), bf16[128,16,128]{2,1,0:T(8,128)(2,1)S(1)}, u32[]{:S(2)}, u32[]{:S(2)}) %all-to-all-start.5) | async-done | bytes 524320 | tf_op jit(solution)/shard_map/all_to_all | solution.py:274
  167.8 1.1 fusion.6
  (65 shorter events, 0.5 us)
Async XLA Ops:
  0.6 15.1 %collective-permute-start = (bf16[192,256]{1,0:T(8,128)(2,1)}, bf16[192,256]{1,0:T(8,128)(2,1)S(1)}, u32[]{:S(2)}, u32[]{:S(2)}) collective-permute-start(bf16[192,256]{1,0:T(8,128)(2,1)} %q_ref.1), channel_id=1, source_target_pairs={{0,96},{32,0},{64,32},{96,64},{1,97},{33,1},{65,33},{97,65},{2,98}... | collective-permute-start | bytes 294920 | tf_op jit(solution)/shard_map/ppermute | solution.py:279
  4.0 11.8 %collective-permute-start.1 = (bf16[192,256]{1,0:T(8,128)(2,1)}, bf16[192,256]{1,0:T(8,128)(2,1)S(1)}, u32[]{:S(2)}, u32[]{:S(2)}) collective-permute-start(bf16[192,256]{1,0:T(8,128)(2,1)} %q_ref.1), channel_id=1, source_target_pairs={{0,64},{32,96},{64,0},{96,32},{1,65},{33,97},{65,1},{97,33},{2,66}... | collective-permute-start | bytes 294920 | tf_op jit(solution)/shard_map/ppermute | solution.py:279
  4.5 11.3 %collective-permute-start.2 = (bf16[192,256]{1,0:T(8,128)(2,1)}, bf16[192,256]{1,0:T(8,128)(2,1)S(1)}, u32[]{:S(2)}, u32[]{:S(2)}) collective-permute-start(bf16[192,256]{1,0:T(8,128)(2,1)} %q_ref.1), channel_id=1, source_target_pairs={{0,32},{32,64},{64,96},{96,0},{1,33},{33,65},{65,97},{97,1},{2,34}... | collective-permute-start | bytes 294920 | tf_op jit(solution)/shard_map/ppermute | solution.py:279
  6.8 14.8 %all-to-all-start = ((s32[32,1,128]{2,1,0:T(1,128)}), s32[32,1,128]{2,1,0:T(1,128)S(1)}, u32[]{:S(2)}, u32[]{:S(2)}) async-start(s32[32,1,128]{2,1,0:T(1,128)} %bitcast.40), calls=%async_computation | async-start | bytes 32768 | tf_op jit(solution)/shard_map/all_to_all | solution.py:274
  15.8 18.9 %copy-start.22 = (bf16[192]{0:T(256)(128)(2,1)S(1)}, bf16[192]{0:T(256)(128)(2,1)}, u32[]{:S(2)}) copy-start(bf16[192]{0:T(256)(128)(2,1)} %param.11) | copy-start | bytes 1156
  15.8 19.6 %copy-start.10 = (bf16[768,256]{1,0:T(8,128)(2,1)}, bf16[768,256]{1,0:T(8,128)(2,1)S(1)}, u32[]{:S(2)}) copy-start(bf16[768,256]{1,0:T(8,128)(2,1)S(1)} %constant_dynamic-update-slice_fusion.4.refs_0_) | copy-start | bytes 1179652
  15.9 32.4 %collective-permute-start.10 = (bf16[768,256]{1,0:T(8,128)(2,1)S(1)}, bf16[768,256]{1,0:T(8,128)(2,1)S(1)}, u32[]{:S(2)}, u32[]{:S(2)}) collective-permute-start(bf16[768,256]{1,0:T(8,128)(2,1)S(1)} %constant_dynamic-update-slice_fusion.4.refs_0_), channel_id=1, source_target_pairs={{0,3},{1,0},{2,1},{3,2},{4,7},{5,4},{6,5},{7,6},{8,11},{9,8},{10,9... | collective-permute-start | bytes 1179656 | tf_op jit(solution)/shard_map/ppermute | solution.py:279
  21.8 34.1 %collective-permute-start.11 = (bf16[768,256]{1,0:T(8,128)(2,1)S(1)}, bf16[768,256]{1,0:T(8,128)(2,1)S(1)}, u32[]{:S(2)}, u32[]{:S(2)}) collective-permute-start(bf16[768,256]{1,0:T(8,128)(2,1)S(1)} %constant_dynamic-update-slice_fusion.4.refs_0_), channel_id=1, source_target_pairs={{0,2},{1,3},{2,0},{3,1},{4,6},{5,7},{6,4},{7,5},{8,10},{9,11},{10,... | collective-permute-start | bytes 1179656 | tf_op jit(solution)/shard_map/ppermute | solution.py:279
  29.5 13.6 %all-to-all-start.1 = ((bf16[32,12,256]{2,1,0:T(8,128)(2,1)}), bf16[32,12,256]{2,1,0:T(8,128)(2,1)S(1)}, u32[]{:S(2)}, u32[]{:S(2)}) async-start(bf16[32,12,256]{2,1,0:T(8,128)(2,1)} %convert_element_type.28), calls=%async_computation.1 | async-start | bytes 524288 | tf_op jit(solution)/shard_map/all_to_all | solution.py:274
  33.9 22.2 %collective-permute-start.12 = (bf16[768,256]{1,0:T(8,128)(2,1)S(1)}, bf16[768,256]{1,0:T(8,128)(2,1)S(1)}, u32[]{:S(2)}, u32[]{:S(2)}) collective-permute-start(bf16[768,256]{1,0:T(8,128)(2,1)S(1)} %constant_dynamic-update-slice_fusion.4.refs_0_), channel_id=1, source_target_pairs={{0,1},{1,2},{2,3},{3,0},{4,5},{5,6},{6,7},{7,4},{8,9},{9,10},{10,1... | collective-permute-start | bytes 1179656 | tf_op jit(solution)/shard_map/ppermute | solution.py:279
  46.1 6.1 %collective-permute-start.3 = (bf16[208,256]{1,0:T(8,128)(2,1)}, bf16[208,256]{1,0:T(8,128)(2,1)S(1)}, u32[]{:S(2)}, u32[]{:S(2)}) collective-permute-start(bf16[208,256]{1,0:T(8,128)(2,1)} %get-tuple-element.22.refs_0_.pay_ref), channel_id=1, source_target_pairs={{0,8},{8,16},{16,24},{24,0},{1,9},{9,17},{17,25},{25,1},{2,10},{10... | collective-permute-start | bytes 319496 | tf_op jit(solution)/shard_map/ppermute | solution.py:279
  46.3 8.9 %collective-permute-start.4 = (bf16[208,256]{1,0:T(8,128)(2,1)}, bf16[208,256]{1,0:T(8,128)(2,1)S(1)}, u32[]{:S(2)}, u32[]{:S(2)}) collective-permute-start(bf16[208,256]{1,0:T(8,128)(2,1)} %get-tuple-element.22.refs_0_.pay_ref), channel_id=1, source_target_pairs={{0,16},{8,24},{16,0},{24,8},{1,17},{9,25},{17,1},{25,9},{2,18},{10... | collective-permute-start | bytes 319496 | tf_op jit(solution)/shard_map/ppermute | solution.py:279
  48.3 7.0 %collective-permute-start.5 = (bf16[208,256]{1,0:T(8,128)(2,1)}, bf16[208,256]{1,0:T(8,128)(2,1)S(1)}, u32[]{:S(2)}, u32[]{:S(2)}) collective-permute-start(bf16[208,256]{1,0:T(8,128)(2,1)} %get-tuple-element.22.refs_0_.pay_ref), channel_id=1, source_target_pairs={{0,24},{8,0},{16,8},{24,16},{1,25},{9,1},{17,9},{25,17},{2,26},{10... | collective-permute-start | bytes 319496 | tf_op jit(solution)/shard_map/ppermute | solution.py:279
  52.2 4.9 %copy-start.15 = (bf16[208,256]{1,0:T(8,128)(2,1)}, bf16[208,256]{1,0:T(8,128)(2,1)S(1)}, u32[]{:S(2)}) copy-start(bf16[208,256]{1,0:T(8,128)(2,1)S(1)} %collective-permute-done.3.refs_1_) | copy-start | bytes 319492
  52.2 4.1 %collective-permute-start.6 = (bf16[208,256]{1,0:T(8,128)(2,1)}, bf16[208,256]{1,0:T(8,128)(2,1)S(1)}, u32[]{:S(2)}, u32[]{:S(2)}) collective-permute-start(bf16[208,256]{1,0:T(8,128)(2,1)} %get-tuple-element.22.refs_0_.pay_ref), channel_id=1, source_target_pairs={{0,4},{4,0},{1,5},{5,1},{2,6},{6,2},{3,7},{7,3},{8,12},{12,8},{9,1... | collective-permute-start | bytes 319496 | tf_op jit(solution)/shard_map/ppermute | solution.py:279
  55.2 1.9 %copy-start.16 = (bf16[208,256]{1,0:T(8,128)(2,1)}, bf16[208,256]{1,0:T(8,128)(2,1)S(1)}, u32[]{:S(2)}) copy-start(bf16[208,256]{1,0:T(8,128)(2,1)S(1)} %collective-permute-done.4.refs_2_) | copy-start | bytes 319492
  55.2 1.3 collective-permute-start.7
  55.3 1.8 %copy-start.17 = (bf16[208,256]{1,0:T(8,128)(2,1)}, bf16[208,256]{1,0:T(8,128)(2,1)S(1)}, u32[]{:S(2)}) copy-start(bf16[208,256]{1,0:T(8,128)(2,1)S(1)} %collective-permute-done.5.refs_3_) | copy-start | bytes 319492
  55.3 1.5 collective-permute-start.8
  55.8 1.3 collective-permute-start.9
  56.2 1.1 copy-start.12
  56.4 1.0 copy-start.18
  56.5 0.8 copy-start.19
  56.8 0.6 copy-start.20
  57.4 0.6 copy-start.21
  66.3 12.9 %all-to-all-start.3 = ((f32[16,24,128]{2,1,0:T(8,128)}), f32[16,24,128]{2,1,0:T(8,128)S(1)}, u32[]{:S(2)}, u32[]{:S(2)}) async-start(f32[16,24,128]{2,1,0:T(8,128)} %shard_map.121.refs_8_), calls=%async_computation.3 | async-start | bytes 393216 | tf_op jit(solution)/shard_map/all_to_all | solution.py:274
  79.3 0.7 copy-start.13
  79.9 34.0 %all-to-all-start.2 = ((bf16[16,192,256]{2,1,0:T(8,128)(2,1)}), bf16[16,192,256]{2,1,0:T(8,128)(2,1)S(1)}, u32[]{:S(2)}, u32[]{:S(2)}) async-start(bf16[16,192,256]{2,1,0:T(8,128)(2,1)} %bitcast.34), calls=%async_computation.2 | async-start | bytes 3145728 | tf_op jit(solution)/shard_map/all_to_all | solution.py:274
  95.4 18.5 %copy-start.3 = (bf16[512,256]{1,0:T(8,128)(2,1)S(1)}, bf16[512,256]{1,0:T(8,128)(2,1)}, u32[]{:S(2)}) copy-start(bf16[512,256]{1,0:T(8,128)(2,1)} %w_out_ref.3) | copy-start | bytes 786436
  95.4 18.5 %copy-start.5 = (bf16[192,512]{1,0:T(8,128)(2,1)S(1)}, bf16[192,512]{1,0:T(8,128)(2,1)}, u32[]{:S(2)}) copy-start(bf16[192,512]{1,0:T(8,128)(2,1)} %get-tuple-element.29.refs_5_) | copy-start | bytes 589828
  95.4 18.5 %copy-start.7 = (bf16[192,256]{1,0:T(8,128)(2,1)S(1)}, bf16[192,256]{1,0:T(8,128)(2,1)}, u32[]{:S(2)}) copy-start(bf16[192,256]{1,0:T(8,128)(2,1)} %get-tuple-element.28.refs_4_) | copy-start | bytes 294916
  95.4 18.5 %copy-start.8 = (f32[32,256]{1,0:T(8,128)S(1)}, f32[32,256]{1,0:T(8,128)}, u32[]{:S(2)}) copy-start(f32[32,256]{1,0:T(8,128)} %get-tuple-element.31.refs_8_) | copy-start | bytes 98308
  95.4 18.5 %copy-start.9 = (s32[1,256]{1,0:T(1,128)S(1)}, s32[1,256]{1,0:T(1,128)}, u32[]{:S(2)}) copy-start(s32[1,256]{1,0:T(1,128)} %get-tuple-element.30.refs_7_) | copy-start | bytes 3076
  95.4 3.1 %collective-permute-start.13 = (f32[4,192,256]{2,1,0:T(8,128)}, f32[4,192,256]{2,1,0:T(8,128)S(1)}, u32[]{:S(2)}, u32[]{:S(2)}) collective-permute-start(f32[4,192,256]{2,1,0:T(8,128)} %get-tuple-element.27), channel_id=1, source_target_pairs={{0,4},{4,0},{1,5},{5,1},{2,6},{6,2},{3,7},{7,3},{8,12},{12,8},{9,1... | collective-permute-start | bytes 2359304 | tf_op jit(solution)/shard_map/ppermute | solution.py:279
  99.9 6.4 %collective-permute-start.14 = (f32[192,256]{1,0:T(8,128)S(1)}, f32[192,256]{1,0:T(8,128)S(1)}, u32[]{:S(2)}, u32[]{:S(2)}) collective-permute-start(f32[192,256]{1,0:T(8,128)S(1)} %get-tuple-element.37), channel_id=1, source_target_pairs={{0,24},{8,0},{16,8},{24,16},{1,25},{9,1},{17,9},{25,17},{2,26},{10... | collective-permute-start | bytes 589832 | tf_op jit(solution)/shard_map/ppermute | solution.py:279
  102.0 7.4 %collective-permute-start.15 = (f32[192,256]{1,0:T(8,128)S(1)}, f32[192,256]{1,0:T(8,128)S(1)}, u32[]{:S(2)}, u32[]{:S(2)}) collective-permute-start(f32[192,256]{1,0:T(8,128)S(1)} %get-tuple-element.36), channel_id=1, source_target_pairs={{0,16},{8,24},{16,0},{24,8},{1,17},{9,25},{17,1},{25,9},{2,18},{10... | collective-permute-start | bytes 589832 | tf_op jit(solution)/shard_map/ppermute | solution.py:279
  102.0 11.9 %collective-permute-start.16 = (f32[192,256]{1,0:T(8,128)S(1)}, f32[192,256]{1,0:T(8,128)S(1)}, u32[]{:S(2)}, u32[]{:S(2)}) collective-permute-start(f32[192,256]{1,0:T(8,128)S(1)} %get-tuple-element.35), channel_id=1, source_target_pairs={{0,8},{8,16},{16,24},{24,0},{1,9},{9,17},{17,25},{25,1},{2,10},{10... | collective-permute-start | bytes 589832 | tf_op jit(solution)/shard_map/ppermute | solution.py:279
  115.6 7.9 %copy-start.2 = (bf16[256,512]{1,0:T(8,128)(2,1)S(1)}, bf16[256,512]{1,0:T(8,128)(2,1)}, u32[]{:S(2)}) copy-start(bf16[256,512]{1,0:T(8,128)(2,1)} %w_in_ref.5) | copy-start | bytes 786436
  115.6 33.1 %all-to-all-start.4 = ((bf16[128,16,384]{2,1,0:T(8,128)(2,1)}), bf16[128,16,384]{2,1,0:T(8,128)(2,1)S(1)}, u32[]{:S(2)}, u32[]{:S(2)}) async-start(bf16[128,16,384]{2,1,0:T(8,128)(2,1)} %bitcast.10), calls=%async_computation.4 | async-start | bytes 3145728 | tf_op jit(solution)/shard_map/all_to_all | solution.py:274
  123.5 1.6 copy-start
  125.1 2.7 %copy-start.14 = (f32[16,24,128]{2,1,0:T(8,128)S(1)}, f32[16,24,128]{2,1,0:T(8,128)}, u32[]{:S(2)}) copy-start(f32[16,24,128]{2,1,0:T(8,128)} %copy-done.13) | copy-start | bytes 589828
  125.1 2.9 %copy-start.4 = (bf16[192,256]{1,0:T(8,128)(2,1)S(1)}, bf16[192,256]{1,0:T(8,128)(2,1)}, u32[]{:S(2)}) copy-start(bf16[192,256]{1,0:T(8,128)(2,1)} %q_ref.1) | copy-start | bytes 294916
  125.1 2.9 %copy-start.6 = (bf16[208,256]{1,0:T(8,128)(2,1)S(1)}, bf16[208,256]{1,0:T(8,128)(2,1)}, u32[]{:S(2)}) copy-start(bf16[208,256]{1,0:T(8,128)(2,1)} %get-tuple-element.22.refs_0_.pay_ref) | copy-start | bytes 319492
  126.5 1.3 copy-start.1
  148.7 6.0 %copy-start.11 = (bf16[128,16,384]{2,1,0:T(8,128)(2,1)}, bf16[128,16,384]{2,1,0:T(8,128)(2,1)S(1)}, u32[]{:S(2)}) copy-start(bf16[128,16,384]{2,1,0:T(8,128)(2,1)S(1)} %all-to-all-done.4.got_ref) | copy-start | bytes 4718596
  149.8 17.9 %all-to-all-start.5 = ((bf16[128,16,128]{2,1,0:T(8,128)(2,1)}), bf16[128,16,128]{2,1,0:T(8,128)(2,1)S(1)}, u32[]{:S(2)}, u32[]{:S(2)}) async-start(bf16[128,16,128]{2,1,0:T(8,128)(2,1)} %broadcast_in_dim.20), calls=%async_computation.5 | async-start | bytes 1048576 | tf_op jit(solution)/shard_map/all_to_all | solution.py:274

commit v4 on v3

--- a/solution.py
+++ b/solution.py
@@ -1,3 +1,5 @@
+import functools
+
 import jax
 import jax.numpy as jnp
 from jax import lax
@@ -15,8 +17,12 @@
 NA = 16
 NB = 8
 QS = NA * PAIRS
+LINES = QS // 128
+SENT = LINES + 8
+PACK = 40
 VS = NB * PAIRS
-LIMIT = 58 << 20
+LIMIT = 20 << 20
+LARGE = 58 << 20
 SMALL = 24 << 20
 score_scale = 0.0625
 learn_rate = 0.1
@@ -61,7 +67,7 @@
     return jnp.sum(jnp.where(eye, lanes, jnp.zeros((), lanes.dtype)), axis=1, keepdims=True)
 
 
-def slots_kernel(owner_ref, row_ref, req_ref, place_ref, pick_ref, ids_ref, pair):
+def slots_kernel(owner_ref, row_ref, req_ref, place_ref, pick_ref, pair):
     pair[...] = jnp.full((8, 256), -1, i32)
     pair[0:1, 0:PAIRS] = owner_ref[...]
     pair[1:2, 0:PAIRS] = row_ref[...]
@@ -78,13 +84,25 @@
     lo = mm(onehot, low, NT)
     hi = mm(onehot, high, NT) - 1.0
     req_ref[...] = jnp.where(hi < 0.0, -1, (hi * 256.0 + lo).astype(i32))
-    ids_ref[:, 0:128] = hi
-    ids_ref[:, 128:256] = lo
     place = jnp.where(owner < 0, -1, owner * SLOT + slot)
     place_ref[...] = place
     flat = jnp.where(owner < 0, -1, owner * CAP + slot).astype(f32)
     col = column(flat, PAIRS).astype(i32)
     pick_ref[...] = (col == iota((PAIRS, OWNERS * CAP), 1)).astype(f32).astype(bf16)
+
+
+COST = 8 << 30
+
+
+def pass_kernel(in_ref, unread_ref, out_ref):
+    out_ref[...] = in_ref[...]
+
+
+def slab_kernel(x_ref, *refs):
+    blocks, out_ref = refs[:4], refs[-1]
+    for k in range(4):
+        at = (x_ref[0] + k) % 4 * PAIRS
+        out_ref[pl.ds(pl.multiple_of(at, 16), PAIRS), :] = blocks[k][...]
 
 
 def tower_kernel(got_ref, pick_ref, w_in_ref, w_out_ref, freq_ref, *refs):
@@ -103,7 +121,7 @@
 
 
 def load_vecs(vec_refs, vec, freq):
-    for b in range(NB):
+    for b in range(len(vec_refs)):
         at = slice(b * PAIRS, (b + 1) * PAIRS)
         line = vec_refs[b][PAIRS : PAIRS + 16, :].astype(f32)[0:1, :]
         freq[at, :] = jnp.broadcast_to(column(line, PAIRS), (PAIRS, 128))
@@ -118,7 +136,8 @@
 
 
 def score_kernel(*refs):
-    vec_refs, (q_ref, lse_ref, vec, freq, *scores) = refs[:NB], refs[NB:]
+    vec_refs, (q_ref, ids_ref, lse_ref, vec, freq, *scores) = refs[:NB], refs[NB:]
+    lse_ref[:, LINES:SENT, :] = jnp.broadcast_to(ids_ref[...][None], (NA, 8, 128))
     load_vecs(vec_refs, vec, freq)
     tops = []
     for j in range(QS // PB + 1):
@@ -157,12 +176,9 @@
     return jnp.concatenate([rows_ref[(*index, pl.ds(at + i, 1), slice(None))] for i in range(n)], axis=1)
 
 
-def query_kernel(pos_ref, *refs):
-    vec_refs, (part_ref, q_ref, o_ref, vec, freq, turned, weight) = refs[:NB], refs[NB:]
-
+def query_kernel(pos_ref, vec, freq, part_ref, q_ref, o_ref, turned, weight):
     @pl.when(pl.program_id(0) == 0)
     def _():
-        load_vecs(vec_refs, vec, freq)
         for k in range(0, VS, 256):
             turned[:, k : k + 256] = vec[k : k + 256, :].astype(f32).T.astype(bf16)
 
@@ -177,7 +193,7 @@
     o_ref[...] = mm(turned[...], weight[...]).T.astype(bf16)
 
 
-def vec_kernel(pos_ref, vec, freq, parts_ref, q_ref, unread_ref, same_ref, other_ref, lse, coef):
+def vec_kernel(first, n, pos_ref, vec, freq, parts_ref, q_ref, g_ref, lse, coef):
     @pl.when(pl.program_id(0) == 0)
     def _():
         top = parts_ref[0]
@@ -187,23 +203,23 @@
         for a in range(1, NA):
             total = total + jnp.exp(parts_ref[a] - top)
         lse[...] = top + jnp.log(total)
-        same_ref[...] = jnp.zeros_like(same_ref)
-        other_ref[...] = jnp.zeros_like(other_ref)
+        g_ref[...] = jnp.zeros_like(g_ref)
 
     q = q_ref[...]
     scaled = q * jnp.asarray(score_scale, bf16)
     norm = query_lanes(lse)
-    for b in range(0, VS, VB):
-        at = slice(b, b + VB)
+    for b in range(0, n, 2):
+        m = min(2, n - b) * PAIRS
+        at = slice((first + b) * PAIRS, (first + b) * PAIRS + m)
         p = jnp.exp(mm(vec[at, :], scaled, NT) - lanes(freq[at, :]) - norm)
-        if b == 0:
-            p = jnp.concatenate([jnp.where(is_pair(pos_ref), p[:PAIRS] - 1.0, p[:PAIRS]), p[PAIRS:]], axis=0)
-        coef[at, :] = p.astype(bf16)
-    for b in range(0, NB, 2):
-        g = mm(coef[b * PAIRS : (b + 2) * PAIRS, :], q)
-        ref = (same_ref, other_ref)[b // 4]
-        ref[b % 4] += g[:PAIRS]
-        ref[b % 4 + 1] += g[PAIRS:]
+        if first == 0:
+            p = jnp.where(is_pair(pos_ref), p - 1.0, p)
+        coef[b * PAIRS : b * PAIRS + m, :] = p.astype(bf16)
+    for b in range(0, n, 2):
+        m = min(2, n - b)
+        g = mm(coef[b * PAIRS : (b + m) * PAIRS, :], q)
+        for k in range(m):
+            g_ref[b + k] += g[k * PAIRS : (k + 1) * PAIRS]
 
 
 def combine_kernel(got_ref, parts_ref, q_ref, pay_ref, out_ref):
@@ -222,7 +238,7 @@
 
 
 def back_kernel(*refs):
-    parts, (emb_ref, hid_ref, w_out_ref, place_ref, ids_ref), out_ref = refs[:4], refs[4:9], refs[-1]
+    parts, (emb_ref, hid_ref, w_out_ref, place_ref), out_ref = refs[:4], refs[4:8], refs[-1]
     total = parts[0][...]
     for part in parts[1:]:
         total = total + part[...]
@@ -230,20 +246,26 @@
     hid = hid_ref[...]
     hg = jnp.where(hid.astype(f32) > 0.0, mm(grad, w_out_ref[...], NT), 0.0).astype(bf16)
     scatter = (iota((OWNERS * SLOT, PAIRS), 0) == place_ref[:, 0:PAIRS]).astype(f32).astype(bf16)
-    slots = mm(scatter, grad).reshape(OWNERS, SLOT, E)
-    ids = ids_ref[...].reshape(OWNERS, 1, E)
-    slots = jnp.where(iota((OWNERS, SLOT, E), 1) == CAP, ids, slots).astype(bf16).reshape(16, 2, SLOT, E)
-    w_out_part = mm(hid, grad, TN)
-    w_in_part = mm(emb_ref[...], hg, TN)
+    slots = mm(scatter, grad).reshape(16, 2, SLOT, E)
     pieces = []
-    for part in (w_out_part, w_in_part):
+    for part in (mm(hid, grad, TN), mm(emb_ref[...], hg, TN)):
         n = part.shape[0] // 8
         tiles = [part[:, k : k + 128].reshape(n, 1, 8, 128) for k in range(0, part.shape[1], 128)]
-        pieces.append(jnp.concatenate(tiles, axis=1).reshape(16, 4, SLOT, 128).astype(bf16))
-    for z in range(4):
-        out_ref[:, :, z, :, 0:E] = slots
-        for c in range(2):
-            out_ref[:, c, z, :, E : E + 128] = pieces[c][:, z]
+        pieces.append(jnp.concatenate(tiles, axis=1).reshape(16, 4, 2, 8, 128))
+    top = iota((16, 8, 128), 1) < 4
+    for c in range(2):
+        left, right = slots[:, c, :, 0:128], slots[:, c, :, 128:E]
+        for z in range(4):
+            w0, w1 = pieces[c][:, z, 0], pieces[c][:, z, 1]
+            rolled = jnp.concatenate([w1[:, 4:8], w1[:, 0:4]], axis=1)
+            rows = [
+                left[:, 0:8],
+                jnp.where(top, left[:, 8:16], w0),
+                right[:, 0:8],
+                jnp.where(top, right[:, 8:16], w1),
+                jnp.where(top, w0, rolled),
+            ]
+            out_ref[:, c, z] = jnp.concatenate(rows, axis=1).astype(bf16)
 
 
 TB = 512
@@ -257,7 +279,7 @@
 def update_kernel(ids_ref, got_ref, table_ref, accum_ref, active_ref, w_in_ref, w_out_ref, table_out, accum_out):
     base = pl.program_id(0) * TB
     onehot = (ids_ref[...] == iota((TB, 128 * SLOT), 0) + base).astype(f32).astype(bf16)
-    vals = got_ref[:, :, 0:E].reshape(128 * SLOT, E)
+    vals = jnp.concatenate([got_ref[:, 0:SLOT, :], got_ref[:, SLOT : 2 * SLOT, :]], axis=2).reshape(128 * SLOT, E)
     vg = mm(onehot, vals)
     high = vg.astype(bf16)
     low = (vg - high.astype(f32)).astype(bf16)
@@ -298,68 +320,71 @@
 def local(queries, item_owner, item_row, log_freq, table, accum, w_in, w_out):
     here_x = lax.axis_index("x").astype(i32)
     here_z = lax.axis_index("z").astype(i32)
-    req, place, pick, ids = call(
+    req, place, pick = call(
         slots_kernel,
         (
             sds((OWNERS, 128), i32),
             sds((1, 256), i32),
             sds((PAIRS, OWNERS * CAP), bf16),
-            sds((OWNERS, E), f32),
         ),
         in_specs=whole(2),
-        out_specs=tuple(whole(4)),
+        out_specs=tuple(whole(3)),
         scratch_shapes=[pltpu.VMEM((8, 256), i32)],
     )(item_owner.reshape(1, PAIRS), item_row.reshape(1, PAIRS))
     asked = a2a(req.reshape(OWNERS, 1, 128), SHARD)
-    slab = jnp.zeros((QB, E), bf16)
-    for k in range(4):
-        block = shift(queries, "x", 4 - k) if k else queries
-        slab = lax.dynamic_update_slice(slab, block, ((here_x + k) % 4 * PAIRS, 0))
-    slabs = [slab] + [shift(slab, "z", 4 - k) for k in range(1, 4)]
-    all_q = jnp.zeros((QS, E), bf16)
-    for k in range(4):
-        all_q = lax.dynamic_update_slice(all_q, slabs[k], ((here_z + k) % 4 * QB, 0))
+    early = call(
+        pass_kernel,
+        sds((PAIRS, E), bf16),
+        cost=(COST, 1 << 20, 0),
+        limit=SMALL,
+        in_specs=whole(1) + unread(1),
+        out_specs=whole(1)[0],
+    )(queries, req)
+    blocks = [queries] + [shift(early, "x", 4 - k) for k in range(1, 4)]
+    ids = asked[:, 0, :SLOT].astype(f32).reshape(OWNERS * SLOT // 128, 128)
+    ids = jnp.pad(ids, ((0, 8 - OWNERS * SLOT // 128), (0, 0)))
     wanted = jnp.maximum(asked[:, 0, :CAP].reshape(OWNERS * CAP), 0)
     picked = table.at[wanted].get(mode="promise_in_bounds").astype(bf16)
+    slab = call(
+        slab_kernel,
+        sds((QB, E), bf16),
+        cost=(COST, 1 << 20, 0),
+        limit=SMALL,
+        in_specs=[pl.BlockSpec(memory_space=pltpu.MemorySpace.SMEM)] + whole(4) + unread(1),
+        out_specs=whole(1)[0],
+    )(here_x.reshape(1), *blocks, picked)
+    above, below = shift(slab, "z", 3), shift(slab, "z", 1)
+    half = QB // 2
+    far = [shift(above[:half], "z", 3), shift(below[half:], "z", 1)]
+    all_q = jnp.zeros((QS, E), bf16)
+    for k, block in ((0, slab), (1, above), (3, below), (2, jnp.concatenate(far, axis=0))):
+        all_q = lax.dynamic_update_slice(all_q, block, ((here_z + k) % 4 * QB, 0))
     got = a2a(picked.reshape(OWNERS, CAP, E), SHARD).reshape(OWNERS * CAP, E)
     freq_row = jnp.pad(log_freq.reshape(1, PAIRS), ((0, 15), (0, 256 - PAIRS)))
     emb, hid, pay = call(
         tower_kernel,
         (sds((PAIRS, E), bf16), sds((PAIRS, H), bf16), sds((PAIRS + 16, E), bf16)),
-        in_specs=whole(5) + unread(1),
+        cost=(24 << 30, 1 << 20, 0),
+        in_specs=whole(5),
         out_specs=tuple(whole(3)),
-    )(got, pick, w_in, w_out, freq_row, slab)
+    )(got, pick, w_in, w_out, freq_row)
     vecs = [pay] + [shift(pay, "y", k) for k in range(1, 4)]
     vecs = vecs + [shift(v, "c", 1) for v in vecs]
 
-    part_lse = call(
+    part_lse, vec_all, freq_all = call(
         score_kernel,
-        sds((NA, QS // 128, 128), f32),
+        (sds((NA, SENT, 128), f32), sds((VS, E), bf16), sds((VS, 128), f32)),
         cost=(2 * VS * QS * E, VS * QS * 2, VS * QS),
         limit=LIMIT,
-        in_specs=whole(NB + 1),
-        out_specs=whole(1)[0],
-        scratch_shapes=[pltpu.VMEM((VS, E), bf16), pltpu.VMEM((VS, 128), f32)] + [pltpu.VMEM((VS, PB), f32)] * 2,
-    )(*vecs, all_q)
+        in_specs=whole(NB + 2),
+        out_specs=tuple(whole(3)),
+        scratch_shapes=[pltpu.VMEM((VS, PB), f32)] * 2,
+    )(*vecs, all_q, ids)
     all_lse = a2a(part_lse, A)
     here = here_z * 4 + here_x
-    o, vec_all, freq_all = call(
+    o = call(
         query_kernel,
-        (sds((QS, E), bf16), sds((VS, E), bf16), sds((VS, 128), f32)),
-        cost=(4 * VS * QS * E, VS * QS, VS * QS),
-        limit=LIMIT,
-        grid_spec=pltpu.PrefetchScalarGridSpec(
-            num_scalar_prefetch=1,
-            grid=(QS // QB,),
-            in_specs=[const(PAIRS + 16, E)] * NB
-            + [const(NA, QS // 128, 128), pl.BlockSpec((QB, E), lambda i, pos: (i, 0))],
-            out_specs=(pl.BlockSpec((QB, E), lambda i, pos: (i, 0)), const(VS, E), const(VS, 128)),
-            scratch_shapes=[pltpu.VMEM((E, VS), bf16), pltpu.VMEM((VS, QB), bf16)],
-        ),
-    )(here.reshape(1), *vecs, part_lse, all_q)
-    same, other = call(
-        vec_kernel,
-        (sds((4, PAIRS, E), f32), sds((4, PAIRS, E), f32)),
+        sds((QS, E), bf16),
         cost=(4 * VS * QS * E, VS * QS, VS * QS),
         limit=LIMIT,
         grid_spec=pltpu.PrefetchScalarGridSpec(
@@ -368,29 +393,60 @@
             in_specs=[
                 const(VS, E),
                 const(VS, 128),
-                const(NA, QS // 128, 128),
+                const(NA, SENT, 128),
                 pl.BlockSpec((QB, E), lambda i, pos: (i, 0)),
-                unread(1)[0],
             ],
-            out_specs=(const(4, PAIRS, E), const(4, PAIRS, E)),
-            scratch_shapes=[pltpu.VMEM((QS // 128, 128), f32), pltpu.VMEM((VS, QB), bf16)],
+            out_specs=pl.BlockSpec((QB, E), lambda i, pos: (i, 0)),
+            scratch_shapes=[
+                pltpu.VMEM((E, VS), bf16),
+                pltpu.VMEM((VS, QB), bf16),
+            ],
         ),
-    )(here.reshape(1), vec_all, freq_all, all_lse, all_q, o)
+    )(here.reshape(1), vec_all, freq_all, part_lse, all_q)
+
+    def vec_grads(first, n, wait):
+        first_lse, _ = lax.optimization_barrier((all_lse, wait))
+        return call(
+            functools.partial(vec_kernel, first, n),
+            sds((n, PAIRS, E), f32),
+            cost=(4 * n * PAIRS * QS * E, n * PAIRS * QS, n * PAIRS * QS),
+            limit=LIMIT,
+            grid_spec=pltpu.PrefetchScalarGridSpec(
+                num_scalar_prefetch=1,
+                grid=(QS // QB,),
+                in_specs=[
+                    const(VS, E),
+                    const(VS, 128),
+                    const(NA, SENT, 128),
+                    pl.BlockSpec((QB, E), lambda i, pos: (i, 0)),
+                ],
+                out_specs=const(n, PAIRS, E),
+                scratch_shapes=[
+                    pltpu.VMEM((SENT, 128), f32),
+                    pltpu.VMEM((n * PAIRS, QB), bf16),
+                ],
+            ),
+        )(here.reshape(1), vec_all, freq_all, first_lse, all_q)
+
     o_got = a2a(o.reshape(NA, PAIRS, E), A)
 
+    other = vec_grads(4, 4, o)
+    same = vec_grads(1, 3, other)
     from_core = shift(other, "c", 1)
-    sums = [same[k] + from_core[k] for k in range(4)]
-    parts = [sums[0]] + [shift(sums[k], "y", 4 - k) for k in range(1, 4)]
+    sums = [same[k - 1] + from_core[k] for k in range(1, 4)]
+    parts = [shift(sums[k - 1], "y", 4 - k) for k in range(1, 4)]
+    mine = vec_grads(0, 1, sums[2])
+    parts = [mine.reshape(PAIRS, E) + from_core[0]] + parts
     out = call(
         back_kernel,
-        sds((16, 2, 4, SLOT, E + 128), bf16),
-        limit=SMALL,
-        in_specs=whole(9) + unread(1),
+        sds((16, 2, 4, PACK, 128), bf16),
+        limit=LARGE,
+        in_specs=whole(8) + unread(1),
         out_specs=whole(1)[0],
-    )(*parts, emb, hid, w_out, place, ids, o_got)
-    back = a2a(out.reshape(128, SLOT, E + 128), ALL)
-
-    own = lax.dynamic_slice(all_lse.reshape(NA, QS), (0, here * PAIRS), (NA, PAIRS))
+    )(*parts, emb, hid, w_out, place, o_got)
+    back = a2a(out.reshape(128, PACK, 128), ALL)
+
+    own = lax.dynamic_slice(all_lse[:, :LINES].reshape(NA, QS), (0, here * PAIRS), (NA, PAIRS))
     query_grad = call(
         combine_kernel,
         sds((PAIRS, E), f32),
@@ -408,22 +464,22 @@
         in_specs=[pl.BlockSpec((TB, E), lambda i: (i, 0)), const(E, H)],
         out_specs=pl.BlockSpec((TB, H), lambda i: (i, 0)),
     )(table, w_in)
-    w_sum = jnp.sum(back[:, :, E:].astype(f32), axis=0)
+    w_sum = jnp.sum(back.astype(f32), axis=0)
+    w_sum = jnp.concatenate([w_sum[32:36], w_sum[12:16], w_sum[36:40], w_sum[28:32]], axis=0)
     w_sum = after(jnp.broadcast_to(w_sum.astype(bf16)[None], (128, SLOT, 128)), query_grad, active)
     w_all = a2a(w_sum, ALL).reshape(16, 2, 4, SLOT, 128).astype(f32)
-    hi = back[:, CAP, 0:CAP].astype(i32)
-    lo = back[:, CAP, 128 : 128 + CAP].astype(i32)
-    row_ids = jnp.where(hi < 0, -1, hi * 256 + lo)
-    row_ids = jnp.pad(row_ids, ((0, 0), (0, SLOT - CAP)), constant_values=-1).reshape(1, 128 * SLOT)
+    row_ids = all_lse.reshape(4, 4, SENT, 128)[:, :, LINES : LINES + 4]
+    row_ids = lax.dynamic_index_in_dim(row_ids, here_x, axis=1, keepdims=False)
+    row_ids = row_ids.reshape(4, OWNERS, SLOT).transpose(1, 0, 2).reshape(1, 128 * SLOT).astype(i32)
     table_new, accum_new = call(
         update_kernel,
         (sds((ROWS, E), f32), sds((ROWS, E), f32)),
         cost=(4 * ROWS * 2048 * E, 4 * ROWS * E * 4, 0),
-        limit=LIMIT,
+        limit=LARGE,
         grid=(ROWS // TB,),
         in_specs=[
             const(1, 128 * SLOT),
-            const(128, SLOT, E + 128),
+            const(128, PACK, 128),
             pl.BlockSpec((TB, E), lambda i: (i, 0)),
             pl.BlockSpec((TB, E), lambda i: (i, 0)),
             pl.BlockSpec((TB, H), lambda i: (i, 0)),

time: 170 us -> 163 us (0.959)
  waiting for transfers between devices: 48.5 us -> 33.7 us
  starting transfers between devices: 57.3 us -> 65 us
  Pallas kernels: 46.1 us -> 42.8 us
  local copies, waits for them, and re-layouts: 14.2 us -> 17 us
    ppermute x17 -> x18, waiting for transfers between devices: 17.8 us -> 8.15 us  [shift(): return lax.ppermute(x, axis, [(i, (i + k) % n) for i in range(n)])]
    all_to_all x6, starting transfers between devices: 34.2 us -> 39.7 us  [a2a(): return lax.all_to_all(x, axes, split_axis=0, concat_axis=0, tiled=True)]
    unnamed x47 -> x43, local copies, waits for them, and re-layouts: 4.6 us -> 9.92 us
    all_to_all x6, waiting for transfers between devices: 30.8 us -> 25.5 us  [a2a(): return lax.all_to_all(x, axes, split_axis=0, concat_axis=0, tiled=True)]
    pallas_call x4 -> x8, Pallas kernels: 28.1 us -> 25 us  [the longest x3 8.74 us: vec_grads(): call(functools.partial(vec_kernel, first, n), sds((n, PAIRS, E), f32), co...]
    ppermute x17 -> x18, starting transfers between devices: 23.1 us -> 25.3 us  [shift(): return lax.ppermute(x, axis, [(i, (i + k) % n) for i in range(n)])]
  transfers between devices with their start and end apart: 23 -> 24, of which waited for: 13 -> 9; matrix products, arithmetic and copies ran while one was open for 5% -> 4% of each run, Pallas kernels for 21% -> 20%
where the time goes in v4:
time: 163 us; the launch traced here: 162 us
  starting transfers between devices  65 us (40%)
  Pallas kernels  42.8 us (26%)
  waiting for transfers between devices  33.7 us (21%)
  local copies, waits for them, and re-layouts  17 us (10%)
  other arithmetic  2.5 us (2%)
    all_to_all x6, starting transfers between devices, a2a(): return lax.all_to_all(x, axes, split_axis=0, concat_axis=0, tiled=True)  39.7 us
    all_to_all x6, waiting for transfers between devices, a2a(): return lax.all_to_all(x, axes, split_axis=0, concat_axis=0, tiled=True)  25.5 us
    ppermute x18, starting transfers between devices, shift(): return lax.ppermute(x, axis, [(i, (i + k) % n) for i in range(n)])  25.3 us
    pallas_call x1, Pallas kernels, local(): call(update_kernel, (sds((ROWS, E), f32), sds((ROWS, E), f32)), cost=(4 *...  11.2 us
    unnamed x43, local copies, waits for them, and re-layouts  9.92 us
    pallas_call x3, Pallas kernels, vec_grads(): call(functools.partial(vec_kernel, first, n), sds((n, PAIRS, E), f32), co...  8.74 us
    ppermute x18, waiting for transfers between devices, shift(): return lax.ppermute(x, axis, [(i, (i + k) % n) for i in range(n)])  8.15 us
    pallas_call x1, Pallas kernels, local(): call(query_kernel, sds((QS, E), bf16), cost=(4 * VS * QS * E, VS * QS, VS...  7.5 us
  transfers between devices with their start and end apart: 24, of which 9 were waited for; matrix products, arithmetic and copies ran while one was open for 4% of the time, Pallas kernels for 20%

profile of v4, /device:TPU:1, one launch (start us, length us, event | category | flops | bytes accessed | tf_op | source)
XLA Modules:
  0.0 162.0 jit_solution(8985624433240641676)
XLA Ops:
  0.6 1.7 %shard_map.119 = (s32[32,128]{1,0:T(8,128)}, s32[1,256]{1,0:T(1,128)}, bf16[192,384]{1,0:T(8,128)(2,1)}) custom-call(s32[1,192]{1,0:T(1,128)} %bitcast.49, s32[1,192]{1,0:T(1,128)} %bitcast.50), custom_call_target="tpu_custom_call" | custom-call | tf_op jit(solution)/shard_map/pallas_call | solution.py:323
  2.3 8.6 %all-to-all-start = ((s32[32,1,128]{2,1,0:T(1,128)}), s32[32,1,128]{2,1,0:T(1,128)S(1)}, u32[]{:S(2)}, u32[]{:S(2)}) async-start(s32[32,1,128]{2,1,0:T(1,128)} %bitcast.41), calls=%async_computation | async-start | bytes 32768 | tf_op jit(solution)/shard_map/all_to_all | solution.py:296
  10.9 0.9 copy-done.14
  11.8 0.7 copy-done.17
  12.5 2.7 %collective-permute-start.7 = (bf16[192,256]{1,0:T(8,128)(2,1)S(1)}, bf16[192,256]{1,0:T(8,128)(2,1)S(1)}, u32[]{:S(2)}, u32[]{:S(2)}) collective-permute-start(bf16[192,256]{1,0:T(8,128)(2,1)S(1)} %shard_map.121), channel_id=1, source_target_pairs={{0,96},{32,0},{64,32},{96,64},{1,97},{33,1},{65,33},{97,65},{2,98}... | collective-permute-start | bytes 294920 | tf_op jit(solution)/shard_map/ppermute | solution.py:301
  15.2 0.5 collective-permute-start.8
  15.8 0.6 collective-permute-start.9
  16.4 0.6 pad.12.freq_ref
  17.0 0.8 all-to-all-done
  17.8 0.1 reshape.140
  17.9 1.7 %gather_fusion = bf16[384,256]{1,0:T(8,128)(2,1)S(1)} fusion(f32[2048,256]{1,0:T(8,128)S(1)} %copy-done.2, s32[1024]{0:T(1024)S(1)} %pad_clamp_fusion), kind=kCustom, calls=%fused_computation | custom fusion | bytes 394752 | tf_op jit(solution)/shard_map/gather | solution.py:347
  19.6 0.7 convert_element_type.42
  20.4 6.6 %all-to-all-start.1 = ((bf16[32,12,256]{2,1,0:T(8,128)(2,1)}), bf16[32,12,256]{2,1,0:T(8,128)(2,1)S(1)}, u32[]{:S(2)}, u32[]{:S(2)}) async-start(bf16[32,12,256]{2,1,0:T(8,128)(2,1)} %convert_element_type.42), calls=%async_computation.1 | async-start | bytes 524288 | tf_op jit(solution)/shard_map/all_to_all | solution.py:296
  27.2 3.8 %collective-permute-start.10 = (bf16[768,256]{1,0:T(8,128)(2,1)S(1)}, bf16[768,256]{1,0:T(8,128)(2,1)S(1)}, u32[]{:S(2)}, u32[]{:S(2)}) collective-permute-start(bf16[768,256]{1,0:T(8,128)(2,1)S(1)} %shard_map.122), channel_id=1, source_target_pairs={{0,3},{1,0},{2,1},{3,2},{4,7},{5,4},{6,5},{7,6},{8,11},{9,8},{10,9... | collective-permute-start | bytes 1179656 | tf_op jit(solution)/shard_map/ppermute | solution.py:301
  31.1 0.1 broadcast_in_dim.4
  31.2 4.8 %all-to-all-done.1 = bf16[32,12,256]{2,1,0:T(8,128)(2,1)S(1)} async-done(((bf16[32,12,256]{2,1,0:T(8,128)(2,1)}), bf16[32,12,256]{2,1,0:T(8,128)(2,1)S(1)}, u32[]{:S(2)}, u32[]{:S(2)}) %all-to-all-start.1) | async-done | bytes 196640 | tf_op jit(solution)/shard_map/all_to_all | solution.py:296
  36.0 0.7 reshape.128.got_ref
  36.7 2.3 %shard_map.120 = (bf16[192,256]{1,0:T(8,128)(2,1)}, bf16[192,512]{1,0:T(8,128)(2,1)}, bf16[208,256]{1,0:T(8,128)(2,1)}) custom-call(bf16[384,256]{1,0:T(8,128)(2,1)} %reshape.128.got_ref, bf16[192,384]{1,0:T(8,128)(2,1)} %get-tuple-element.21.pick_ref, bf16[256,512]{1,0:T(8,128)(2,1)} %w_in_ref.5, bf16[512,256]{1,0:T(8,128)(2,1)} %w_out_ref.3, ...), custom_call_target="tpu_custom_call" | custom-call | flops 25769803776 | bytes 1048576 | tf_op jit(solution)/shard_map/pallas_call | solution.py:364
  39.1 0.2 collective-permute-start
  39.3 1.9 %collective-permute-start.1 = (bf16[208,256]{1,0:T(8,128)(2,1)}, bf16[208,256]{1,0:T(8,128)(2,1)S(1)}, u32[]{:S(2)}, u32[]{:S(2)}) collective-permute-start(bf16[208,256]{1,0:T(8,128)(2,1)} %get-tuple-element.22.refs_0_.pay_ref), channel_id=1, source_target_pairs={{0,16},{8,24},{16,0},{24,8},{1,17},{9,25},{17,1},{25,9},{2,18},{10... | collective-permute-start | bytes 319496 | tf_op jit(solution)/shard_map/ppermute | solution.py:301
  41.2 0.5 collective-permute-start.2
  41.7 0.7 collective-permute-done.11
  42.5 1.0 collective-permute-start.13
  43.5 2.2 %collective-permute-start.12 = (bf16[384,256]{1,0:T(8,128)(2,1)S(1)}, bf16[384,256]{1,0:T(8,128)(2,1)S(1)}, u32[]{:S(2)}, u32[]{:S(2)}) collective-permute-start(bf16[384,256]{1,0:T(8,128)(2,1)S(1)} %slice.83), channel_id=1, source_target_pairs={{0,3},{1,0},{2,1},{3,2},{4,7},{5,4},{6,5},{7,6},{8,11},{9,8},{10,9... | collective-permute-start | bytes 589832 | tf_op jit(solution)/shard_map/ppermute | solution.py:301
  45.8 2.4 %collective-permute-start.3 = (bf16[208,256]{1,0:T(8,128)(2,1)S(1)}, bf16[208,256]{1,0:T(8,128)(2,1)S(1)}, u32[]{:S(2)}, u32[]{:S(2)}) collective-permute-start(bf16[208,256]{1,0:T(8,128)(2,1)S(1)} %copy-done.13), channel_id=1, source_target_pairs={{0,4},{4,0},{1,5},{5,1},{2,6},{6,2},{3,7},{7,3},{8,12},{12,8},{9,1... | collective-permute-start | bytes 319496 | tf_op jit(solution)/shard_map/ppermute | solution.py:301
  48.2 0.1 collective-permute-start.4
  48.2 0.5 collective-permute-start.5
  48.8 0.6 collective-permute-done.13
  49.4 2.0 %collective-permute-start.6 = (bf16[208,256]{1,0:T(8,128)(2,1)S(1)}, bf16[208,256]{1,0:T(8,128)(2,1)S(1)}, u32[]{:S(2)}, u32[]{:S(2)}) collective-permute-start(bf16[208,256]{1,0:T(8,128)(2,1)S(1)} %collective-permute-done.2.refs_3_), channel_id=1, source_target_pairs={{0,4},{4,0},{1,5},{5,1},{2,6},{6,2},{3,7},{7,3},{8,12},{12,8},{9,1... | collective-permute-start | bytes 319496 | tf_op jit(solution)/shard_map/ppermute | solution.py:301
  51.5 0.9 collective-permute-done.6.refs_7_
  52.4 5.8 %shard_map.123 = (f32[16,32,128]{2,1,0:T(8,128)S(1)}, bf16[1536,256]{1,0:T(8,128)(2,1)S(1)}, f32[1536,128]{1,0:T(8,128)S(1)}) custom-call(bf16[208,256]{1,0:T(8,128)(2,1)S(1)} %copy-done.13, bf16[208,256]{1,0:T(8,128)(2,1)S(1)} %collective-permute-done.refs_1_, bf16[208,256]{1,0:T(8,128)(2,1)S(1)} %collective-permute-done.1.refs_2_, ...), custom_call_target="tpu_custom_call" | custom-call | flops 2415919104 | bytes 9437184 | tf_op jit(solution)/shard_map/pallas_call | solution.py:374
  58.2 0.7 copy-done.11
  58.9 3.9 %all-to-all-start.3 = ((f32[16,32,128]{2,1,0:T(8,128)}), f32[16,32,128]{2,1,0:T(8,128)S(1)}, u32[]{:S(2)}, u32[]{:S(2)}) async-start(f32[16,32,128]{2,1,0:T(8,128)} %copy-done.11), calls=%async_computation.3 | async-start | bytes 524288 | tf_op jit(solution)/shard_map/all_to_all | solution.py:296
  62.9 1.0 copy-done.12
  63.9 7.5 %shard_map.124 = bf16[3072,256]{1,0:T(8,128)(2,1)S(1)} custom-call(s32[1]{0:T(128)} %bitcast.pos_ref, bf16[1536,256]{1,0:T(8,128)(2,1)S(1)} %get-tuple-element.23.vec, f32[1536,128]{1,0:T(8,128)S(1)} %get-tuple-element.24.freq, f32[16,32,128]{2,1,0:T(8,128)S(1)} %copy-done.12, bf16[3072,256]{1,0:T(8,128)(2,1)S(1)} %maximum_dynamic-update-slice_fusion.refs_8_.q_ref), custom_call_target="tpu_custom_call" | custom-call | flops 4831838208 | bytes 4718592 | tf_op jit(solution)/shard_map/pallas_call | solution.py:385
  71.4 1.1 copy-done.5
  72.5 6.7 %all-to-all-start.2 = ((bf16[16,192,256]{2,1,0:T(8,128)(2,1)}), bf16[16,192,256]{2,1,0:T(8,128)(2,1)S(1)}, u32[]{:S(2)}, u32[]{:S(2)}) async-start(bf16[16,192,256]{2,1,0:T(8,128)(2,1)} %bitcast.40), calls=%async_computation.2 | async-start | bytes 3145728 | tf_op jit(solution)/shard_map/all_to_all | solution.py:296
  79.2 1.1 copy-done.7
  80.3 1.1 copy-done.9
  81.5 3.7 %shard_map.126 = f32[4,192,256]{2,1,0:T(8,128)S(1)} custom-call(s32[1]{0:T(128)} %bitcast.pos_ref, bf16[1536,256]{1,0:T(8,128)(2,1)S(1)} %copy-done.7, f32[1536,128]{1,0:T(8,128)S(1)} %copy-done.9, f32[16,32,128]{2,1,0:T(8,128)S(1)} %all-to-all-done.3.parts_ref, bf16[3072,256]{1,0:T(8,128)(2,1)S(1)} %maximum_dynamic-update-slice_fusion.refs_8_.q_ref), custom_call_target="tpu_custom_call" | custom-call | flops 2415919104 | bytes 2359296 | tf_op jit(solution)/shard_map/pallas_call | solution.py:409
  85.1 2.5 %collective-permute-start.14 = (f32[4,192,256]{2,1,0:T(8,128)S(1)}, f32[4,192,256]{2,1,0:T(8,128)S(1)}, u32[]{:S(2)}, u32[]{:S(2)}) collective-permute-start(f32[4,192,256]{2,1,0:T(8,128)S(1)} %shard_map.126), channel_id=1, source_target_pairs={{0,4},{4,0},{1,5},{5,1},{2,6},{6,2},{3,7},{7,3},{8,12},{12,8},{9,1... | collective-permute-start | bytes 2359304 | tf_op jit(solution)/shard_map/ppermute | solution.py:301
  87.6 3.0 %shard_map.127 = f32[3,192,256]{2,1,0:T(8,128)S(1)} custom-call(s32[1]{0:T(128)} %bitcast.pos_ref, bf16[1536,256]{1,0:T(8,128)(2,1)S(1)} %copy-done.7, f32[1536,128]{1,0:T(8,128)S(1)} %copy-done.9, f32[16,32,128]{2,1,0:T(8,128)S(1)} %all-to-all-done.3.parts_ref, bf16[3072,256]{1,0:T(8,128)(2,1)S(1)} %maximum_dynamic-update-slice_fusion.refs_8_.q_ref), custom_call_target="tpu_custom_call" | custom-call | flops 1811939328 | bytes 1769472 | tf_op jit(solution)/shard_map/pallas_call | solution.py:409
  90.7 1.2 collective-permute-start.17
  92.0 1.5 collective-permute-start.15
  93.5 1.5 collective-permute-start.16
  95.0 2.1 %shard_map.128 = f32[1,192,256]{2,1,0:T(8,128)S(1)} custom-call(s32[1]{0:T(128)} %bitcast.pos_ref, bf16[1536,256]{1,0:T(8,128)(2,1)S(1)} %copy-done.7, f32[1536,128]{1,0:T(8,128)S(1)} %copy-done.9, f32[16,32,128]{2,1,0:T(8,128)S(1)} %all-to-all-done.3.parts_ref, bf16[3072,256]{1,0:T(8,128)(2,1)S(1)} %maximum_dynamic-update-slice_fusion.refs_8_.q_ref), custom_call_target="tpu_custom_call" | custom-call | flops 603979776 | bytes 589824 | tf_op jit(solution)/shard_map/pallas_call | solution.py:409
  97.0 0.7 fusion.2.refs_0_
  97.8 0.5 collective-permute-done.15.refs_1_
  98.3 5.4 %collective-permute-done.16.refs_2_ = f32[192,256]{1,0:T(8,128)S(1)} collective-permute-done((f32[192,256]{1,0:T(8,128)S(1)}, f32[192,256]{1,0:T(8,128)S(1)}, u32[]{:S(2)}, u32[]{:S(2)}) %collective-permute-start.16) | collective-permute-done | bytes 196640 | tf_op jit(solution)/shard_map/ppermute | solution.py:301
  103.6 0.7 copy-done.19
  104.3 1.1 copy-done
  105.5 2.9 %shard_map.129 = bf16[16,2,4,40,128]{4,3,2,1,0:T(8,128)(2,1)} custom-call(f32[192,256]{1,0:T(8,128)} %fusion.2.refs_0_, f32[192,256]{1,0:T(8,128)} %copy-done.18, f32[192,256]{1,0:T(8,128)} %copy-done.19, f32[192,256]{1,0:T(8,128)} %collective-permute-done.17.refs_3_, bf16[192,256]{1,0:T(8,128)(2,1)} %get-tuple-element.29.refs_4_, ...), custom_call_target="tpu_custom_call" | custom-call | tf_op jit(solution)/shard_map/pallas_call | solution.py:440
  108.4 10.1 %all-to-all-start.4 = ((bf16[128,40,128]{2,1,0:T(8,128)(2,1)}), bf16[128,40,128]{2,1,0:T(8,128)(2,1)}, u32[]{:S(2)}, u32[]{:S(2)}) async-start(bf16[128,40,128]{2,1,0:T(8,128)(2,1)} %bitcast.42), calls=%async_computation.4 | async-start | bytes 2621440 | tf_op jit(solution)/shard_map/all_to_all | solution.py:296
  118.5 1.4 shard_map.130.active_ref
  119.9 1.3 copy-done.4
  121.4 1.3 shard_map.125
  122.7 17.9 %all-to-all-done.4.got_ref = bf16[128,40,128]{2,1,0:T(8,128)(2,1)} async-done(((bf16[128,40,128]{2,1,0:T(8,128)(2,1)}), bf16[128,40,128]{2,1,0:T(8,128)(2,1)}, u32[]{:S(2)}, u32[]{:S(2)}) %all-to-all-start.4) | async-done | bytes 1310752 | tf_op jit(solution)/shard_map/all_to_all | solution.py:296
  140.6 1.6 reduce
  142.2 0.9 broadcast_in_dim.5
  143.0 3.8 %all-to-all-start.5 = ((bf16[128,16,128]{2,1,0:T(8,128)(2,1)}), bf16[128,16,128]{2,1,0:T(8,128)(2,1)S(1)}, u32[]{:S(2)}, u32[]{:S(2)}) async-start(bf16[128,16,128]{2,1,0:T(8,128)(2,1)} %broadcast_in_dim.5), calls=%async_computation.5 | async-start | bytes 1048576 | tf_op jit(solution)/shard_map/all_to_all | solution.py:296
  147.0 0.7 convert_element_type.48.ids_ref
  147.7 11.2 %shard_map.131 = (f32[2048,256]{1,0:T(8,128)}, f32[2048,256]{1,0:T(8,128)}) custom-call(s32[1,2048]{1,0:T(1,128)} %convert_element_type.48.ids_ref, bf16[128,40,128]{2,1,0:T(8,128)(2,1)} %all-to-all-done.4.got_ref, f32[2048,256]{1,0:T(8,128)} %table_ref.3, f32[2048,256]{1,0:T(8,128)} %accum_ref.1, bf16[2048,512]{1,0:T(8,128)(2,1)} %copy-done.4, ...), custom_call_target="tpu_custom_call" | custom-call | flops 4294967296 | bytes 8388608 | tf_op jit(solution)/shard_map/pallas_call | solution.py:474
  158.9 2.0 %all-to-all-done.5 = bf16[128,16,128]{2,1,0:T(8,128)(2,1)S(1)} async-done(((bf16[128,16,128]{2,1,0:T(8,128)(2,1)}), bf16[128,16,128]{2,1,0:T(8,128)(2,1)S(1)}, u32[]{:S(2)}, u32[]{:S(2)}) %all-to-all-start.5) | async-done | bytes 524320 | tf_op jit(solution)/shard_map/all_to_all | solution.py:296
  160.9 1.1 fusion.6
  (73 shorter events, 0.9 us)
Async XLA Ops:
  2.3 15.5 %all-to-all-start = ((s32[32,1,128]{2,1,0:T(1,128)}), s32[32,1,128]{2,1,0:T(1,128)S(1)}, u32[]{:S(2)}, u32[]{:S(2)}) async-start(s32[32,1,128]{2,1,0:T(1,128)} %bitcast.41), calls=%async_computation | async-start | bytes 32768 | tf_op jit(solution)/shard_map/all_to_all | solution.py:296
  10.9 0.9 copy-start.14
  11.8 0.7 copy-start.17
  12.5 3.9 %copy-start.20 = (bf16[192]{0:T(256)(128)(2,1)S(1)}, bf16[192]{0:T(256)(128)(2,1)}, u32[]{:S(2)}) copy-start(bf16[192]{0:T(256)(128)(2,1)} %param.11) | copy-start | bytes 1156
  12.5 5.4 %copy-start.2 = (f32[2048,256]{1,0:T(8,128)S(1)}, f32[2048,256]{1,0:T(8,128)}, u32[]{:S(2)}) copy-start(f32[2048,256]{1,0:T(8,128)} %table_ref.3) | copy-start | bytes 6291460
  12.5 14.7 %copy-start.15 = (bf16[192,256]{1,0:T(8,128)(2,1)S(1)}, bf16[192,256]{1,0:T(8,128)(2,1)}, u32[]{:S(2)}) copy-start(bf16[192,256]{1,0:T(8,128)(2,1)} %q_ref.1) | copy-start | bytes 294916
  12.5 14.6 %collective-permute-start.7 = (bf16[192,256]{1,0:T(8,128)(2,1)S(1)}, bf16[192,256]{1,0:T(8,128)(2,1)S(1)}, u32[]{:S(2)}, u32[]{:S(2)}) collective-permute-start(bf16[192,256]{1,0:T(8,128)(2,1)S(1)} %shard_map.121), channel_id=1, source_target_pairs={{0,96},{32,0},{64,32},{96,64},{1,97},{33,1},{65,33},{97,65},{2,98}... | collective-permute-start | bytes 294920 | tf_op jit(solution)/shard_map/ppermute | solution.py:301
  15.2 11.9 %collective-permute-start.8 = (bf16[192,256]{1,0:T(8,128)(2,1)S(1)}, bf16[192,256]{1,0:T(8,128)(2,1)S(1)}, u32[]{:S(2)}, u32[]{:S(2)}) collective-permute-start(bf16[192,256]{1,0:T(8,128)(2,1)S(1)} %shard_map.121), channel_id=1, source_target_pairs={{0,64},{32,96},{64,0},{96,32},{1,65},{33,97},{65,1},{97,33},{2,66}... | collective-permute-start | bytes 294920 | tf_op jit(solution)/shard_map/ppermute | solution.py:301
  15.8 11.4 %collective-permute-start.9 = (bf16[192,256]{1,0:T(8,128)(2,1)S(1)}, bf16[192,256]{1,0:T(8,128)(2,1)S(1)}, u32[]{:S(2)}, u32[]{:S(2)}) collective-permute-start(bf16[192,256]{1,0:T(8,128)(2,1)S(1)} %shard_map.121), channel_id=1, source_target_pairs={{0,32},{32,64},{64,96},{96,0},{1,33},{33,65},{65,97},{97,1},{2,34}... | collective-permute-start | bytes 294920 | tf_op jit(solution)/shard_map/ppermute | solution.py:301
  20.4 15.6 %all-to-all-start.1 = ((bf16[32,12,256]{2,1,0:T(8,128)(2,1)}), bf16[32,12,256]{2,1,0:T(8,128)(2,1)S(1)}, u32[]{:S(2)}, u32[]{:S(2)}) async-start(bf16[32,12,256]{2,1,0:T(8,128)(2,1)} %convert_element_type.42), calls=%async_computation.1 | async-start | bytes 524288 | tf_op jit(solution)/shard_map/all_to_all | solution.py:296
  27.2 16.2 %collective-permute-start.10 = (bf16[768,256]{1,0:T(8,128)(2,1)S(1)}, bf16[768,256]{1,0:T(8,128)(2,1)S(1)}, u32[]{:S(2)}, u32[]{:S(2)}) collective-permute-start(bf16[768,256]{1,0:T(8,128)(2,1)S(1)} %shard_map.122), channel_id=1, source_target_pairs={{0,3},{1,0},{2,1},{3,2},{4,7},{5,4},{6,5},{7,6},{8,11},{9,8},{10,9... | collective-permute-start | bytes 1179656 | tf_op jit(solution)/shard_map/ppermute | solution.py:301
  31.1 11.4 %collective-permute-start.11 = (bf16[768,256]{1,0:T(8,128)(2,1)S(1)}, bf16[768,256]{1,0:T(8,128)(2,1)S(1)}, u32[]{:S(2)}, u32[]{:S(2)}) collective-permute-start(bf16[768,256]{1,0:T(8,128)(2,1)S(1)} %shard_map.122), channel_id=1, source_target_pairs={{0,1},{1,2},{2,3},{3,0},{4,5},{5,6},{6,7},{7,4},{8,9},{9,10},{10,1... | collective-permute-start | bytes 1179656 | tf_op jit(solution)/shard_map/ppermute | solution.py:301
  39.1 6.7 %copy-start.13 = (bf16[208,256]{1,0:T(8,128)(2,1)S(1)}, bf16[208,256]{1,0:T(8,128)(2,1)}, u32[]{:S(2)}) copy-start(bf16[208,256]{1,0:T(8,128)(2,1)} %get-tuple-element.22.refs_0_.pay_ref) | copy-start | bytes 319492
  39.1 6.7 %collective-permute-start = (bf16[208,256]{1,0:T(8,128)(2,1)}, bf16[208,256]{1,0:T(8,128)(2,1)S(1)}, u32[]{:S(2)}, u32[]{:S(2)}) collective-permute-start(bf16[208,256]{1,0:T(8,128)(2,1)} %get-tuple-element.22.refs_0_.pay_ref), channel_id=1, source_target_pairs={{0,8},{8,16},{16,24},{24,0},{1,9},{9,17},{17,25},{25,1},{2,10},{10... | collective-permute-start | bytes 319496 | tf_op jit(solution)/shard_map/ppermute | solution.py:301
  39.3 8.9 %collective-permute-start.1 = (bf16[208,256]{1,0:T(8,128)(2,1)}, bf16[208,256]{1,0:T(8,128)(2,1)S(1)}, u32[]{:S(2)}, u32[]{:S(2)}) collective-permute-start(bf16[208,256]{1,0:T(8,128)(2,1)} %get-tuple-element.22.refs_0_.pay_ref), channel_id=1, source_target_pairs={{0,16},{8,24},{16,0},{24,8},{1,17},{9,25},{17,1},{25,9},{2,18},{10... | collective-permute-start | bytes 319496 | tf_op jit(solution)/shard_map/ppermute | solution.py:301
  41.2 7.0 %collective-permute-start.2 = (bf16[208,256]{1,0:T(8,128)(2,1)}, bf16[208,256]{1,0:T(8,128)(2,1)S(1)}, u32[]{:S(2)}, u32[]{:S(2)}) collective-permute-start(bf16[208,256]{1,0:T(8,128)(2,1)} %get-tuple-element.22.refs_0_.pay_ref), channel_id=1, source_target_pairs={{0,24},{8,0},{16,8},{24,16},{1,25},{9,1},{17,9},{25,17},{2,26},{10... | collective-permute-start | bytes 319496 | tf_op jit(solution)/shard_map/ppermute | solution.py:301
  42.5 7.0 %collective-permute-start.13 = (bf16[384,256]{1,0:T(8,128)(2,1)S(1)}, bf16[384,256]{1,0:T(8,128)(2,1)S(1)}, u32[]{:S(2)}, u32[]{:S(2)}) collective-permute-start(bf16[384,256]{1,0:T(8,128)(2,1)S(1)} %slice.84), channel_id=1, source_target_pairs={{0,1},{1,2},{2,3},{3,0},{4,5},{5,6},{6,7},{7,4},{8,9},{9,10},{10,1... | collective-permute-start | bytes 589832 | tf_op jit(solution)/shard_map/ppermute | solution.py:301
  43.5 8.0 %collective-permute-start.12 = (bf16[384,256]{1,0:T(8,128)(2,1)S(1)}, bf16[384,256]{1,0:T(8,128)(2,1)S(1)}, u32[]{:S(2)}, u32[]{:S(2)}) collective-permute-start(bf16[384,256]{1,0:T(8,128)(2,1)S(1)} %slice.83), channel_id=1, source_target_pairs={{0,3},{1,0},{2,1},{3,2},{4,7},{5,4},{6,5},{7,6},{8,11},{9,8},{10,9... | collective-permute-start | bytes 589832 | tf_op jit(solution)/shard_map/ppermute | solution.py:301
  45.8 5.7 %collective-permute-start.3 = (bf16[208,256]{1,0:T(8,128)(2,1)S(1)}, bf16[208,256]{1,0:T(8,128)(2,1)S(1)}, u32[]{:S(2)}, u32[]{:S(2)}) collective-permute-start(bf16[208,256]{1,0:T(8,128)(2,1)S(1)} %copy-done.13), channel_id=1, source_target_pairs={{0,4},{4,0},{1,5},{5,1},{2,6},{6,2},{3,7},{7,3},{8,12},{12,8},{9,1... | collective-permute-start | bytes 319496 | tf_op jit(solution)/shard_map/ppermute | solution.py:301
  48.2 3.3 %collective-permute-start.4 = (bf16[208,256]{1,0:T(8,128)(2,1)S(1)}, bf16[208,256]{1,0:T(8,128)(2,1)S(1)}, u32[]{:S(2)}, u32[]{:S(2)}) collective-permute-start(bf16[208,256]{1,0:T(8,128)(2,1)S(1)} %collective-permute-done.refs_1_), channel_id=1, source_target_pairs={{0,4},{4,0},{1,5},{5,1},{2,6},{6,2},{3,7},{7,3},{8,12},{12,8},{9,1... | collective-permute-start | bytes 319496 | tf_op jit(solution)/shard_map/ppermute | solution.py:301
  48.2 3.3 %collective-permute-start.5 = (bf16[208,256]{1,0:T(8,128)(2,1)S(1)}, bf16[208,256]{1,0:T(8,128)(2,1)S(1)}, u32[]{:S(2)}, u32[]{:S(2)}) collective-permute-start(bf16[208,256]{1,0:T(8,128)(2,1)S(1)} %collective-permute-done.1.refs_2_), channel_id=1, source_target_pairs={{0,4},{4,0},{1,5},{5,1},{2,6},{6,2},{3,7},{7,3},{8,12},{12,8},{9,1... | collective-permute-start | bytes 319496 | tf_op jit(solution)/shard_map/ppermute | solution.py:301
  49.4 3.0 %collective-permute-start.6 = (bf16[208,256]{1,0:T(8,128)(2,1)S(1)}, bf16[208,256]{1,0:T(8,128)(2,1)S(1)}, u32[]{:S(2)}, u32[]{:S(2)}) collective-permute-start(bf16[208,256]{1,0:T(8,128)(2,1)S(1)} %collective-permute-done.2.refs_3_), channel_id=1, source_target_pairs={{0,4},{4,0},{1,5},{5,1},{2,6},{6,2},{3,7},{7,3},{8,12},{12,8},{9,1... | collective-permute-start | bytes 319496 | tf_op jit(solution)/shard_map/ppermute | solution.py:301
  58.2 0.7 copy-start.11
  58.9 12.4 %copy-start.6 = (bf16[1536,256]{1,0:T(8,128)(2,1)}, bf16[1536,256]{1,0:T(8,128)(2,1)S(1)}, u32[]{:S(2)}) copy-start(bf16[1536,256]{1,0:T(8,128)(2,1)S(1)} %get-tuple-element.23.vec) | copy-start | bytes 2359300
  58.9 12.4 %copy-start.8 = (f32[1536,128]{1,0:T(8,128)}, f32[1536,128]{1,0:T(8,128)S(1)}, u32[]{:S(2)}) copy-start(f32[1536,128]{1,0:T(8,128)S(1)} %get-tuple-element.24.freq) | copy-start | bytes 2359300
  58.9 13.6 %all-to-all-start.3 = ((f32[16,32,128]{2,1,0:T(8,128)}), f32[16,32,128]{2,1,0:T(8,128)S(1)}, u32[]{:S(2)}, u32[]{:S(2)}) async-start(f32[16,32,128]{2,1,0:T(8,128)} %copy-done.11), calls=%async_computation.3 | async-start | bytes 524288 | tf_op jit(solution)/shard_map/all_to_all | solution.py:296
  62.9 1.0 copy-start.12
  71.4 1.1 copy-start.5
  72.5 31.8 %all-to-all-start.2 = ((bf16[16,192,256]{2,1,0:T(8,128)(2,1)}), bf16[16,192,256]{2,1,0:T(8,128)(2,1)S(1)}, u32[]{:S(2)}, u32[]{:S(2)}) async-start(bf16[16,192,256]{2,1,0:T(8,128)(2,1)} %bitcast.40), calls=%async_computation.2 | async-start | bytes 3145728 | tf_op jit(solution)/shard_map/all_to_all | solution.py:296
  79.2 1.1 copy-start.7
  80.3 1.1 copy-start.9
  85.1 5.5 %collective-permute-start.14 = (f32[4,192,256]{2,1,0:T(8,128)S(1)}, f32[4,192,256]{2,1,0:T(8,128)S(1)}, u32[]{:S(2)}, u32[]{:S(2)}) collective-permute-start(f32[4,192,256]{2,1,0:T(8,128)S(1)} %shard_map.126), channel_id=1, source_target_pairs={{0,4},{4,0},{1,5},{5,1},{2,6},{6,2},{3,7},{7,3},{8,12},{12,8},{9,1... | collective-permute-start | bytes 2359304 | tf_op jit(solution)/shard_map/ppermute | solution.py:301
  90.7 13.6 %collective-permute-start.17 = (f32[192,256]{1,0:T(8,128)S(1)}, f32[192,256]{1,0:T(8,128)}, u32[]{:S(2)}, u32[]{:S(2)}) collective-permute-start(f32[192,256]{1,0:T(8,128)S(1)} %get-tuple-element.37), channel_id=1, source_target_pairs={{0,8},{8,16},{16,24},{24,0},{1,9},{9,17},{17,25},{25,1},{2,10},{10... | collective-permute-start | bytes 589832 | tf_op jit(solution)/shard_map/ppermute | solution.py:301
  92.0 6.3 %collective-permute-start.15 = (f32[192,256]{1,0:T(8,128)S(1)}, f32[192,256]{1,0:T(8,128)S(1)}, u32[]{:S(2)}, u32[]{:S(2)}) collective-permute-start(f32[192,256]{1,0:T(8,128)S(1)} %get-tuple-element.36), channel_id=1, source_target_pairs={{0,24},{8,0},{16,8},{24,16},{1,25},{9,1},{17,9},{25,17},{2,26},{10... | collective-permute-start | bytes 589832 | tf_op jit(solution)/shard_map/ppermute | solution.py:301
  93.5 10.2 %collective-permute-start.16 = (f32[192,256]{1,0:T(8,128)S(1)}, f32[192,256]{1,0:T(8,128)S(1)}, u32[]{:S(2)}, u32[]{:S(2)}) collective-permute-start(f32[192,256]{1,0:T(8,128)S(1)} %get-tuple-element.35), channel_id=1, source_target_pairs={{0,16},{8,24},{16,0},{24,8},{1,17},{9,25},{17,1},{25,9},{2,18},{10... | collective-permute-start | bytes 589832 | tf_op jit(solution)/shard_map/ppermute | solution.py:301
  98.3 5.4 %copy-start.18 = (f32[192,256]{1,0:T(8,128)}, f32[192,256]{1,0:T(8,128)S(1)}, u32[]{:S(2)}) copy-start(f32[192,256]{1,0:T(8,128)S(1)} %collective-permute-done.15.refs_1_) | copy-start | bytes 589828
  103.6 0.7 copy-start.19
  104.3 1.1 copy-start
  108.4 10.1 %copy-start.3 = (f32[2048,256]{1,0:T(8,128)S(1)}, f32[2048,256]{1,0:T(8,128)}, u32[]{:S(2)}) copy-start(f32[2048,256]{1,0:T(8,128)} %table_ref.3) | copy-start | bytes 6291460
  108.4 10.1 %copy-start.10 = (bf16[256,512]{1,0:T(8,128)(2,1)S(1)}, bf16[256,512]{1,0:T(8,128)(2,1)}, u32[]{:S(2)}) copy-start(bf16[256,512]{1,0:T(8,128)(2,1)} %w_in_ref.5) | copy-start | bytes 786436
  108.4 32.2 %all-to-all-start.4 = ((bf16[128,40,128]{2,1,0:T(8,128)(2,1)}), bf16[128,40,128]{2,1,0:T(8,128)(2,1)}, u32[]{:S(2)}, u32[]{:S(2)}) async-start(bf16[128,40,128]{2,1,0:T(8,128)(2,1)} %bitcast.42), calls=%async_computation.4 | async-start | bytes 2621440 | tf_op jit(solution)/shard_map/all_to_all | solution.py:296
  118.5 2.9 %copy-start.1 = (bf16[16,192,256]{2,1,0:T(8,128)(2,1)S(1)}, bf16[16,192,256]{2,1,0:T(8,128)(2,1)}, u32[]{:S(2)}) copy-start(bf16[16,192,256]{2,1,0:T(8,128)(2,1)} %copy-done) | copy-start | bytes 4718596
  118.5 2.9 %copy-start.16 = (bf16[192,256]{1,0:T(8,128)(2,1)S(1)}, bf16[192,256]{1,0:T(8,128)(2,1)}, u32[]{:S(2)}) copy-start(bf16[192,256]{1,0:T(8,128)(2,1)} %q_ref.1) | copy-start | bytes 294916
  119.9 1.3 copy-start.4
  143.0 17.9 %all-to-all-start.5 = ((bf16[128,16,128]{2,1,0:T(8,128)(2,1)}), bf16[128,16,128]{2,1,0:T(8,128)(2,1)S(1)}, u32[]{:S(2)}, u32[]{:S(2)}) async-start(bf16[128,16,128]{2,1,0:T(8,128)(2,1)} %broadcast_in_dim.5), calls=%async_computation.5 | async-start | bytes 1048576 | tf_op jit(solution)/shard_map/all_to_all | solution.py:296

commit v5 on v4

--- a/solution.py
+++ b/solution.py
@@ -35,6 +35,7 @@
 bf16 = jnp.bfloat16
 i32 = jnp.int32
 VMEM = pltpu.MemorySpace.VMEM
+HBM = pltpu.MemorySpace.HBM
 NT = (((1,), (1,)), ((), ()))
 TN = (((0,), (0,)), ((), ()))
 
@@ -136,7 +137,7 @@
 
 
 def score_kernel(*refs):
-    vec_refs, (q_ref, ids_ref, lse_ref, vec, freq, *scores) = refs[:NB], refs[NB:]
+    vec_refs, (q_ref, ids_ref, lse_ref, part_ref, vec, freq, *scores) = refs[:NB], refs[NB:]
     lse_ref[:, LINES:SENT, :] = jnp.broadcast_to(ids_ref[...][None], (NA, 8, 128))
     load_vecs(vec_refs, vec, freq)
     tops = []
@@ -163,6 +164,7 @@
                 row = part[:, k * 128 : (k + 1) * 128].reshape(1, 1, 128)
                 at = (j - 1) * n + k
                 lse_ref[:, at : at + 1, :] = jnp.broadcast_to(row, (NA, 1, 128))
+                part_ref[at : at + 1, :] = row.reshape(1, 128)
 
 
 def is_pair(pos_ref):
@@ -183,7 +185,7 @@
             turned[:, k : k + 256] = vec[k : k + 256, :].astype(f32).T.astype(bf16)
 
     q = q_ref[...] * jnp.asarray(score_scale, bf16)
-    norm = query_lanes(part_ref, 0).reshape(1, QB)
+    norm = query_lanes(part_ref)
     for b in range(0, VS, VB):
         at = slice(b, b + VB)
         p = jnp.exp(mm(vec[at, :], q, NT) - lanes(freq[at, :]) - norm)
@@ -268,6 +270,12 @@
             out_ref[:, c, z] = jnp.concatenate(rows, axis=1).astype(bf16)
 
 
+def sum_kernel(got_ref, out_ref):
+    total = jnp.sum(got_ref[...].astype(f32), axis=0)
+    total = jnp.concatenate([total[32:36], total[12:16], total[36:40], total[28:32]], axis=0)
+    out_ref[...] = jnp.broadcast_to(total.astype(bf16)[None], (128, SLOT, 128))
+
+
 TB = 512
 
 
@@ -307,10 +315,6 @@
 
 def unread(n):
     return [pl.BlockSpec(memory_space=pl.ANY)] * n
-
-
-def after(x, *others):
-    return lax.optimization_barrier((x, *others))[0]
 
 
 def const(*shape):
@@ -371,20 +375,20 @@
     vecs = [pay] + [shift(pay, "y", k) for k in range(1, 4)]
     vecs = vecs + [shift(v, "c", 1) for v in vecs]
 
-    part_lse, vec_all, freq_all = call(
+    sent_lse, part_lse, vec_all, freq_all = call(
         score_kernel,
-        (sds((NA, SENT, 128), f32), sds((VS, E), bf16), sds((VS, 128), f32)),
+        (HBM((NA, SENT, 128), f32), sds((LINES, 128), f32), sds((VS, E), bf16), sds((VS, 128), f32)),
         cost=(2 * VS * QS * E, VS * QS * 2, VS * QS),
         limit=LIMIT,
         in_specs=whole(NB + 2),
-        out_specs=tuple(whole(3)),
+        out_specs=tuple(whole(4)),
         scratch_shapes=[pltpu.VMEM((VS, PB), f32)] * 2,
     )(*vecs, all_q, ids)
-    all_lse = a2a(part_lse, A)
+    all_lse = a2a(sent_lse, A)
     here = here_z * 4 + here_x
     o = call(
         query_kernel,
-        sds((QS, E), bf16),
+        HBM((QS, E), bf16),
         cost=(4 * VS * QS * E, VS * QS, VS * QS),
         limit=LIMIT,
         grid_spec=pltpu.PrefetchScalarGridSpec(
@@ -393,7 +397,7 @@
             in_specs=[
                 const(VS, E),
                 const(VS, 128),
-                const(NA, SENT, 128),
+                const(LINES, 128),
                 pl.BlockSpec((QB, E), lambda i, pos: (i, 0)),
             ],
             out_specs=pl.BlockSpec((QB, E), lambda i, pos: (i, 0)),
@@ -464,9 +468,14 @@
         in_specs=[pl.BlockSpec((TB, E), lambda i: (i, 0)), const(E, H)],
         out_specs=pl.BlockSpec((TB, H), lambda i: (i, 0)),
     )(table, w_in)
-    w_sum = jnp.sum(back.astype(f32), axis=0)
-    w_sum = jnp.concatenate([w_sum[32:36], w_sum[12:16], w_sum[36:40], w_sum[28:32]], axis=0)
-    w_sum = after(jnp.broadcast_to(w_sum.astype(bf16)[None], (128, SLOT, 128)), query_grad, active)
+    back, query_grad, active = lax.optimization_barrier((back, query_grad, active))
+    w_sum = call(
+        sum_kernel,
+        HBM((128, SLOT, 128), bf16),
+        limit=LIMIT,
+        in_specs=whole(1),
+        out_specs=whole(1)[0],
+    )(back)
     w_all = a2a(w_sum, ALL).reshape(16, 2, 4, SLOT, 128).astype(f32)
     row_ids = all_lse.reshape(4, 4, SENT, 128)[:, :, LINES : LINES + 4]
     row_ids = lax.dynamic_index_in_dim(row_ids, here_x, axis=1, keepdims=False)

time: 163 us -> 159 us (0.975)
  local copies, waits for them, and re-layouts: 17 us -> 14.2 us
    unnamed x43, local copies, waits for them, and re-layouts: 9.92 us -> 8.04 us
    pallas_call x2 -> x3, Pallas kernels: 13.3 us -> 15 us  [the longest x1 7.78 us: local(): call(query_kernel, HBM((QS, E), bf16), cost=(4 * VS * QS * E, VS * QS, VS...]
  transfers between devices with their start and end apart: 24 -> 24, of which waited for: 9 -> 9; matrix products, arithmetic and copies ran while one was open for 4% -> 4% of each run, Pallas kernels for 20% -> 21%
where the time goes in v5:
time: 159 us; the launch traced here: 158 us
  starting transfers between devices  64.5 us (41%)
  Pallas kernels  44.4 us (28%)
  waiting for transfers between devices  33.1 us (21%)
  local copies, waits for them, and re-layouts  14.2 us (9%)
    all_to_all x6, starting transfers between devices, a2a(): return lax.all_to_all(x, axes, split_axis=0, concat_axis=0, tiled=True)  39.3 us
    ppermute x18, starting transfers between devices, shift(): return lax.ppermute(x, axis, [(i, (i + k) % n) for i in range(n)])  25.3 us
    all_to_all x6, waiting for transfers between devices, a2a(): return lax.all_to_all(x, axes, split_axis=0, concat_axis=0, tiled=True)  24.9 us
    pallas_call x1, Pallas kernels, local(): call(update_kernel, (sds((ROWS, E), f32), sds((ROWS, E), f32)), cost=(4 *...  11.2 us
    pallas_call x3, Pallas kernels, vec_grads(): call(functools.partial(vec_kernel, first, n), sds((n, PAIRS, E), f32), co...  8.62 us
    ppermute x18, waiting for transfers between devices, shift(): return lax.ppermute(x, axis, [(i, (i + k) % n) for i in range(n)])  8.17 us
    unnamed x43, local copies, waits for them, and re-layouts  8.04 us
    pallas_call x1, Pallas kernels, local(): call(query_kernel, HBM((QS, E), bf16), cost=(4 * VS * QS * E, VS * QS, VS...  7.78 us
  transfers between devices with their start and end apart: 24, of which 9 were waited for; matrix products, arithmetic and copies ran while one was open for 4% of the time, Pallas kernels for 21%

profile of v5, /device:TPU:1, one launch (start us, length us, event | category | flops | bytes accessed | tf_op | source)
XLA Modules:
  0.0 158.2 jit_solution(7944144227602129446)
XLA Ops:
  0.6 1.7 %shard_map.119 = (s32[32,128]{1,0:T(8,128)}, s32[1,256]{1,0:T(1,128)}, bf16[192,384]{1,0:T(8,128)(2,1)}) custom-call(s32[1,192]{1,0:T(1,128)} %bitcast.49, s32[1,192]{1,0:T(1,128)} %bitcast.50), custom_call_target="tpu_custom_call" | custom-call | tf_op jit(solution)/shard_map/pallas_call | solution.py:327
  2.3 8.6 %all-to-all-start = ((s32[32,1,128]{2,1,0:T(1,128)}), s32[32,1,128]{2,1,0:T(1,128)S(1)}, u32[]{:S(2)}, u32[]{:S(2)}) async-start(s32[32,1,128]{2,1,0:T(1,128)} %bitcast.41), calls=%async_computation | async-start | bytes 32768 | tf_op jit(solution)/shard_map/all_to_all | solution.py:304
  10.9 0.9 copy-done.14
  11.8 0.7 copy-done.17
  12.5 2.7 %collective-permute-start.7 = (bf16[192,256]{1,0:T(8,128)(2,1)S(1)}, bf16[192,256]{1,0:T(8,128)(2,1)S(1)}, u32[]{:S(2)}, u32[]{:S(2)}) collective-permute-start(bf16[192,256]{1,0:T(8,128)(2,1)S(1)} %shard_map.121), channel_id=1, source_target_pairs={{0,96},{32,0},{64,32},{96,64},{1,97},{33,1},{65,33},{97,65},{2,98}... | collective-permute-start | bytes 294920 | tf_op jit(solution)/shard_map/ppermute | solution.py:309
  15.2 0.5 collective-permute-start.8
  15.8 0.6 collective-permute-start.9
  16.4 0.6 pad.12.freq_ref
  17.0 0.8 all-to-all-done
  17.8 0.1 reshape.111
  17.9 1.7 %gather_fusion = bf16[384,256]{1,0:T(8,128)(2,1)S(1)} fusion(f32[2048,256]{1,0:T(8,128)S(1)} %copy-done.2, s32[1024]{0:T(1024)S(1)} %pad_clamp_fusion), kind=kCustom, calls=%fused_computation | custom fusion | bytes 394752 | tf_op jit(solution)/shard_map/gather | solution.py:351
  19.6 0.7 convert_element_type.34
  20.4 6.6 %all-to-all-start.1 = ((bf16[32,12,256]{2,1,0:T(8,128)(2,1)}), bf16[32,12,256]{2,1,0:T(8,128)(2,1)S(1)}, u32[]{:S(2)}, u32[]{:S(2)}) async-start(bf16[32,12,256]{2,1,0:T(8,128)(2,1)} %convert_element_type.34), calls=%async_computation.1 | async-start | bytes 524288 | tf_op jit(solution)/shard_map/all_to_all | solution.py:304
  27.2 3.8 %collective-permute-start.10 = (bf16[768,256]{1,0:T(8,128)(2,1)S(1)}, bf16[768,256]{1,0:T(8,128)(2,1)S(1)}, u32[]{:S(2)}, u32[]{:S(2)}) collective-permute-start(bf16[768,256]{1,0:T(8,128)(2,1)S(1)} %shard_map.122), channel_id=1, source_target_pairs={{0,3},{1,0},{2,1},{3,2},{4,7},{5,4},{6,5},{7,6},{8,11},{9,8},{10,9... | collective-permute-start | bytes 1179656 | tf_op jit(solution)/shard_map/ppermute | solution.py:309
  31.1 0.1 broadcast_in_dim.4
  31.2 4.8 %all-to-all-done.1 = bf16[32,12,256]{2,1,0:T(8,128)(2,1)S(1)} async-done(((bf16[32,12,256]{2,1,0:T(8,128)(2,1)}), bf16[32,12,256]{2,1,0:T(8,128)(2,1)S(1)}, u32[]{:S(2)}, u32[]{:S(2)}) %all-to-all-start.1) | async-done | bytes 196640 | tf_op jit(solution)/shard_map/all_to_all | solution.py:304
  36.0 0.7 reshape.99.got_ref
  36.7 2.3 %shard_map.120 = (bf16[192,256]{1,0:T(8,128)(2,1)}, bf16[192,512]{1,0:T(8,128)(2,1)}, bf16[208,256]{1,0:T(8,128)(2,1)}) custom-call(bf16[384,256]{1,0:T(8,128)(2,1)} %reshape.99.got_ref, bf16[192,384]{1,0:T(8,128)(2,1)} %get-tuple-element.24.pick_ref, bf16[256,512]{1,0:T(8,128)(2,1)} %w_in_ref.5, bf16[512,256]{1,0:T(8,128)(2,1)} %w_out_ref.3, ...), custom_call_target="tpu_custom_call" | custom-call | flops 25769803776 | bytes 1048576 | tf_op jit(solution)/shard_map/pallas_call | solution.py:368
  39.1 0.2 collective-permute-start
  39.3 1.9 %collective-permute-start.1 = (bf16[208,256]{1,0:T(8,128)(2,1)}, bf16[208,256]{1,0:T(8,128)(2,1)S(1)}, u32[]{:S(2)}, u32[]{:S(2)}) collective-permute-start(bf16[208,256]{1,0:T(8,128)(2,1)} %get-tuple-element.25.refs_0_.pay_ref), channel_id=1, source_target_pairs={{0,16},{8,24},{16,0},{24,8},{1,17},{9,25},{17,1},{25,9},{2,18},{10... | collective-permute-start | bytes 319496 | tf_op jit(solution)/shard_map/ppermute | solution.py:309
  41.2 0.5 collective-permute-start.2
  41.7 0.7 collective-permute-done.11
  42.5 1.0 collective-permute-start.13
  43.5 2.2 %collective-permute-start.12 = (bf16[384,256]{1,0:T(8,128)(2,1)S(1)}, bf16[384,256]{1,0:T(8,128)(2,1)S(1)}, u32[]{:S(2)}, u32[]{:S(2)}) collective-permute-start(bf16[384,256]{1,0:T(8,128)(2,1)S(1)} %slice.63), channel_id=1, source_target_pairs={{0,3},{1,0},{2,1},{3,2},{4,7},{5,4},{6,5},{7,6},{8,11},{9,8},{10,9... | collective-permute-start | bytes 589832 | tf_op jit(solution)/shard_map/ppermute | solution.py:309
  45.8 2.4 %collective-permute-start.3 = (bf16[208,256]{1,0:T(8,128)(2,1)S(1)}, bf16[208,256]{1,0:T(8,128)(2,1)S(1)}, u32[]{:S(2)}, u32[]{:S(2)}) collective-permute-start(bf16[208,256]{1,0:T(8,128)(2,1)S(1)} %copy-done.13), channel_id=1, source_target_pairs={{0,4},{4,0},{1,5},{5,1},{2,6},{6,2},{3,7},{7,3},{8,12},{12,8},{9,1... | collective-permute-start | bytes 319496 | tf_op jit(solution)/shard_map/ppermute | solution.py:309
  48.2 0.1 collective-permute-start.4
  48.2 0.5 collective-permute-start.5
  48.8 0.6 collective-permute-done.13
  49.4 2.0 %collective-permute-start.6 = (bf16[208,256]{1,0:T(8,128)(2,1)S(1)}, bf16[208,256]{1,0:T(8,128)(2,1)S(1)}, u32[]{:S(2)}, u32[]{:S(2)}) collective-permute-start(bf16[208,256]{1,0:T(8,128)(2,1)S(1)} %collective-permute-done.2.refs_3_), channel_id=1, source_target_pairs={{0,4},{4,0},{1,5},{5,1},{2,6},{6,2},{3,7},{7,3},{8,12},{12,8},{9,1... | collective-permute-start | bytes 319496 | tf_op jit(solution)/shard_map/ppermute | solution.py:309
  51.5 0.9 collective-permute-done.6.refs_7_
  52.4 6.1 %shard_map.123 = (f32[16,32,128]{2,1,0:T(8,128)}, f32[24,128]{1,0:T(8,128)S(1)}, bf16[1536,256]{1,0:T(8,128)(2,1)S(1)}, f32[1536,128]{1,0:T(8,128)S(1)}) custom-call(bf16[208,256]{1,0:T(8,128)(2,1)S(1)} %copy-done.13, bf16[208,256]{1,0:T(8,128)(2,1)S(1)} %collective-permute-done.refs_1_, bf16[208,256]{1,0:T(8,128)(2,1)S(1)} %collective-permute-done.1.refs_2_, ...), custom_call_target="tpu_custom_call" | custom-call | flops 2415919104 | bytes 9437184 | tf_op jit(solution)/shard_map/pallas_call | solution.py:378
  58.5 3.9 %all-to-all-start.2 = ((f32[16,32,128]{2,1,0:T(8,128)}), f32[16,32,128]{2,1,0:T(8,128)S(1)}, u32[]{:S(2)}, u32[]{:S(2)}) async-start(f32[16,32,128]{2,1,0:T(8,128)} %get-tuple-element.28), calls=%async_computation.2 | async-start | bytes 524288 | tf_op jit(solution)/shard_map/all_to_all | solution.py:304
  62.5 7.8 %shard_map.124 = bf16[3072,256]{1,0:T(8,128)(2,1)} custom-call(s32[1]{0:T(128)} %bitcast.pos_ref, bf16[1536,256]{1,0:T(8,128)(2,1)S(1)} %get-tuple-element.26.vec, f32[1536,128]{1,0:T(8,128)S(1)} %get-tuple-element.27.freq, f32[24,128]{1,0:T(8,128)S(1)} %get-tuple-element.29.part_ref, bf16[3072,256]{1,0:T(8,128)(2,1)S(1)} %maximum_dynamic-update-slice_fusion.refs_8_.q_ref), custom_call_target="tpu_custom_call" | custom-call | flops 4831838208 | bytes 4718592 | tf_op jit(solution)/shard_map/pallas_call | solution.py:389
  70.3 6.7 %all-to-all-start.3 = ((bf16[16,192,256]{2,1,0:T(8,128)(2,1)}), bf16[16,192,256]{2,1,0:T(8,128)(2,1)S(1)}, u32[]{:S(2)}, u32[]{:S(2)}) async-start(bf16[16,192,256]{2,1,0:T(8,128)(2,1)} %bitcast.44), calls=%async_computation.3 | async-start | bytes 3145728 | tf_op jit(solution)/shard_map/all_to_all | solution.py:304
  77.0 1.1 copy-done.9
  78.1 1.1 copy-done.11
  79.2 3.6 %shard_map.125 = f32[4,192,256]{2,1,0:T(8,128)S(1)} custom-call(s32[1]{0:T(128)} %bitcast.pos_ref, bf16[1536,256]{1,0:T(8,128)(2,1)S(1)} %copy-done.9, f32[1536,128]{1,0:T(8,128)S(1)} %copy-done.11, f32[16,32,128]{2,1,0:T(8,128)S(1)} %all-to-all-done.2.parts_ref, bf16[3072,256]{1,0:T(8,128)(2,1)S(1)} %maximum_dynamic-update-slice_fusion.refs_8_.q_ref), custom_call_target="tpu_custom_call" | custom-call | flops 2415919104 | bytes 2359296 | tf_op jit(solution)/shard_map/pallas_call | solution.py:413
  82.8 2.5 %collective-permute-start.14 = (f32[4,192,256]{2,1,0:T(8,128)S(1)}, f32[4,192,256]{2,1,0:T(8,128)S(1)}, u32[]{:S(2)}, u32[]{:S(2)}) collective-permute-start(f32[4,192,256]{2,1,0:T(8,128)S(1)} %shard_map.125), channel_id=1, source_target_pairs={{0,4},{4,0},{1,5},{5,1},{2,6},{6,2},{3,7},{7,3},{8,12},{12,8},{9,1... | collective-permute-start | bytes 2359304 | tf_op jit(solution)/shard_map/ppermute | solution.py:309
  85.3 3.0 %shard_map.126 = f32[3,192,256]{2,1,0:T(8,128)S(1)} custom-call(s32[1]{0:T(128)} %bitcast.pos_ref, bf16[1536,256]{1,0:T(8,128)(2,1)S(1)} %copy-done.9, f32[1536,128]{1,0:T(8,128)S(1)} %copy-done.11, f32[16,32,128]{2,1,0:T(8,128)S(1)} %all-to-all-done.2.parts_ref, bf16[3072,256]{1,0:T(8,128)(2,1)S(1)} %maximum_dynamic-update-slice_fusion.refs_8_.q_ref), custom_call_target="tpu_custom_call" | custom-call | flops 1811939328 | bytes 1769472 | tf_op jit(solution)/shard_map/pallas_call | solution.py:413
  88.3 0.1 fusion
  88.4 1.2 collective-permute-start.17
  89.6 1.5 collective-permute-start.15
  91.1 1.5 collective-permute-start.16
  92.6 2.1 %shard_map.127 = f32[1,192,256]{2,1,0:T(8,128)S(1)} custom-call(s32[1]{0:T(128)} %bitcast.pos_ref, bf16[1536,256]{1,0:T(8,128)(2,1)S(1)} %copy-done.9, f32[1536,128]{1,0:T(8,128)S(1)} %copy-done.11, f32[16,32,128]{2,1,0:T(8,128)S(1)} %all-to-all-done.2.parts_ref, bf16[3072,256]{1,0:T(8,128)(2,1)S(1)} %maximum_dynamic-update-slice_fusion.refs_8_.q_ref), custom_call_target="tpu_custom_call" | custom-call | flops 603979776 | bytes 589824 | tf_op jit(solution)/shard_map/pallas_call | solution.py:413
  94.6 0.7 fusion.2.refs_0_
  95.4 0.5 collective-permute-done.15.refs_1_
  95.9 5.4 %collective-permute-done.16.refs_2_ = f32[192,256]{1,0:T(8,128)S(1)} collective-permute-done((f32[192,256]{1,0:T(8,128)S(1)}, f32[192,256]{1,0:T(8,128)S(1)}, u32[]{:S(2)}, u32[]{:S(2)}) %collective-permute-start.16) | collective-permute-done | bytes 196640 | tf_op jit(solution)/shard_map/ppermute | solution.py:309
  101.3 0.7 copy-done.19
  102.0 1.1 copy-done
  103.1 2.9 %shard_map.128 = bf16[16,2,4,40,128]{4,3,2,1,0:T(8,128)(2,1)} custom-call(f32[192,256]{1,0:T(8,128)} %fusion.2.refs_0_, f32[192,256]{1,0:T(8,128)} %copy-done.18, f32[192,256]{1,0:T(8,128)} %copy-done.19, f32[192,256]{1,0:T(8,128)} %collective-permute-done.17.refs_3_, bf16[192,256]{1,0:T(8,128)(2,1)} %get-tuple-element.33.refs_4_, ...), custom_call_target="tpu_custom_call" | custom-call | tf_op jit(solution)/shard_map/pallas_call | solution.py:444
  106.0 9.7 %all-to-all-start.4 = ((bf16[128,40,128]{2,1,0:T(8,128)(2,1)}), bf16[128,40,128]{2,1,0:T(8,128)(2,1)S(1)}, u32[]{:S(2)}, u32[]{:S(2)}) async-start(bf16[128,40,128]{2,1,0:T(8,128)(2,1)} %bitcast.42), calls=%async_computation.4 | async-start | bytes 2621440 | tf_op jit(solution)/shard_map/all_to_all | solution.py:304
  115.7 0.9 copy-done.12
  116.6 1.4 shard_map.130.active_ref
  118.0 1.3 copy-done.7
  119.4 0.1 constant_dynamic-slice_fusion
  119.5 1.3 shard_map.129
  120.8 17.3 %all-to-all-done.4.got_ref = bf16[128,40,128]{2,1,0:T(8,128)(2,1)S(1)} async-done(((bf16[128,40,128]{2,1,0:T(8,128)(2,1)}), bf16[128,40,128]{2,1,0:T(8,128)(2,1)S(1)}, u32[]{:S(2)}, u32[]{:S(2)}) %all-to-all-start.4) | async-done | bytes 1310752 | tf_op jit(solution)/shard_map/all_to_all | solution.py:304
  138.1 1.1 shard_map.132
  139.2 3.8 %all-to-all-start.5 = ((bf16[128,16,128]{2,1,0:T(8,128)(2,1)}), bf16[128,16,128]{2,1,0:T(8,128)(2,1)S(1)}, u32[]{:S(2)}, u32[]{:S(2)}) async-start(bf16[128,16,128]{2,1,0:T(8,128)(2,1)} %shard_map.132), calls=%async_computation.5 | async-start | bytes 1048576 | tf_op jit(solution)/shard_map/all_to_all | solution.py:304
  143.0 0.1 convert_element_type.38
  143.2 0.7 convert_element_type.40.ids_ref
  143.9 11.2 %shard_map.131 = (f32[2048,256]{1,0:T(8,128)}, f32[2048,256]{1,0:T(8,128)}) custom-call(s32[1,2048]{1,0:T(1,128)} %convert_element_type.40.ids_ref, bf16[128,40,128]{2,1,0:T(8,128)(2,1)} %copy-done.4, f32[2048,256]{1,0:T(8,128)} %table_ref.3, f32[2048,256]{1,0:T(8,128)} %accum_ref.1, bf16[2048,512]{1,0:T(8,128)(2,1)} %copy-done.7, ...), custom_call_target="tpu_custom_call" | custom-call | flops 4294967296 | bytes 8388608 | tf_op jit(solution)/shard_map/pallas_call | solution.py:483
  155.1 2.0 %all-to-all-done.5 = bf16[128,16,128]{2,1,0:T(8,128)(2,1)S(1)} async-done(((bf16[128,16,128]{2,1,0:T(8,128)(2,1)}), bf16[128,16,128]{2,1,0:T(8,128)(2,1)S(1)}, u32[]{:S(2)}, u32[]{:S(2)}) %all-to-all-start.5) | async-done | bytes 524320 | tf_op jit(solution)/shard_map/all_to_all | solution.py:304
  157.1 1.1 fusion.6
  (71 shorter events, 0.6 us)
Async XLA Ops:
  2.3 15.5 %all-to-all-start = ((s32[32,1,128]{2,1,0:T(1,128)}), s32[32,1,128]{2,1,0:T(1,128)S(1)}, u32[]{:S(2)}, u32[]{:S(2)}) async-start(s32[32,1,128]{2,1,0:T(1,128)} %bitcast.41), calls=%async_computation | async-start | bytes 32768 | tf_op jit(solution)/shard_map/all_to_all | solution.py:304
  10.9 0.9 copy-start.14
  11.8 0.7 copy-start.17
  12.5 3.9 %copy-start.20 = (bf16[192]{0:T(256)(128)(2,1)S(1)}, bf16[192]{0:T(256)(128)(2,1)}, u32[]{:S(2)}) copy-start(bf16[192]{0:T(256)(128)(2,1)} %param.11) | copy-start | bytes 1156
  12.5 5.4 %copy-start.2 = (f32[2048,256]{1,0:T(8,128)S(1)}, f32[2048,256]{1,0:T(8,128)}, u32[]{:S(2)}) copy-start(f32[2048,256]{1,0:T(8,128)} %table_ref.3) | copy-start | bytes 6291460
  12.5 14.7 %copy-start.15 = (bf16[192,256]{1,0:T(8,128)(2,1)S(1)}, bf16[192,256]{1,0:T(8,128)(2,1)}, u32[]{:S(2)}) copy-start(bf16[192,256]{1,0:T(8,128)(2,1)} %q_ref.1) | copy-start | bytes 294916
  12.5 14.6 %collective-permute-start.7 = (bf16[192,256]{1,0:T(8,128)(2,1)S(1)}, bf16[192,256]{1,0:T(8,128)(2,1)S(1)}, u32[]{:S(2)}, u32[]{:S(2)}) collective-permute-start(bf16[192,256]{1,0:T(8,128)(2,1)S(1)} %shard_map.121), channel_id=1, source_target_pairs={{0,96},{32,0},{64,32},{96,64},{1,97},{33,1},{65,33},{97,65},{2,98}... | collective-permute-start | bytes 294920 | tf_op jit(solution)/shard_map/ppermute | solution.py:309
  15.2 11.9 %collective-permute-start.8 = (bf16[192,256]{1,0:T(8,128)(2,1)S(1)}, bf16[192,256]{1,0:T(8,128)(2,1)S(1)}, u32[]{:S(2)}, u32[]{:S(2)}) collective-permute-start(bf16[192,256]{1,0:T(8,128)(2,1)S(1)} %shard_map.121), channel_id=1, source_target_pairs={{0,64},{32,96},{64,0},{96,32},{1,65},{33,97},{65,1},{97,33},{2,66}... | collective-permute-start | bytes 294920 | tf_op jit(solution)/shard_map/ppermute | solution.py:309
  15.8 11.4 %collective-permute-start.9 = (bf16[192,256]{1,0:T(8,128)(2,1)S(1)}, bf16[192,256]{1,0:T(8,128)(2,1)S(1)}, u32[]{:S(2)}, u32[]{:S(2)}) collective-permute-start(bf16[192,256]{1,0:T(8,128)(2,1)S(1)} %shard_map.121), channel_id=1, source_target_pairs={{0,32},{32,64},{64,96},{96,0},{1,33},{33,65},{65,97},{97,1},{2,34}... | collective-permute-start | bytes 294920 | tf_op jit(solution)/shard_map/ppermute | solution.py:309
  20.4 15.6 %all-to-all-start.1 = ((bf16[32,12,256]{2,1,0:T(8,128)(2,1)}), bf16[32,12,256]{2,1,0:T(8,128)(2,1)S(1)}, u32[]{:S(2)}, u32[]{:S(2)}) async-start(bf16[32,12,256]{2,1,0:T(8,128)(2,1)} %convert_element_type.34), calls=%async_computation.1 | async-start | bytes 524288 | tf_op jit(solution)/shard_map/all_to_all | solution.py:304
  27.2 16.2 %collective-permute-start.10 = (bf16[768,256]{1,0:T(8,128)(2,1)S(1)}, bf16[768,256]{1,0:T(8,128)(2,1)S(1)}, u32[]{:S(2)}, u32[]{:S(2)}) collective-permute-start(bf16[768,256]{1,0:T(8,128)(2,1)S(1)} %shard_map.122), channel_id=1, source_target_pairs={{0,3},{1,0},{2,1},{3,2},{4,7},{5,4},{6,5},{7,6},{8,11},{9,8},{10,9... | collective-permute-start | bytes 1179656 | tf_op jit(solution)/shard_map/ppermute | solution.py:309
  31.1 11.4 %collective-permute-start.11 = (bf16[768,256]{1,0:T(8,128)(2,1)S(1)}, bf16[768,256]{1,0:T(8,128)(2,1)S(1)}, u32[]{:S(2)}, u32[]{:S(2)}) collective-permute-start(bf16[768,256]{1,0:T(8,128)(2,1)S(1)} %shard_map.122), channel_id=1, source_target_pairs={{0,1},{1,2},{2,3},{3,0},{4,5},{5,6},{6,7},{7,4},{8,9},{9,10},{10,1... | collective-permute-start | bytes 1179656 | tf_op jit(solution)/shard_map/ppermute | solution.py:309
  39.1 6.7 %copy-start.13 = (bf16[208,256]{1,0:T(8,128)(2,1)S(1)}, bf16[208,256]{1,0:T(8,128)(2,1)}, u32[]{:S(2)}) copy-start(bf16[208,256]{1,0:T(8,128)(2,1)} %get-tuple-element.25.refs_0_.pay_ref) | copy-start | bytes 319492
  39.1 6.7 %collective-permute-start = (bf16[208,256]{1,0:T(8,128)(2,1)}, bf16[208,256]{1,0:T(8,128)(2,1)S(1)}, u32[]{:S(2)}, u32[]{:S(2)}) collective-permute-start(bf16[208,256]{1,0:T(8,128)(2,1)} %get-tuple-element.25.refs_0_.pay_ref), channel_id=1, source_target_pairs={{0,8},{8,16},{16,24},{24,0},{1,9},{9,17},{17,25},{25,1},{2,10},{10... | collective-permute-start | bytes 319496 | tf_op jit(solution)/shard_map/ppermute | solution.py:309
  39.3 8.9 %collective-permute-start.1 = (bf16[208,256]{1,0:T(8,128)(2,1)}, bf16[208,256]{1,0:T(8,128)(2,1)S(1)}, u32[]{:S(2)}, u32[]{:S(2)}) collective-permute-start(bf16[208,256]{1,0:T(8,128)(2,1)} %get-tuple-element.25.refs_0_.pay_ref), channel_id=1, source_target_pairs={{0,16},{8,24},{16,0},{24,8},{1,17},{9,25},{17,1},{25,9},{2,18},{10... | collective-permute-start | bytes 319496 | tf_op jit(solution)/shard_map/ppermute | solution.py:309
  41.2 7.0 %collective-permute-start.2 = (bf16[208,256]{1,0:T(8,128)(2,1)}, bf16[208,256]{1,0:T(8,128)(2,1)S(1)}, u32[]{:S(2)}, u32[]{:S(2)}) collective-permute-start(bf16[208,256]{1,0:T(8,128)(2,1)} %get-tuple-element.25.refs_0_.pay_ref), channel_id=1, source_target_pairs={{0,24},{8,0},{16,8},{24,16},{1,25},{9,1},{17,9},{25,17},{2,26},{10... | collective-permute-start | bytes 319496 | tf_op jit(solution)/shard_map/ppermute | solution.py:309
  42.5 7.0 %collective-permute-start.13 = (bf16[384,256]{1,0:T(8,128)(2,1)S(1)}, bf16[384,256]{1,0:T(8,128)(2,1)S(1)}, u32[]{:S(2)}, u32[]{:S(2)}) collective-permute-start(bf16[384,256]{1,0:T(8,128)(2,1)S(1)} %slice.64), channel_id=1, source_target_pairs={{0,1},{1,2},{2,3},{3,0},{4,5},{5,6},{6,7},{7,4},{8,9},{9,10},{10,1... | collective-permute-start | bytes 589832 | tf_op jit(solution)/shard_map/ppermute | solution.py:309
  43.5 8.0 %collective-permute-start.12 = (bf16[384,256]{1,0:T(8,128)(2,1)S(1)}, bf16[384,256]{1,0:T(8,128)(2,1)S(1)}, u32[]{:S(2)}, u32[]{:S(2)}) collective-permute-start(bf16[384,256]{1,0:T(8,128)(2,1)S(1)} %slice.63), channel_id=1, source_target_pairs={{0,3},{1,0},{2,1},{3,2},{4,7},{5,4},{6,5},{7,6},{8,11},{9,8},{10,9... | collective-permute-start | bytes 589832 | tf_op jit(solution)/shard_map/ppermute | solution.py:309
  45.8 5.7 %collective-permute-start.3 = (bf16[208,256]{1,0:T(8,128)(2,1)S(1)}, bf16[208,256]{1,0:T(8,128)(2,1)S(1)}, u32[]{:S(2)}, u32[]{:S(2)}) collective-permute-start(bf16[208,256]{1,0:T(8,128)(2,1)S(1)} %copy-done.13), channel_id=1, source_target_pairs={{0,4},{4,0},{1,5},{5,1},{2,6},{6,2},{3,7},{7,3},{8,12},{12,8},{9,1... | collective-permute-start | bytes 319496 | tf_op jit(solution)/shard_map/ppermute | solution.py:309
  48.2 3.3 %collective-permute-start.4 = (bf16[208,256]{1,0:T(8,128)(2,1)S(1)}, bf16[208,256]{1,0:T(8,128)(2,1)S(1)}, u32[]{:S(2)}, u32[]{:S(2)}) collective-permute-start(bf16[208,256]{1,0:T(8,128)(2,1)S(1)} %collective-permute-done.refs_1_), channel_id=1, source_target_pairs={{0,4},{4,0},{1,5},{5,1},{2,6},{6,2},{3,7},{7,3},{8,12},{12,8},{9,1... | collective-permute-start | bytes 319496 | tf_op jit(solution)/shard_map/ppermute | solution.py:309
  48.2 3.3 %collective-permute-start.5 = (bf16[208,256]{1,0:T(8,128)(2,1)S(1)}, bf16[208,256]{1,0:T(8,128)(2,1)S(1)}, u32[]{:S(2)}, u32[]{:S(2)}) collective-permute-start(bf16[208,256]{1,0:T(8,128)(2,1)S(1)} %collective-permute-done.1.refs_2_), channel_id=1, source_target_pairs={{0,4},{4,0},{1,5},{5,1},{2,6},{6,2},{3,7},{7,3},{8,12},{12,8},{9,1... | collective-permute-start | bytes 319496 | tf_op jit(solution)/shard_map/ppermute | solution.py:309
  49.4 3.0 %collective-permute-start.6 = (bf16[208,256]{1,0:T(8,128)(2,1)S(1)}, bf16[208,256]{1,0:T(8,128)(2,1)S(1)}, u32[]{:S(2)}, u32[]{:S(2)}) collective-permute-start(bf16[208,256]{1,0:T(8,128)(2,1)S(1)} %collective-permute-done.2.refs_3_), channel_id=1, source_target_pairs={{0,4},{4,0},{1,5},{5,1},{2,6},{6,2},{3,7},{7,3},{8,12},{12,8},{9,1... | collective-permute-start | bytes 319496 | tf_op jit(solution)/shard_map/ppermute | solution.py:309
  58.5 11.7 %copy-start.8 = (bf16[1536,256]{1,0:T(8,128)(2,1)}, bf16[1536,256]{1,0:T(8,128)(2,1)S(1)}, u32[]{:S(2)}) copy-start(bf16[1536,256]{1,0:T(8,128)(2,1)S(1)} %get-tuple-element.26.vec) | copy-start | bytes 2359300
  58.5 11.7 %copy-start.10 = (f32[1536,128]{1,0:T(8,128)}, f32[1536,128]{1,0:T(8,128)S(1)}, u32[]{:S(2)}) copy-start(f32[1536,128]{1,0:T(8,128)S(1)} %get-tuple-element.27.freq) | copy-start | bytes 2359300
  58.5 11.7 %all-to-all-start.2 = ((f32[16,32,128]{2,1,0:T(8,128)}), f32[16,32,128]{2,1,0:T(8,128)S(1)}, u32[]{:S(2)}, u32[]{:S(2)}) async-start(f32[16,32,128]{2,1,0:T(8,128)} %get-tuple-element.28), calls=%async_computation.2 | async-start | bytes 524288 | tf_op jit(solution)/shard_map/all_to_all | solution.py:304
  70.3 22.3 %copy-start.5 = (f32[16,32,128]{2,1,0:T(8,128)}, f32[16,32,128]{2,1,0:T(8,128)S(1)}, u32[]{:S(2)}) copy-start(f32[16,32,128]{2,1,0:T(8,128)S(1)} %all-to-all-done.2.parts_ref) | copy-start | bytes 786436
  70.3 31.7 %all-to-all-start.3 = ((bf16[16,192,256]{2,1,0:T(8,128)(2,1)}), bf16[16,192,256]{2,1,0:T(8,128)(2,1)S(1)}, u32[]{:S(2)}, u32[]{:S(2)}) async-start(bf16[16,192,256]{2,1,0:T(8,128)(2,1)} %bitcast.44), calls=%async_computation.3 | async-start | bytes 3145728 | tf_op jit(solution)/shard_map/all_to_all | solution.py:304
  76.9 1.1 copy-start.9
  78.1 1.1 copy-start.11
  82.8 5.5 %collective-permute-start.14 = (f32[4,192,256]{2,1,0:T(8,128)S(1)}, f32[4,192,256]{2,1,0:T(8,128)S(1)}, u32[]{:S(2)}, u32[]{:S(2)}) collective-permute-start(f32[4,192,256]{2,1,0:T(8,128)S(1)} %shard_map.125), channel_id=1, source_target_pairs={{0,4},{4,0},{1,5},{5,1},{2,6},{6,2},{3,7},{7,3},{8,12},{12,8},{9,1... | collective-permute-start | bytes 2359304 | tf_op jit(solution)/shard_map/ppermute | solution.py:309
  88.4 13.6 %collective-permute-start.17 = (f32[192,256]{1,0:T(8,128)S(1)}, f32[192,256]{1,0:T(8,128)}, u32[]{:S(2)}, u32[]{:S(2)}) collective-permute-start(f32[192,256]{1,0:T(8,128)S(1)} %get-tuple-element.43), channel_id=1, source_target_pairs={{0,8},{8,16},{16,24},{24,0},{1,9},{9,17},{17,25},{25,1},{2,10},{10... | collective-permute-start | bytes 589832 | tf_op jit(solution)/shard_map/ppermute | solution.py:309
  89.6 6.3 %collective-permute-start.15 = (f32[192,256]{1,0:T(8,128)S(1)}, f32[192,256]{1,0:T(8,128)S(1)}, u32[]{:S(2)}, u32[]{:S(2)}) collective-permute-start(f32[192,256]{1,0:T(8,128)S(1)} %get-tuple-element.42), channel_id=1, source_target_pairs={{0,24},{8,0},{16,8},{24,16},{1,25},{9,1},{17,9},{25,17},{2,26},{10... | collective-permute-start | bytes 589832 | tf_op jit(solution)/shard_map/ppermute | solution.py:309
  91.1 10.2 %collective-permute-start.16 = (f32[192,256]{1,0:T(8,128)S(1)}, f32[192,256]{1,0:T(8,128)S(1)}, u32[]{:S(2)}, u32[]{:S(2)}) collective-permute-start(f32[192,256]{1,0:T(8,128)S(1)} %get-tuple-element.41), channel_id=1, source_target_pairs={{0,16},{8,24},{16,0},{24,8},{1,17},{9,25},{17,1},{25,9},{2,18},{10... | collective-permute-start | bytes 589832 | tf_op jit(solution)/shard_map/ppermute | solution.py:309
  95.9 5.4 %copy-start.18 = (f32[192,256]{1,0:T(8,128)}, f32[192,256]{1,0:T(8,128)S(1)}, u32[]{:S(2)}) copy-start(f32[192,256]{1,0:T(8,128)S(1)} %collective-permute-done.15.refs_1_) | copy-start | bytes 589828
  101.3 0.7 copy-start.19
  102.0 1.1 copy-start
  106.0 9.7 %copy-start.3 = (f32[2048,256]{1,0:T(8,128)S(1)}, f32[2048,256]{1,0:T(8,128)}, u32[]{:S(2)}) copy-start(f32[2048,256]{1,0:T(8,128)} %table_ref.3) | copy-start | bytes 6291460
  106.0 32.1 %all-to-all-start.4 = ((bf16[128,40,128]{2,1,0:T(8,128)(2,1)}), bf16[128,40,128]{2,1,0:T(8,128)(2,1)S(1)}, u32[]{:S(2)}, u32[]{:S(2)}) async-start(bf16[128,40,128]{2,1,0:T(8,128)(2,1)} %bitcast.42), calls=%async_computation.4 | async-start | bytes 2621440 | tf_op jit(solution)/shard_map/all_to_all | solution.py:304
  115.7 1.0 copy-start.12
  116.6 2.7 %slice-start = ((f32[16,32,128]{2,1,0:T(8,128)}), f32[16,24,128]{2,1,0:T(8,128)S(1)}, s32[]{:S(2)}) async-start(f32[16,32,128]{2,1,0:T(8,128)} %copy-done.5), calls=%async_computation.6 | async-start | bytes 393216 | tf_op jit(solution)/shard_map/slice | solution.py:453
  116.6 2.8 %copy-start.1 = (bf16[16,192,256]{2,1,0:T(8,128)(2,1)S(1)}, bf16[16,192,256]{2,1,0:T(8,128)(2,1)}, u32[]{:S(2)}) copy-start(bf16[16,192,256]{2,1,0:T(8,128)(2,1)} %copy-done) | copy-start | bytes 4718596
  116.6 2.9 %copy-start.16 = (bf16[192,256]{1,0:T(8,128)(2,1)S(1)}, bf16[192,256]{1,0:T(8,128)(2,1)}, u32[]{:S(2)}) copy-start(bf16[192,256]{1,0:T(8,128)(2,1)} %q_ref.1) | copy-start | bytes 294916
  118.0 1.3 copy-start.7
  120.8 22.2 %copy-start.6 = (f32[16,32,128]{2,1,0:T(8,128)S(1)}, f32[16,32,128]{2,1,0:T(8,128)}, u32[]{:S(2)}) copy-start(f32[16,32,128]{2,1,0:T(8,128)} %copy-done.5) | copy-start | bytes 786436
  138.1 5.1 %copy-start.4 = (bf16[128,40,128]{2,1,0:T(8,128)(2,1)}, bf16[128,40,128]{2,1,0:T(8,128)(2,1)S(1)}, u32[]{:S(2)}) copy-start(bf16[128,40,128]{2,1,0:T(8,128)(2,1)S(1)} %all-to-all-done.4.got_ref) | copy-start | bytes 3932164
  139.2 17.9 %all-to-all-start.5 = ((bf16[128,16,128]{2,1,0:T(8,128)(2,1)}), bf16[128,16,128]{2,1,0:T(8,128)(2,1)S(1)}, u32[]{:S(2)}, u32[]{:S(2)}) async-start(bf16[128,16,128]{2,1,0:T(8,128)(2,1)} %shard_map.132), calls=%async_computation.5 | async-start | bytes 1048576 | tf_op jit(solution)/shard_map/all_to_all | solution.py:304

commit v6 on v5

--- a/solution.py
+++ b/solution.py
@@ -11,7 +11,6 @@
 H = 512
 PAIRS = 192
 ROWS = 2048
-CAP = 12
 SLOT = 16
 OWNERS = 32
 NA = 16
@@ -87,9 +86,8 @@
     req_ref[...] = jnp.where(hi < 0.0, -1, (hi * 256.0 + lo).astype(i32))
     place = jnp.where(owner < 0, -1, owner * SLOT + slot)
     place_ref[...] = place
-    flat = jnp.where(owner < 0, -1, owner * CAP + slot).astype(f32)
-    col = column(flat, PAIRS).astype(i32)
-    pick_ref[...] = (col == iota((PAIRS, OWNERS * CAP), 1)).astype(f32).astype(bf16)
+    col = column(place.astype(f32), PAIRS).astype(i32)
+    pick_ref[...] = (col == iota((PAIRS, OWNERS * SLOT), 1)).astype(f32).astype(bf16)
 
 
 COST = 8 << 30
@@ -121,12 +119,16 @@
 VB = 384
 
 
-def load_vecs(vec_refs, vec, freq):
+def load_vecs(vec_refs, rows):
     for b in range(len(vec_refs)):
         at = slice(b * PAIRS, (b + 1) * PAIRS)
         line = vec_refs[b][PAIRS : PAIRS + 16, :].astype(f32)[0:1, :]
-        freq[at, :] = jnp.broadcast_to(column(line, PAIRS), (PAIRS, 128))
-        vec[at, :] = vec_refs[b][0:PAIRS, :]
+        rows[at, E : E + 128] = jnp.broadcast_to(column(line, PAIRS), (PAIRS, 128)).astype(bf16)
+        rows[at, 0:E] = vec_refs[b][0:PAIRS, :]
+
+
+def products(rows, at, q):
+    return mm(rows[at, 0:E], q, NT) - lanes(rows[at, E : E + 128].astype(f32), q.shape[0])
 
 
 def lanes(col, n=QB):
@@ -137,9 +139,9 @@
 
 
 def score_kernel(*refs):
-    vec_refs, (q_ref, ids_ref, lse_ref, part_ref, vec, freq, *scores) = refs[:NB], refs[NB:]
+    vec_refs, (q_ref, ids_ref, lse_ref, part_ref, rows, *scores) = refs[:NB], refs[NB:]
     lse_ref[:, LINES:SENT, :] = jnp.broadcast_to(ids_ref[...][None], (NA, 8, 128))
-    load_vecs(vec_refs, vec, freq)
+    load_vecs(vec_refs, rows)
     tops = []
     for j in range(QS // PB + 1):
         top, total = None, jnp.zeros((8, PB), f32)
@@ -148,7 +150,7 @@
         for b in range(0, VS, VB):
             at = slice(b, b + VB)
             if j < QS // PB:
-                s = mm(vec[at, :], q, NT) - lanes(freq[at, :], PB)
+                s = products(rows, at, q)
                 scores[j % 2][at, :] = s
                 t = jnp.max(s.reshape(VB // 8, 8, PB), axis=0)
                 top = t if top is None else jnp.maximum(top, t)
@@ -178,24 +180,24 @@
     return jnp.concatenate([rows_ref[(*index, pl.ds(at + i, 1), slice(None))] for i in range(n)], axis=1)
 
 
-def query_kernel(pos_ref, vec, freq, part_ref, q_ref, o_ref, turned, weight):
+def query_kernel(pos_ref, rows, part_ref, q_ref, o_ref, turned, weight):
     @pl.when(pl.program_id(0) == 0)
     def _():
         for k in range(0, VS, 256):
-            turned[:, k : k + 256] = vec[k : k + 256, :].astype(f32).T.astype(bf16)
+            turned[:, k : k + 256] = rows[k : k + 256, 0:E].astype(f32).T.astype(bf16)
 
     q = q_ref[...] * jnp.asarray(score_scale, bf16)
     norm = query_lanes(part_ref)
     for b in range(0, VS, VB):
         at = slice(b, b + VB)
-        p = jnp.exp(mm(vec[at, :], q, NT) - lanes(freq[at, :]) - norm)
+        p = jnp.exp(products(rows, at, q) - norm)
         if b == 0:
             p = jnp.concatenate([jnp.where(is_pair(pos_ref), 0.0, p[:PAIRS]), p[PAIRS:]], axis=0)
         weight[at, :] = p.astype(bf16)
     o_ref[...] = mm(turned[...], weight[...]).T.astype(bf16)
 
 
-def vec_kernel(first, n, pos_ref, vec, freq, parts_ref, q_ref, g_ref, lse, coef):
+def vec_kernel(first, n, pos_ref, rows, parts_ref, q_ref, g_ref, lse, coef):
     @pl.when(pl.program_id(0) == 0)
     def _():
         top = parts_ref[0]
@@ -213,7 +215,7 @@
     for b in range(0, n, 2):
         m = min(2, n - b) * PAIRS
         at = slice((first + b) * PAIRS, (first + b) * PAIRS + m)
-        p = jnp.exp(mm(vec[at, :], scaled, NT) - lanes(freq[at, :]) - norm)
+        p = jnp.exp(products(rows, at, scaled) - norm)
         if first == 0:
             p = jnp.where(is_pair(pos_ref), p - 1.0, p)
         coef[b * PAIRS : b * PAIRS + m, :] = p.astype(bf16)
@@ -329,7 +331,7 @@
         (
             sds((OWNERS, 128), i32),
             sds((1, 256), i32),
-            sds((PAIRS, OWNERS * CAP), bf16),
+            sds((PAIRS, OWNERS * SLOT), bf16),
         ),
         in_specs=whole(2),
         out_specs=tuple(whole(3)),
@@ -347,7 +349,7 @@
     blocks = [queries] + [shift(early, "x", 4 - k) for k in range(1, 4)]
     ids = asked[:, 0, :SLOT].astype(f32).reshape(OWNERS * SLOT // 128, 128)
     ids = jnp.pad(ids, ((0, 8 - OWNERS * SLOT // 128), (0, 0)))
-    wanted = jnp.maximum(asked[:, 0, :CAP].reshape(OWNERS * CAP), 0)
+    wanted = jnp.maximum(asked[:, 0, :SLOT].reshape(OWNERS * SLOT), 0)
     picked = table.at[wanted].get(mode="promise_in_bounds").astype(bf16)
     slab = call(
         slab_kernel,
@@ -363,7 +365,7 @@
     all_q = jnp.zeros((QS, E), bf16)
     for k, block in ((0, slab), (1, above), (3, below), (2, jnp.concatenate(far, axis=0))):
         all_q = lax.dynamic_update_slice(all_q, block, ((here_z + k) % 4 * QB, 0))
-    got = a2a(picked.reshape(OWNERS, CAP, E), SHARD).reshape(OWNERS * CAP, E)
+    got = a2a(picked.reshape(OWNERS, SLOT, E), SHARD).reshape(OWNERS * SLOT, E)
     freq_row = jnp.pad(log_freq.reshape(1, PAIRS), ((0, 15), (0, 256 - PAIRS)))
     emb, hid, pay = call(
         tower_kernel,
@@ -375,13 +377,13 @@
     vecs = [pay] + [shift(pay, "y", k) for k in range(1, 4)]
     vecs = vecs + [shift(v, "c", 1) for v in vecs]
 
-    sent_lse, part_lse, vec_all, freq_all = call(
+    sent_lse, part_lse, vec_rows = call(
         score_kernel,
-        (HBM((NA, SENT, 128), f32), sds((LINES, 128), f32), sds((VS, E), bf16), sds((VS, 128), f32)),
+        (HBM((NA, SENT, 128), f32), sds((LINES, 128), f32), sds((VS, E + 128), bf16)),
         cost=(2 * VS * QS * E, VS * QS * 2, VS * QS),
         limit=LIMIT,
         in_specs=whole(NB + 2),
-        out_specs=tuple(whole(4)),
+        out_specs=tuple(whole(3)),
         scratch_shapes=[pltpu.VMEM((VS, PB), f32)] * 2,
     )(*vecs, all_q, ids)
     all_lse = a2a(sent_lse, A)
@@ -395,8 +397,7 @@
             num_scalar_prefetch=1,
             grid=(QS // QB,),
             in_specs=[
-                const(VS, E),
-                const(VS, 128),
+                const(VS, E + 128),
                 const(LINES, 128),
                 pl.BlockSpec((QB, E), lambda i, pos: (i, 0)),
             ],
@@ -406,7 +407,7 @@
                 pltpu.VMEM((VS, QB), bf16),
             ],
         ),
-    )(here.reshape(1), vec_all, freq_all, part_lse, all_q)
+    )(here.reshape(1), vec_rows, part_lse, all_q)
 
     def vec_grads(first, n, wait):
         first_lse, _ = lax.optimization_barrier((all_lse, wait))
@@ -419,8 +420,7 @@
                 num_scalar_prefetch=1,
                 grid=(QS // QB,),
                 in_specs=[
-                    const(VS, E),
-                    const(VS, 128),
+                    const(VS, E + 128),
                     const(NA, SENT, 128),
                     pl.BlockSpec((QB, E), lambda i, pos: (i, 0)),
                 ],
@@ -430,7 +430,7 @@
                     pltpu.VMEM((n * PAIRS, QB), bf16),
                 ],
             ),
-        )(here.reshape(1), vec_all, freq_all, first_lse, all_q)
+        )(here.reshape(1), vec_rows, first_lse, all_q)
 
     o_got = a2a(o.reshape(NA, PAIRS, E), A)
 

time: 159 us -> 158 us (level)
    unnamed x43 -> x41, local copies, waits for them, and re-layouts: 8.04 us -> 7.76 us
  transfers between devices with their start and end apart: 24 -> 24, of which waited for: 9 -> 9; matrix products, arithmetic and copies ran while one was open for 4% -> 3% of each run, Pallas kernels for 21% -> 21%
where the time goes in v6:
time: 158 us; the launch traced here: 157 us
  starting transfers between devices  64.5 us (41%)
  Pallas kernels  44.5 us (28%)
  waiting for transfers between devices  33 us (21%)
  local copies, waits for them, and re-layouts  13 us (8%)
    all_to_all x6, starting transfers between devices, a2a(): return lax.all_to_all(x, axes, split_axis=0, concat_axis=0, tiled=True)  39.3 us
    ppermute x18, starting transfers between devices, shift(): return lax.ppermute(x, axis, [(i, (i + k) % n) for i in range(n)])  25.3 us
    all_to_all x6, waiting for transfers between devices, a2a(): return lax.all_to_all(x, axes, split_axis=0, concat_axis=0, tiled=True)  24.9 us
    pallas_call x1, Pallas kernels, local(): call(update_kernel, (sds((ROWS, E), f32), sds((ROWS, E), f32)), cost=(4 *...  11.2 us
    pallas_call x3, Pallas kernels, vec_grads(): call(functools.partial(vec_kernel, first, n), sds((n, PAIRS, E), f32), co...  8.7 us
    ppermute x18, waiting for transfers between devices, shift(): return lax.ppermute(x, axis, [(i, (i + k) % n) for i in range(n)])  8.16 us
    pallas_call x1, Pallas kernels, local(): call(query_kernel, HBM((QS, E), bf16), cost=(4 * VS * QS * E, VS * QS, VS...  7.8 us
    unnamed x41, local copies, waits for them, and re-layouts  7.76 us
  transfers between devices with their start and end apart: 24, of which 9 were waited for; matrix products, arithmetic and copies ran while one was open for 3% of the time, Pallas kernels for 21%

profile of v6, /device:TPU:1, one launch (start us, length us, event | category | flops | bytes accessed | tf_op | source)
XLA Modules:
  0.0 157.0 jit_solution(2048336635637210746)
XLA Ops:
  0.6 1.7 %shard_map.119 = (s32[32,128]{1,0:T(8,128)}, s32[1,256]{1,0:T(1,128)}, bf16[192,512]{1,0:T(8,128)(2,1)}) custom-call(s32[1,192]{1,0:T(1,128)} %bitcast.52, s32[1,192]{1,0:T(1,128)} %bitcast.53), custom_call_target="tpu_custom_call" | custom-call | tf_op jit(solution)/shard_map/pallas_call | solution.py:329
  2.3 8.6 %all-to-all-start = ((s32[32,1,128]{2,1,0:T(1,128)}), s32[32,1,128]{2,1,0:T(1,128)S(1)}, u32[]{:S(2)}, u32[]{:S(2)}) async-start(s32[32,1,128]{2,1,0:T(1,128)} %bitcast.43), calls=%async_computation | async-start | bytes 32768 | tf_op jit(solution)/shard_map/all_to_all | solution.py:306
  10.9 0.9 copy-done.12
  11.8 0.7 copy-done.15
  12.5 2.7 %collective-permute-start.7 = (bf16[192,256]{1,0:T(8,128)(2,1)S(1)}, bf16[192,256]{1,0:T(8,128)(2,1)S(1)}, u32[]{:S(2)}, u32[]{:S(2)}) collective-permute-start(bf16[192,256]{1,0:T(8,128)(2,1)S(1)} %shard_map.121), channel_id=1, source_target_pairs={{0,96},{32,0},{64,32},{96,64},{1,97},{33,1},{65,33},{97,65},{2,98}... | collective-permute-start | bytes 294920 | tf_op jit(solution)/shard_map/ppermute | solution.py:311
  15.2 0.5 collective-permute-start.8
  15.8 0.6 collective-permute-start.9
  16.4 0.6 pad.12.freq_ref
  17.0 0.8 all-to-all-done
  17.8 0.1 maximum_reduce_fusion
  17.8 0.1 reshape.111
  17.9 2.2 %gather_fusion = bf16[512,256]{1,0:T(8,128)(2,1)} fusion(f32[2048,256]{1,0:T(8,128)S(1)} %copy-done.2, s32[1024]{0:T(1024)S(1)} %pad_clamp_fusion), kind=kCustom, calls=%fused_computation | custom fusion | bytes 526336 | tf_op jit(solution)/shard_map/gather | solution.py:353
  20.1 6.6 %all-to-all-start.1 = ((bf16[32,16,256]{2,1,0:T(8,128)(2,1)}), bf16[32,16,256]{2,1,0:T(8,128)(2,1)S(1)}, u32[]{:S(2)}, u32[]{:S(2)}) async-start(bf16[32,16,256]{2,1,0:T(8,128)(2,1)} %bitcast.5), calls=%async_computation.1 | async-start | bytes 524288 | tf_op jit(solution)/shard_map/all_to_all | solution.py:306
  26.8 0.1 convert_element_type.36
  27.0 3.8 %collective-permute-start.10 = (bf16[768,256]{1,0:T(8,128)(2,1)S(1)}, bf16[768,256]{1,0:T(8,128)(2,1)S(1)}, u32[]{:S(2)}, u32[]{:S(2)}) collective-permute-start(bf16[768,256]{1,0:T(8,128)(2,1)S(1)} %shard_map.122), channel_id=1, source_target_pairs={{0,3},{1,0},{2,1},{3,2},{4,7},{5,4},{6,5},{7,6},{8,11},{9,8},{10,9... | collective-permute-start | bytes 1179656 | tf_op jit(solution)/shard_map/ppermute | solution.py:311
  30.8 0.1 broadcast_in_dim.4
  31.0 4.8 %all-to-all-done.1 = bf16[32,16,256]{2,1,0:T(8,128)(2,1)S(1)} async-done(((bf16[32,16,256]{2,1,0:T(8,128)(2,1)}), bf16[32,16,256]{2,1,0:T(8,128)(2,1)S(1)}, u32[]{:S(2)}, u32[]{:S(2)}) %all-to-all-start.1) | async-done | bytes 262176 | tf_op jit(solution)/shard_map/all_to_all | solution.py:306
  35.7 0.7 copy-done.16
  36.4 2.4 %shard_map.120 = (bf16[192,256]{1,0:T(8,128)(2,1)}, bf16[192,512]{1,0:T(8,128)(2,1)}, bf16[208,256]{1,0:T(8,128)(2,1)}) custom-call(bf16[512,256]{1,0:T(8,128)(2,1)} %bitcast.49, bf16[192,512]{1,0:T(8,128)(2,1)} %get-tuple-element.23.pick_ref, bf16[256,512]{1,0:T(8,128)(2,1)} %w_in_ref.5, bf16[512,256]{1,0:T(8,128)(2,1)} %w_out_ref.3, ...), custom_call_target="tpu_custom_call" | custom-call | flops 25769803776 | bytes 1048576 | tf_op jit(solution)/shard_map/pallas_call | solution.py:370
  38.8 0.2 collective-permute-start
  39.0 1.9 %collective-permute-start.1 = (bf16[208,256]{1,0:T(8,128)(2,1)}, bf16[208,256]{1,0:T(8,128)(2,1)S(1)}, u32[]{:S(2)}, u32[]{:S(2)}) collective-permute-start(bf16[208,256]{1,0:T(8,128)(2,1)} %get-tuple-element.24.refs_0_.pay_ref), channel_id=1, source_target_pairs={{0,16},{8,24},{16,0},{24,8},{1,17},{9,25},{17,1},{25,9},{2,18},{10... | collective-permute-start | bytes 319496 | tf_op jit(solution)/shard_map/ppermute | solution.py:311
  41.0 0.5 collective-permute-start.2
  41.5 0.7 collective-permute-done.11
  42.2 1.0 collective-permute-start.13
  43.2 2.2 %collective-permute-start.12 = (bf16[384,256]{1,0:T(8,128)(2,1)S(1)}, bf16[384,256]{1,0:T(8,128)(2,1)S(1)}, u32[]{:S(2)}, u32[]{:S(2)}) collective-permute-start(bf16[384,256]{1,0:T(8,128)(2,1)S(1)} %slice.60), channel_id=1, source_target_pairs={{0,3},{1,0},{2,1},{3,2},{4,7},{5,4},{6,5},{7,6},{8,11},{9,8},{10,9... | collective-permute-start | bytes 589832 | tf_op jit(solution)/shard_map/ppermute | solution.py:311
  45.5 2.4 %collective-permute-start.3 = (bf16[208,256]{1,0:T(8,128)(2,1)S(1)}, bf16[208,256]{1,0:T(8,128)(2,1)S(1)}, u32[]{:S(2)}, u32[]{:S(2)}) collective-permute-start(bf16[208,256]{1,0:T(8,128)(2,1)S(1)} %copy-done.11), channel_id=1, source_target_pairs={{0,4},{4,0},{1,5},{5,1},{2,6},{6,2},{3,7},{7,3},{8,12},{12,8},{9,1... | collective-permute-start | bytes 319496 | tf_op jit(solution)/shard_map/ppermute | solution.py:311
  47.9 0.1 collective-permute-start.4
  48.0 0.5 collective-permute-start.5
  48.5 0.6 collective-permute-done.13
  49.2 2.0 %collective-permute-start.6 = (bf16[208,256]{1,0:T(8,128)(2,1)S(1)}, bf16[208,256]{1,0:T(8,128)(2,1)S(1)}, u32[]{:S(2)}, u32[]{:S(2)}) collective-permute-start(bf16[208,256]{1,0:T(8,128)(2,1)S(1)} %collective-permute-done.2.refs_3_), channel_id=1, source_target_pairs={{0,4},{4,0},{1,5},{5,1},{2,6},{6,2},{3,7},{7,3},{8,12},{12,8},{9,1... | collective-permute-start | bytes 319496 | tf_op jit(solution)/shard_map/ppermute | solution.py:311
  51.3 0.9 collective-permute-done.6.refs_7_
  52.1 6.1 %shard_map.123 = (f32[16,32,128]{2,1,0:T(8,128)}, f32[24,128]{1,0:T(8,128)S(1)}, bf16[1536,384]{1,0:T(8,128)(2,1)S(1)}) custom-call(bf16[208,256]{1,0:T(8,128)(2,1)S(1)} %copy-done.11, bf16[208,256]{1,0:T(8,128)(2,1)S(1)} %collective-permute-done.refs_1_, bf16[208,256]{1,0:T(8,128)(2,1)S(1)} %collective-permute-done.1.refs_2_, ...), custom_call_target="tpu_custom_call" | custom-call | flops 2415919104 | bytes 9437184 | tf_op jit(solution)/shard_map/pallas_call | solution.py:380
  58.3 3.9 %all-to-all-start.2 = ((f32[16,32,128]{2,1,0:T(8,128)}), f32[16,32,128]{2,1,0:T(8,128)S(1)}, u32[]{:S(2)}, u32[]{:S(2)}) async-start(f32[16,32,128]{2,1,0:T(8,128)} %get-tuple-element.26), calls=%async_computation.2 | async-start | bytes 524288 | tf_op jit(solution)/shard_map/all_to_all | solution.py:306
  62.2 7.8 %shard_map.124 = bf16[3072,256]{1,0:T(8,128)(2,1)} custom-call(s32[1]{0:T(128)} %bitcast.pos_ref, bf16[1536,384]{1,0:T(8,128)(2,1)S(1)} %get-tuple-element.25.rows, f32[24,128]{1,0:T(8,128)S(1)} %get-tuple-element.27.part_ref, bf16[3072,256]{1,0:T(8,128)(2,1)S(1)} %maximum_dynamic-update-slice_fusion.refs_8_.q_ref), custom_call_target="tpu_custom_call" | custom-call | flops 4831838208 | bytes 4718592 | tf_op jit(solution)/shard_map/pallas_call | solution.py:391
  70.0 6.7 %all-to-all-start.3 = ((bf16[16,192,256]{2,1,0:T(8,128)(2,1)}), bf16[16,192,256]{2,1,0:T(8,128)(2,1)S(1)}, u32[]{:S(2)}, u32[]{:S(2)}) async-start(bf16[16,192,256]{2,1,0:T(8,128)(2,1)} %bitcast.46), calls=%async_computation.3 | async-start | bytes 3145728 | tf_op jit(solution)/shard_map/all_to_all | solution.py:306
  76.7 1.3 copy-done.9
  78.0 3.6 %shard_map.125 = f32[4,192,256]{2,1,0:T(8,128)S(1)} custom-call(s32[1]{0:T(128)} %bitcast.pos_ref, bf16[1536,384]{1,0:T(8,128)(2,1)S(1)} %copy-done.9, f32[16,32,128]{2,1,0:T(8,128)S(1)} %all-to-all-done.2.parts_ref, bf16[3072,256]{1,0:T(8,128)(2,1)S(1)} %maximum_dynamic-update-slice_fusion.refs_8_.q_ref), custom_call_target="tpu_custom_call" | custom-call | flops 2415919104 | bytes 2359296 | tf_op jit(solution)/shard_map/pallas_call | solution.py:414
  81.6 2.5 %collective-permute-start.14 = (f32[4,192,256]{2,1,0:T(8,128)S(1)}, f32[4,192,256]{2,1,0:T(8,128)S(1)}, u32[]{:S(2)}, u32[]{:S(2)}) collective-permute-start(f32[4,192,256]{2,1,0:T(8,128)S(1)} %shard_map.125), channel_id=1, source_target_pairs={{0,4},{4,0},{1,5},{5,1},{2,6},{6,2},{3,7},{7,3},{8,12},{12,8},{9,1... | collective-permute-start | bytes 2359304 | tf_op jit(solution)/shard_map/ppermute | solution.py:311
  84.1 3.0 %shard_map.126 = f32[3,192,256]{2,1,0:T(8,128)S(1)} custom-call(s32[1]{0:T(128)} %bitcast.pos_ref, bf16[1536,384]{1,0:T(8,128)(2,1)S(1)} %copy-done.9, f32[16,32,128]{2,1,0:T(8,128)S(1)} %all-to-all-done.2.parts_ref, bf16[3072,256]{1,0:T(8,128)(2,1)S(1)} %maximum_dynamic-update-slice_fusion.refs_8_.q_ref), custom_call_target="tpu_custom_call" | custom-call | flops 1811939328 | bytes 1769472 | tf_op jit(solution)/shard_map/pallas_call | solution.py:414
  87.1 0.1 fusion
  87.2 1.3 collective-permute-start.17
  88.4 1.5 collective-permute-start.15
  89.9 1.5 collective-permute-start.16
  91.4 2.1 %shard_map.127 = f32[1,192,256]{2,1,0:T(8,128)S(1)} custom-call(s32[1]{0:T(128)} %bitcast.pos_ref, bf16[1536,384]{1,0:T(8,128)(2,1)S(1)} %copy-done.9, f32[16,32,128]{2,1,0:T(8,128)S(1)} %all-to-all-done.2.parts_ref, bf16[3072,256]{1,0:T(8,128)(2,1)S(1)} %maximum_dynamic-update-slice_fusion.refs_8_.q_ref), custom_call_target="tpu_custom_call" | custom-call | flops 603979776 | bytes 589824 | tf_op jit(solution)/shard_map/pallas_call | solution.py:414
  93.5 0.7 fusion.2.refs_0_
  94.2 0.5 collective-permute-done.15.refs_1_
  94.7 5.4 %collective-permute-done.16.refs_2_ = f32[192,256]{1,0:T(8,128)S(1)} collective-permute-done((f32[192,256]{1,0:T(8,128)S(1)}, f32[192,256]{1,0:T(8,128)S(1)}, u32[]{:S(2)}, u32[]{:S(2)}) %collective-permute-start.16) | collective-permute-done | bytes 196640 | tf_op jit(solution)/shard_map/ppermute | solution.py:311
  100.1 0.7 copy-done.18
  100.8 1.1 copy-done
  101.9 2.9 %shard_map.128 = bf16[16,2,4,40,128]{4,3,2,1,0:T(8,128)(2,1)} custom-call(f32[192,256]{1,0:T(8,128)} %fusion.2.refs_0_, f32[192,256]{1,0:T(8,128)} %copy-done.17, f32[192,256]{1,0:T(8,128)} %copy-done.18, f32[192,256]{1,0:T(8,128)} %collective-permute-done.17.refs_3_, bf16[192,256]{1,0:T(8,128)(2,1)} %get-tuple-element.31.refs_4_, ...), custom_call_target="tpu_custom_call" | custom-call | tf_op jit(solution)/shard_map/pallas_call | solution.py:444
  104.9 9.7 %all-to-all-start.4 = ((bf16[128,40,128]{2,1,0:T(8,128)(2,1)}), bf16[128,40,128]{2,1,0:T(8,128)(2,1)S(1)}, u32[]{:S(2)}, u32[]{:S(2)}) async-start(bf16[128,40,128]{2,1,0:T(8,128)(2,1)} %bitcast.44), calls=%async_computation.4 | async-start | bytes 2621440 | tf_op jit(solution)/shard_map/all_to_all | solution.py:306
  114.5 0.9 copy-done.10
  115.5 1.4 shard_map.130.active_ref
  116.9 1.3 copy-done.7
  118.3 0.1 constant_dynamic-slice_fusion
  118.4 1.3 shard_map.129
  119.6 17.3 %all-to-all-done.4.got_ref = bf16[128,40,128]{2,1,0:T(8,128)(2,1)S(1)} async-done(((bf16[128,40,128]{2,1,0:T(8,128)(2,1)}), bf16[128,40,128]{2,1,0:T(8,128)(2,1)S(1)}, u32[]{:S(2)}, u32[]{:S(2)}) %all-to-all-start.4) | async-done | bytes 1310752 | tf_op jit(solution)/shard_map/all_to_all | solution.py:306
  136.9 1.1 shard_map.132
  138.0 3.8 %all-to-all-start.5 = ((bf16[128,16,128]{2,1,0:T(8,128)(2,1)}), bf16[128,16,128]{2,1,0:T(8,128)(2,1)S(1)}, u32[]{:S(2)}, u32[]{:S(2)}) async-start(bf16[128,16,128]{2,1,0:T(8,128)(2,1)} %shard_map.132), calls=%async_computation.5 | async-start | bytes 1048576 | tf_op jit(solution)/shard_map/all_to_all | solution.py:306
  141.9 0.1 convert_element_type.38
  142.0 0.7 convert_element_type.40.ids_ref
  142.7 11.2 %shard_map.131 = (f32[2048,256]{1,0:T(8,128)}, f32[2048,256]{1,0:T(8,128)}) custom-call(s32[1,2048]{1,0:T(1,128)} %convert_element_type.40.ids_ref, bf16[128,40,128]{2,1,0:T(8,128)(2,1)} %copy-done.4, f32[2048,256]{1,0:T(8,128)} %table_ref.3, f32[2048,256]{1,0:T(8,128)} %accum_ref.1, bf16[2048,512]{1,0:T(8,128)(2,1)} %copy-done.7, ...), custom_call_target="tpu_custom_call" | custom-call | flops 4294967296 | bytes 8388608 | tf_op jit(solution)/shard_map/pallas_call | solution.py:483
  153.9 2.0 %all-to-all-done.5 = bf16[128,16,128]{2,1,0:T(8,128)(2,1)S(1)} async-done(((bf16[128,16,128]{2,1,0:T(8,128)(2,1)}), bf16[128,16,128]{2,1,0:T(8,128)(2,1)S(1)}, u32[]{:S(2)}, u32[]{:S(2)}) %all-to-all-start.5) | async-done | bytes 524320 | tf_op jit(solution)/shard_map/all_to_all | solution.py:306
  156.0 1.1 fusion.4
  (67 shorter events, 0.5 us)
Async XLA Ops:
  2.3 15.5 %all-to-all-start = ((s32[32,1,128]{2,1,0:T(1,128)}), s32[32,1,128]{2,1,0:T(1,128)S(1)}, u32[]{:S(2)}, u32[]{:S(2)}) async-start(s32[32,1,128]{2,1,0:T(1,128)} %bitcast.43), calls=%async_computation | async-start | bytes 32768 | tf_op jit(solution)/shard_map/all_to_all | solution.py:306
  10.9 0.9 copy-start.12
  11.8 0.7 copy-start.15
  12.5 3.8 %copy-start.19 = (bf16[192]{0:T(256)(128)(2,1)S(1)}, bf16[192]{0:T(256)(128)(2,1)}, u32[]{:S(2)}) copy-start(bf16[192]{0:T(256)(128)(2,1)} %param.11) | copy-start | bytes 1156
  12.5 5.4 %copy-start.2 = (f32[2048,256]{1,0:T(8,128)S(1)}, f32[2048,256]{1,0:T(8,128)}, u32[]{:S(2)}) copy-start(f32[2048,256]{1,0:T(8,128)} %table_ref.3) | copy-start | bytes 6291460
  12.5 14.4 %collective-permute-start.7 = (bf16[192,256]{1,0:T(8,128)(2,1)S(1)}, bf16[192,256]{1,0:T(8,128)(2,1)S(1)}, u32[]{:S(2)}, u32[]{:S(2)}) collective-permute-start(bf16[192,256]{1,0:T(8,128)(2,1)S(1)} %shard_map.121), channel_id=1, source_target_pairs={{0,96},{32,0},{64,32},{96,64},{1,97},{33,1},{65,33},{97,65},{2,98}... | collective-permute-start | bytes 294920 | tf_op jit(solution)/shard_map/ppermute | solution.py:311
  15.2 11.7 %collective-permute-start.8 = (bf16[192,256]{1,0:T(8,128)(2,1)S(1)}, bf16[192,256]{1,0:T(8,128)(2,1)S(1)}, u32[]{:S(2)}, u32[]{:S(2)}) collective-permute-start(bf16[192,256]{1,0:T(8,128)(2,1)S(1)} %shard_map.121), channel_id=1, source_target_pairs={{0,64},{32,96},{64,0},{96,32},{1,65},{33,97},{65,1},{97,33},{2,66}... | collective-permute-start | bytes 294920 | tf_op jit(solution)/shard_map/ppermute | solution.py:311
  15.8 11.1 %collective-permute-start.9 = (bf16[192,256]{1,0:T(8,128)(2,1)S(1)}, bf16[192,256]{1,0:T(8,128)(2,1)S(1)}, u32[]{:S(2)}, u32[]{:S(2)}) collective-permute-start(bf16[192,256]{1,0:T(8,128)(2,1)S(1)} %shard_map.121), channel_id=1, source_target_pairs={{0,32},{32,64},{64,96},{96,0},{1,33},{33,65},{65,97},{97,1},{2,34}... | collective-permute-start | bytes 294920 | tf_op jit(solution)/shard_map/ppermute | solution.py:311
  16.3 10.6 %copy-start.13 = (bf16[192,256]{1,0:T(8,128)(2,1)S(1)}, bf16[192,256]{1,0:T(8,128)(2,1)}, u32[]{:S(2)}) copy-start(bf16[192,256]{1,0:T(8,128)(2,1)} %q_ref.1) | copy-start | bytes 294916
  20.1 15.6 %all-to-all-start.1 = ((bf16[32,16,256]{2,1,0:T(8,128)(2,1)}), bf16[32,16,256]{2,1,0:T(8,128)(2,1)S(1)}, u32[]{:S(2)}, u32[]{:S(2)}) async-start(bf16[32,16,256]{2,1,0:T(8,128)(2,1)} %bitcast.5), calls=%async_computation.1 | async-start | bytes 524288 | tf_op jit(solution)/shard_map/all_to_all | solution.py:306
  27.0 16.2 %collective-permute-start.10 = (bf16[768,256]{1,0:T(8,128)(2,1)S(1)}, bf16[768,256]{1,0:T(8,128)(2,1)S(1)}, u32[]{:S(2)}, u32[]{:S(2)}) collective-permute-start(bf16[768,256]{1,0:T(8,128)(2,1)S(1)} %shard_map.122), channel_id=1, source_target_pairs={{0,3},{1,0},{2,1},{3,2},{4,7},{5,4},{6,5},{7,6},{8,11},{9,8},{10,9... | collective-permute-start | bytes 1179656 | tf_op jit(solution)/shard_map/ppermute | solution.py:311
  30.8 11.4 %collective-permute-start.11 = (bf16[768,256]{1,0:T(8,128)(2,1)S(1)}, bf16[768,256]{1,0:T(8,128)(2,1)S(1)}, u32[]{:S(2)}, u32[]{:S(2)}) collective-permute-start(bf16[768,256]{1,0:T(8,128)(2,1)S(1)} %shard_map.122), channel_id=1, source_target_pairs={{0,1},{1,2},{2,3},{3,0},{4,5},{5,6},{6,7},{7,4},{8,9},{9,10},{10,1... | collective-permute-start | bytes 1179656 | tf_op jit(solution)/shard_map/ppermute | solution.py:311
  35.7 0.7 copy-start.16
  38.8 6.7 %copy-start.11 = (bf16[208,256]{1,0:T(8,128)(2,1)S(1)}, bf16[208,256]{1,0:T(8,128)(2,1)}, u32[]{:S(2)}) copy-start(bf16[208,256]{1,0:T(8,128)(2,1)} %get-tuple-element.24.refs_0_.pay_ref) | copy-start | bytes 319492
  38.8 6.7 %collective-permute-start = (bf16[208,256]{1,0:T(8,128)(2,1)}, bf16[208,256]{1,0:T(8,128)(2,1)S(1)}, u32[]{:S(2)}, u32[]{:S(2)}) collective-permute-start(bf16[208,256]{1,0:T(8,128)(2,1)} %get-tuple-element.24.refs_0_.pay_ref), channel_id=1, source_target_pairs={{0,8},{8,16},{16,24},{24,0},{1,9},{9,17},{17,25},{25,1},{2,10},{10... | collective-permute-start | bytes 319496 | tf_op jit(solution)/shard_map/ppermute | solution.py:311
  39.0 8.9 %collective-permute-start.1 = (bf16[208,256]{1,0:T(8,128)(2,1)}, bf16[208,256]{1,0:T(8,128)(2,1)S(1)}, u32[]{:S(2)}, u32[]{:S(2)}) collective-permute-start(bf16[208,256]{1,0:T(8,128)(2,1)} %get-tuple-element.24.refs_0_.pay_ref), channel_id=1, source_target_pairs={{0,16},{8,24},{16,0},{24,8},{1,17},{9,25},{17,1},{25,9},{2,18},{10... | collective-permute-start | bytes 319496 | tf_op jit(solution)/shard_map/ppermute | solution.py:311
  41.0 7.0 %collective-permute-start.2 = (bf16[208,256]{1,0:T(8,128)(2,1)}, bf16[208,256]{1,0:T(8,128)(2,1)S(1)}, u32[]{:S(2)}, u32[]{:S(2)}) collective-permute-start(bf16[208,256]{1,0:T(8,128)(2,1)} %get-tuple-element.24.refs_0_.pay_ref), channel_id=1, source_target_pairs={{0,24},{8,0},{16,8},{24,16},{1,25},{9,1},{17,9},{25,17},{2,26},{10... | collective-permute-start | bytes 319496 | tf_op jit(solution)/shard_map/ppermute | solution.py:311
  42.2 7.0 %collective-permute-start.13 = (bf16[384,256]{1,0:T(8,128)(2,1)S(1)}, bf16[384,256]{1,0:T(8,128)(2,1)S(1)}, u32[]{:S(2)}, u32[]{:S(2)}) collective-permute-start(bf16[384,256]{1,0:T(8,128)(2,1)S(1)} %slice.61), channel_id=1, source_target_pairs={{0,1},{1,2},{2,3},{3,0},{4,5},{5,6},{6,7},{7,4},{8,9},{9,10},{10,1... | collective-permute-start | bytes 589832 | tf_op jit(solution)/shard_map/ppermute | solution.py:311
  43.2 8.0 %collective-permute-start.12 = (bf16[384,256]{1,0:T(8,128)(2,1)S(1)}, bf16[384,256]{1,0:T(8,128)(2,1)S(1)}, u32[]{:S(2)}, u32[]{:S(2)}) collective-permute-start(bf16[384,256]{1,0:T(8,128)(2,1)S(1)} %slice.60), channel_id=1, source_target_pairs={{0,3},{1,0},{2,1},{3,2},{4,7},{5,4},{6,5},{7,6},{8,11},{9,8},{10,9... | collective-permute-start | bytes 589832 | tf_op jit(solution)/shard_map/ppermute | solution.py:311
  45.5 5.7 %collective-permute-start.3 = (bf16[208,256]{1,0:T(8,128)(2,1)S(1)}, bf16[208,256]{1,0:T(8,128)(2,1)S(1)}, u32[]{:S(2)}, u32[]{:S(2)}) collective-permute-start(bf16[208,256]{1,0:T(8,128)(2,1)S(1)} %copy-done.11), channel_id=1, source_target_pairs={{0,4},{4,0},{1,5},{5,1},{2,6},{6,2},{3,7},{7,3},{8,12},{12,8},{9,1... | collective-permute-start | bytes 319496 | tf_op jit(solution)/shard_map/ppermute | solution.py:311
  47.9 3.3 %collective-permute-start.4 = (bf16[208,256]{1,0:T(8,128)(2,1)S(1)}, bf16[208,256]{1,0:T(8,128)(2,1)S(1)}, u32[]{:S(2)}, u32[]{:S(2)}) collective-permute-start(bf16[208,256]{1,0:T(8,128)(2,1)S(1)} %collective-permute-done.refs_1_), channel_id=1, source_target_pairs={{0,4},{4,0},{1,5},{5,1},{2,6},{6,2},{3,7},{7,3},{8,12},{12,8},{9,1... | collective-permute-start | bytes 319496 | tf_op jit(solution)/shard_map/ppermute | solution.py:311
  48.0 3.3 %collective-permute-start.5 = (bf16[208,256]{1,0:T(8,128)(2,1)S(1)}, bf16[208,256]{1,0:T(8,128)(2,1)S(1)}, u32[]{:S(2)}, u32[]{:S(2)}) collective-permute-start(bf16[208,256]{1,0:T(8,128)(2,1)S(1)} %collective-permute-done.1.refs_2_), channel_id=1, source_target_pairs={{0,4},{4,0},{1,5},{5,1},{2,6},{6,2},{3,7},{7,3},{8,12},{12,8},{9,1... | collective-permute-start | bytes 319496 | tf_op jit(solution)/shard_map/ppermute | solution.py:311
  49.2 3.0 %collective-permute-start.6 = (bf16[208,256]{1,0:T(8,128)(2,1)S(1)}, bf16[208,256]{1,0:T(8,128)(2,1)S(1)}, u32[]{:S(2)}, u32[]{:S(2)}) collective-permute-start(bf16[208,256]{1,0:T(8,128)(2,1)S(1)} %collective-permute-done.2.refs_3_), channel_id=1, source_target_pairs={{0,4},{4,0},{1,5},{5,1},{2,6},{6,2},{3,7},{7,3},{8,12},{12,8},{9,1... | collective-permute-start | bytes 319496 | tf_op jit(solution)/shard_map/ppermute | solution.py:311
  58.3 11.7 %copy-start.8 = (bf16[1536,384]{1,0:T(8,128)(2,1)}, bf16[1536,384]{1,0:T(8,128)(2,1)S(1)}, u32[]{:S(2)}) copy-start(bf16[1536,384]{1,0:T(8,128)(2,1)S(1)} %get-tuple-element.25.rows) | copy-start | bytes 3538948
  58.3 11.7 %all-to-all-start.2 = ((f32[16,32,128]{2,1,0:T(8,128)}), f32[16,32,128]{2,1,0:T(8,128)S(1)}, u32[]{:S(2)}, u32[]{:S(2)}) async-start(f32[16,32,128]{2,1,0:T(8,128)} %get-tuple-element.26), calls=%async_computation.2 | async-start | bytes 524288 | tf_op jit(solution)/shard_map/all_to_all | solution.py:306
  70.0 21.4 %copy-start.5 = (f32[16,32,128]{2,1,0:T(8,128)}, f32[16,32,128]{2,1,0:T(8,128)S(1)}, u32[]{:S(2)}) copy-start(f32[16,32,128]{2,1,0:T(8,128)S(1)} %all-to-all-done.2.parts_ref) | copy-start | bytes 786436
  70.0 30.8 %all-to-all-start.3 = ((bf16[16,192,256]{2,1,0:T(8,128)(2,1)}), bf16[16,192,256]{2,1,0:T(8,128)(2,1)S(1)}, u32[]{:S(2)}, u32[]{:S(2)}) async-start(bf16[16,192,256]{2,1,0:T(8,128)(2,1)} %bitcast.46), calls=%async_computation.3 | async-start | bytes 3145728 | tf_op jit(solution)/shard_map/all_to_all | solution.py:306
  76.7 1.3 copy-start.9
  81.6 5.5 %collective-permute-start.14 = (f32[4,192,256]{2,1,0:T(8,128)S(1)}, f32[4,192,256]{2,1,0:T(8,128)S(1)}, u32[]{:S(2)}, u32[]{:S(2)}) collective-permute-start(f32[4,192,256]{2,1,0:T(8,128)S(1)} %shard_map.125), channel_id=1, source_target_pairs={{0,4},{4,0},{1,5},{5,1},{2,6},{6,2},{3,7},{7,3},{8,12},{12,8},{9,1... | collective-permute-start | bytes 2359304 | tf_op jit(solution)/shard_map/ppermute | solution.py:311
  87.2 13.6 %collective-permute-start.17 = (f32[192,256]{1,0:T(8,128)S(1)}, f32[192,256]{1,0:T(8,128)}, u32[]{:S(2)}, u32[]{:S(2)}) collective-permute-start(f32[192,256]{1,0:T(8,128)S(1)} %get-tuple-element.41), channel_id=1, source_target_pairs={{0,8},{8,16},{16,24},{24,0},{1,9},{9,17},{17,25},{25,1},{2,10},{10... | collective-permute-start | bytes 589832 | tf_op jit(solution)/shard_map/ppermute | solution.py:311
  88.4 6.3 %collective-permute-start.15 = (f32[192,256]{1,0:T(8,128)S(1)}, f32[192,256]{1,0:T(8,128)S(1)}, u32[]{:S(2)}, u32[]{:S(2)}) collective-permute-start(f32[192,256]{1,0:T(8,128)S(1)} %get-tuple-element.40), channel_id=1, source_target_pairs={{0,24},{8,0},{16,8},{24,16},{1,25},{9,1},{17,9},{25,17},{2,26},{10... | collective-permute-start | bytes 589832 | tf_op jit(solution)/shard_map/ppermute | solution.py:311
  89.9 10.2 %collective-permute-start.16 = (f32[192,256]{1,0:T(8,128)S(1)}, f32[192,256]{1,0:T(8,128)S(1)}, u32[]{:S(2)}, u32[]{:S(2)}) collective-permute-start(f32[192,256]{1,0:T(8,128)S(1)} %get-tuple-element.39), channel_id=1, source_target_pairs={{0,16},{8,24},{16,0},{24,8},{1,17},{9,25},{17,1},{25,9},{2,18},{10... | collective-permute-start | bytes 589832 | tf_op jit(solution)/shard_map/ppermute | solution.py:311
  94.7 5.4 %copy-start.17 = (f32[192,256]{1,0:T(8,128)}, f32[192,256]{1,0:T(8,128)S(1)}, u32[]{:S(2)}) copy-start(f32[192,256]{1,0:T(8,128)S(1)} %collective-permute-done.15.refs_1_) | copy-start | bytes 589828
  100.1 0.7 copy-start.18
  100.8 1.1 copy-start
  104.9 9.7 %copy-start.3 = (f32[2048,256]{1,0:T(8,128)S(1)}, f32[2048,256]{1,0:T(8,128)}, u32[]{:S(2)}) copy-start(f32[2048,256]{1,0:T(8,128)} %table_ref.3) | copy-start | bytes 6291460
  104.9 32.1 %all-to-all-start.4 = ((bf16[128,40,128]{2,1,0:T(8,128)(2,1)}), bf16[128,40,128]{2,1,0:T(8,128)(2,1)S(1)}, u32[]{:S(2)}, u32[]{:S(2)}) async-start(bf16[128,40,128]{2,1,0:T(8,128)(2,1)} %bitcast.44), calls=%async_computation.4 | async-start | bytes 2621440 | tf_op jit(solution)/shard_map/all_to_all | solution.py:306
  114.5 1.0 copy-start.10
  115.5 2.7 %slice-start = ((f32[16,32,128]{2,1,0:T(8,128)}), f32[16,24,128]{2,1,0:T(8,128)S(1)}, s32[]{:S(2)}) async-start(f32[16,32,128]{2,1,0:T(8,128)} %copy-done.5), calls=%async_computation.6 | async-start | bytes 393216 | tf_op jit(solution)/shard_map/slice | solution.py:453
  115.5 2.9 %copy-start.1 = (bf16[16,192,256]{2,1,0:T(8,128)(2,1)S(1)}, bf16[16,192,256]{2,1,0:T(8,128)(2,1)}, u32[]{:S(2)}) copy-start(bf16[16,192,256]{2,1,0:T(8,128)(2,1)} %copy-done) | copy-start | bytes 4718596
  115.5 2.9 %copy-start.14 = (bf16[192,256]{1,0:T(8,128)(2,1)S(1)}, bf16[192,256]{1,0:T(8,128)(2,1)}, u32[]{:S(2)}) copy-start(bf16[192,256]{1,0:T(8,128)(2,1)} %q_ref.1) | copy-start | bytes 294916
  116.9 1.3 copy-start.7
  119.6 22.2 %copy-start.6 = (f32[16,32,128]{2,1,0:T(8,128)S(1)}, f32[16,32,128]{2,1,0:T(8,128)}, u32[]{:S(2)}) copy-start(f32[16,32,128]{2,1,0:T(8,128)} %copy-done.5) | copy-start | bytes 786436
  136.9 5.1 %copy-start.4 = (bf16[128,40,128]{2,1,0:T(8,128)(2,1)}, bf16[128,40,128]{2,1,0:T(8,128)(2,1)S(1)}, u32[]{:S(2)}) copy-start(bf16[128,40,128]{2,1,0:T(8,128)(2,1)S(1)} %all-to-all-done.4.got_ref) | copy-start | bytes 3932164
  138.0 17.9 %all-to-all-start.5 = ((bf16[128,16,128]{2,1,0:T(8,128)(2,1)}), bf16[128,16,128]{2,1,0:T(8,128)(2,1)S(1)}, u32[]{:S(2)}, u32[]{:S(2)}) async-start(bf16[128,16,128]{2,1,0:T(8,128)(2,1)} %shard_map.132), calls=%async_computation.5 | async-start | bytes 1048576 | tf_op jit(solution)/shard_map/all_to_all | solution.py:306

commit v7 on v6

--- a/solution.py
+++ b/solution.py
@@ -441,13 +441,14 @@
     parts = [shift(sums[k - 1], "y", 4 - k) for k in range(1, 4)]
     mine = vec_grads(0, 1, sums[2])
     parts = [mine.reshape(PAIRS, E) + from_core[0]] + parts
+    parts[0], o_got = lax.optimization_barrier((parts[0], o_got))
     out = call(
         back_kernel,
         sds((16, 2, 4, PACK, 128), bf16),
         limit=LARGE,
-        in_specs=whole(8) + unread(1),
+        in_specs=whole(8),
         out_specs=whole(1)[0],
-    )(*parts, emb, hid, w_out, place, o_got)
+    )(*parts, emb, hid, w_out, place)
     back = a2a(out.reshape(128, PACK, 128), ALL)
 
     own = lax.dynamic_slice(all_lse[:, :LINES].reshape(NA, QS), (0, here * PAIRS), (NA, PAIRS))

time: 158 us -> 161 us (1.019)
  Pallas kernels: 44.5 us -> 52.3 us
  waiting for transfers between devices: 33 us -> 27.2 us
    pallas_call x3, Pallas kernels: 8.7 us -> 12.7 us  [vec_grads(): call(functools.partial(vec_kernel, first, n), sds((n, PAIRS, E), f32), co...]
    all_to_all x6, waiting for transfers between devices: 24.9 us -> 21.6 us  [a2a(): return lax.all_to_all(x, axes, split_axis=0, concat_axis=0, tiled=True)]
    unnamed x41 -> x29, local copies, waits for them, and re-layouts: 7.76 us -> 4.66 us
    ppermute x18, waiting for transfers between devices: 8.16 us -> 5.61 us  [shift(): return lax.ppermute(x, axis, [(i, (i + k) % n) for i in range(n)])]
    dynamic_update_slice x3, local copies, waits for them, and re-layouts: 0.1 us -> 2.31 us  [local(): all_q = lax.dynamic_update_slice(all_q, block, ((here_z + k) % 4 * QB, 0))]
  transfers between devices with their start and end apart: 24 -> 24, of which waited for: 9 -> 7; matrix products, arithmetic and copies ran while one was open for 3% -> 6% of each run, Pallas kernels for 21% -> 25%
where the time goes in v7:
time: 161 us; the launch traced here: 160 us
  starting transfers between devices  63.7 us (40%)
  Pallas kernels  52.3 us (32%)
  waiting for transfers between devices  27.2 us (17%)
  local copies, waits for them, and re-layouts  13.2 us (8%)
  other arithmetic  2.42 us (2%)
    all_to_all x6, starting transfers between devices, a2a(): return lax.all_to_all(x, axes, split_axis=0, concat_axis=0, tiled=True)  38.6 us
    ppermute x18, starting transfers between devices, shift(): return lax.ppermute(x, axis, [(i, (i + k) % n) for i in range(n)])  25.1 us
    all_to_all x6, waiting for transfers between devices, a2a(): return lax.all_to_all(x, axes, split_axis=0, concat_axis=0, tiled=True)  21.6 us
    pallas_call x3, Pallas kernels, vec_grads(): call(functools.partial(vec_kernel, first, n), sds((n, PAIRS, E), f32), co...  12.7 us
    pallas_call x1, Pallas kernels, local(): call(update_kernel, (sds((ROWS, E), f32), sds((ROWS, E), f32)), cost=(4 *...  11.2 us
    pallas_call x1, Pallas kernels, local(): call(query_kernel, HBM((QS, E), bf16), cost=(4 * VS * QS * E, VS * QS, VS...  8.81 us
    pallas_call x1, Pallas kernels, local(): call(score_kernel, (HBM((NA, SENT, 128), f32), sds((LINES, 128), f32), sd...  7.53 us
    ppermute x18, waiting for transfers between devices, shift(): return lax.ppermute(x, axis, [(i, (i + k) % n) for i in range(n)])  5.61 us
  transfers between devices with their start and end apart: 24, of which 7 were waited for; matrix products, arithmetic and copies ran while one was open for 6% of the time, Pallas kernels for 25%

profile of v7, /device:TPU:1, one launch (start us, length us, event | category | flops | bytes accessed | tf_op | source)
XLA Modules:
  0.0 159.8 jit_solution(6137170320026082899)
XLA Ops:
  0.6 1.7 %shard_map.119 = (s32[32,128]{1,0:T(8,128)}, s32[1,256]{1,0:T(1,128)}, bf16[192,512]{1,0:T(8,128)(2,1)}) custom-call(s32[1,192]{1,0:T(1,128)} %bitcast.52, s32[1,192]{1,0:T(1,128)} %bitcast.53), custom_call_target="tpu_custom_call" | custom-call | tf_op jit(solution)/shard_map/pallas_call | solution.py:329
  2.3 8.6 %all-to-all-start = ((s32[32,1,128]{2,1,0:T(1,128)}), s32[32,1,128]{2,1,0:T(1,128)S(1)}, u32[]{:S(2)}, u32[]{:S(2)}) async-start(s32[32,1,128]{2,1,0:T(1,128)} %bitcast.43), calls=%async_computation | async-start | bytes 32768 | tf_op jit(solution)/shard_map/all_to_all | solution.py:306
  10.9 0.0 copy-start.8
  10.9 0.9 copy-done.8
  11.8 0.7 copy-done.11
  12.5 2.7 %collective-permute-start.7 = (bf16[192,256]{1,0:T(8,128)(2,1)S(1)}, bf16[192,256]{1,0:T(8,128)(2,1)S(1)}, u32[]{:S(2)}, u32[]{:S(2)}) collective-permute-start(bf16[192,256]{1,0:T(8,128)(2,1)S(1)} %shard_map.121), channel_id=1, source_target_pairs={{0,96},{32,0},{64,32},{96,64},{1,97},{33,1},{65,33},{97,65},{2,98}... | collective-permute-start | bytes 294920 | tf_op jit(solution)/shard_map/ppermute | solution.py:311
  15.2 0.5 collective-permute-start.8
  15.8 0.6 collective-permute-start.9
  16.4 0.6 pad.12.freq_ref
  17.0 0.8 all-to-all-done
  17.8 0.1 maximum_reduce_fusion
  17.8 0.1 reshape.111
  17.9 2.2 %gather_fusion = bf16[512,256]{1,0:T(8,128)(2,1)} fusion(f32[2048,256]{1,0:T(8,128)S(1)} %copy-done, s32[1024]{0:T(1024)S(1)} %pad_clamp_fusion), kind=kCustom, calls=%fused_computation | custom fusion | bytes 526336 | tf_op jit(solution)/shard_map/gather | solution.py:353
  20.1 6.6 %all-to-all-start.1 = ((bf16[32,16,256]{2,1,0:T(8,128)(2,1)}), bf16[32,16,256]{2,1,0:T(8,128)(2,1)S(1)}, u32[]{:S(2)}, u32[]{:S(2)}) async-start(bf16[32,16,256]{2,1,0:T(8,128)(2,1)} %bitcast.5), calls=%async_computation.1 | async-start | bytes 524288 | tf_op jit(solution)/shard_map/all_to_all | solution.py:306
  26.8 0.1 convert_element_type.36
  27.0 3.8 %collective-permute-start.10 = (bf16[768,256]{1,0:T(8,128)(2,1)S(1)}, bf16[768,256]{1,0:T(8,128)(2,1)S(1)}, u32[]{:S(2)}, u32[]{:S(2)}) collective-permute-start(bf16[768,256]{1,0:T(8,128)(2,1)S(1)} %shard_map.122), channel_id=1, source_target_pairs={{0,3},{1,0},{2,1},{3,2},{4,7},{5,4},{6,5},{7,6},{8,11},{9,8},{10,9... | collective-permute-start | bytes 1179656 | tf_op jit(solution)/shard_map/ppermute | solution.py:311
  30.8 1.2 broadcast_in_dim.4
  32.0 0.8 constant_dynamic-update-slice_fusion.2
  32.8 2.9 %all-to-all-done.1 = bf16[32,16,256]{2,1,0:T(8,128)(2,1)S(1)} async-done(((bf16[32,16,256]{2,1,0:T(8,128)(2,1)}), bf16[32,16,256]{2,1,0:T(8,128)(2,1)S(1)}, u32[]{:S(2)}, u32[]{:S(2)}) %all-to-all-start.1) | async-done | bytes 262176 | tf_op jit(solution)/shard_map/all_to_all | solution.py:306
  35.7 0.7 copy-done.12
  36.4 2.4 %shard_map.120 = (bf16[192,256]{1,0:T(8,128)(2,1)}, bf16[192,512]{1,0:T(8,128)(2,1)}, bf16[208,256]{1,0:T(8,128)(2,1)}) custom-call(bf16[512,256]{1,0:T(8,128)(2,1)} %bitcast.49, bf16[192,512]{1,0:T(8,128)(2,1)} %get-tuple-element.25.pick_ref, bf16[256,512]{1,0:T(8,128)(2,1)} %w_in_ref.5, bf16[512,256]{1,0:T(8,128)(2,1)} %w_out_ref.3, ...), custom_call_target="tpu_custom_call" | custom-call | flops 25769803776 | bytes 1048576 | tf_op jit(solution)/shard_map/pallas_call | solution.py:370
  38.8 0.2 collective-permute-start
  39.0 1.9 %collective-permute-start.1 = (bf16[208,256]{1,0:T(8,128)(2,1)}, bf16[208,256]{1,0:T(8,128)(2,1)S(1)}, u32[]{:S(2)}, u32[]{:S(2)}) collective-permute-start(bf16[208,256]{1,0:T(8,128)(2,1)} %get-tuple-element.26.refs_0_.pay_ref), channel_id=1, source_target_pairs={{0,16},{8,24},{16,0},{24,8},{1,17},{9,25},{17,1},{25,9},{2,18},{10... | collective-permute-start | bytes 319496 | tf_op jit(solution)/shard_map/ppermute | solution.py:311
  40.9 0.5 collective-permute-start.2
  41.5 0.7 collective-permute-done.11
  42.2 1.0 collective-permute-start.13
  43.2 2.2 %collective-permute-start.12 = (bf16[384,256]{1,0:T(8,128)(2,1)S(1)}, bf16[384,256]{1,0:T(8,128)(2,1)S(1)}, u32[]{:S(2)}, u32[]{:S(2)}) collective-permute-start(bf16[384,256]{1,0:T(8,128)(2,1)S(1)} %slice.60), channel_id=1, source_target_pairs={{0,3},{1,0},{2,1},{3,2},{4,7},{5,4},{6,5},{7,6},{8,11},{9,8},{10,9... | collective-permute-start | bytes 589832 | tf_op jit(solution)/shard_map/ppermute | solution.py:311
  45.4 0.8 constant_dynamic-update-slice_fusion.1
  46.2 0.8 constant_dynamic-update-slice_fusion
  47.0 1.7 %collective-permute-start.3 = (bf16[208,256]{1,0:T(8,128)(2,1)S(1)}, bf16[208,256]{1,0:T(8,128)(2,1)S(1)}, u32[]{:S(2)}, u32[]{:S(2)}) collective-permute-start(bf16[208,256]{1,0:T(8,128)(2,1)S(1)} %copy-done.6), channel_id=1, source_target_pairs={{0,4},{4,0},{1,5},{5,1},{2,6},{6,2},{3,7},{7,3},{8,12},{12,8},{9,1... | collective-permute-start | bytes 319496 | tf_op jit(solution)/shard_map/ppermute | solution.py:311
  48.6 0.1 collective-permute-start.4
  48.7 0.4 collective-permute-start.5
  49.2 2.0 %collective-permute-start.6 = (bf16[208,256]{1,0:T(8,128)(2,1)S(1)}, bf16[208,256]{1,0:T(8,128)(2,1)S(1)}, u32[]{:S(2)}, u32[]{:S(2)}) collective-permute-start(bf16[208,256]{1,0:T(8,128)(2,1)S(1)} %collective-permute-done.2.refs_3_), channel_id=1, source_target_pairs={{0,4},{4,0},{1,5},{5,1},{2,6},{6,2},{3,7},{7,3},{8,12},{12,8},{9,1... | collective-permute-start | bytes 319496 | tf_op jit(solution)/shard_map/ppermute | solution.py:311
  51.2 0.8 maximum_dynamic-update-slice_fusion.refs_8_.q_ref
  52.0 0.2 collective-permute-done.6.refs_7_
  52.1 7.5 %shard_map.123 = (f32[16,32,128]{2,1,0:T(8,128)}, f32[24,128]{1,0:T(8,128)S(1)}, bf16[1536,384]{1,0:T(8,128)(2,1)S(1)}) custom-call(bf16[208,256]{1,0:T(8,128)(2,1)S(1)} %copy-done.6, bf16[208,256]{1,0:T(8,128)(2,1)S(1)} %collective-permute-done.refs_1_, bf16[208,256]{1,0:T(8,128)(2,1)S(1)} %collective-permute-done.1.refs_2_, ...), custom_call_target="tpu_custom_call" | custom-call | flops 2415919104 | bytes 9437184 | tf_op jit(solution)/shard_map/pallas_call | solution.py:380
  59.7 3.9 %all-to-all-start.2 = ((f32[16,32,128]{2,1,0:T(8,128)}), f32[16,32,128]{2,1,0:T(8,128)S(1)}, u32[]{:S(2)}, u32[]{:S(2)}) async-start(f32[16,32,128]{2,1,0:T(8,128)} %get-tuple-element.28), calls=%async_computation.2 | async-start | bytes 524288 | tf_op jit(solution)/shard_map/all_to_all | solution.py:306
  63.6 8.8 %shard_map.124 = bf16[3072,256]{1,0:T(8,128)(2,1)} custom-call(s32[1]{0:T(128)} %bitcast.pos_ref, bf16[1536,384]{1,0:T(8,128)(2,1)S(1)} %get-tuple-element.27.rows, f32[24,128]{1,0:T(8,128)S(1)} %get-tuple-element.29.part_ref, bf16[3072,256]{1,0:T(8,128)(2,1)} %maximum_dynamic-update-slice_fusion.refs_8_.q_ref), custom_call_target="tpu_custom_call" | custom-call | flops 4831838208 | bytes 4718592 | tf_op jit(solution)/shard_map/pallas_call | solution.py:391
  72.4 6.7 %all-to-all-start.3 = ((bf16[16,192,256]{2,1,0:T(8,128)(2,1)}), bf16[16,192,256]{2,1,0:T(8,128)(2,1)}, u32[]{:S(2)}, u32[]{:S(2)}) async-start(bf16[16,192,256]{2,1,0:T(8,128)(2,1)} %bitcast.46), calls=%async_computation.3 | async-start | bytes 3145728 | tf_op jit(solution)/shard_map/all_to_all | solution.py:306
  79.1 4.8 %shard_map.125 = f32[4,192,256]{2,1,0:T(8,128)S(1)} custom-call(s32[1]{0:T(128)} %bitcast.pos_ref, bf16[1536,384]{1,0:T(8,128)(2,1)S(1)} %get-tuple-element.27.rows, f32[16,32,128]{2,1,0:T(8,128)S(1)} %all-to-all-done.2.parts_ref, bf16[3072,256]{1,0:T(8,128)(2,1)} %maximum_dynamic-update-slice_fusion.refs_8_.q_ref), custom_call_target="tpu_custom_call" | custom-call | flops 2415919104 | bytes 2359296 | tf_op jit(solution)/shard_map/pallas_call | solution.py:414
  83.9 3.2 %collective-permute-start.14 = (f32[4,192,256]{2,1,0:T(8,128)S(1)}, f32[4,192,256]{2,1,0:T(8,128)S(1)}, u32[]{:S(2)}, u32[]{:S(2)}) collective-permute-start(f32[4,192,256]{2,1,0:T(8,128)S(1)} %shard_map.125), channel_id=1, source_target_pairs={{0,4},{4,0},{1,5},{5,1},{2,6},{6,2},{3,7},{7,3},{8,12},{12,8},{9,1... | collective-permute-start | bytes 2359304 | tf_op jit(solution)/shard_map/ppermute | solution.py:311
  87.2 4.3 %shard_map.126 = f32[3,192,256]{2,1,0:T(8,128)S(1)} custom-call(s32[1]{0:T(128)} %bitcast.pos_ref, bf16[1536,384]{1,0:T(8,128)(2,1)S(1)} %get-tuple-element.27.rows, f32[16,32,128]{2,1,0:T(8,128)S(1)} %all-to-all-done.2.parts_ref, bf16[3072,256]{1,0:T(8,128)(2,1)} %maximum_dynamic-update-slice_fusion.refs_8_.q_ref), custom_call_target="tpu_custom_call" | custom-call | flops 1811939328 | bytes 1769472 | tf_op jit(solution)/shard_map/pallas_call | solution.py:414
  91.5 0.8 fusion
  92.3 1.2 collective-permute-start.17
  93.5 1.5 collective-permute-start.15
  95.0 1.5 collective-permute-start.16
  96.4 3.6 %shard_map.127 = f32[1,192,256]{2,1,0:T(8,128)S(1)} custom-call(s32[1]{0:T(128)} %bitcast.pos_ref, bf16[1536,384]{1,0:T(8,128)(2,1)S(1)} %get-tuple-element.27.rows, f32[16,32,128]{2,1,0:T(8,128)S(1)} %all-to-all-done.2.parts_ref, bf16[3072,256]{1,0:T(8,128)(2,1)} %maximum_dynamic-update-slice_fusion.refs_8_.q_ref), custom_call_target="tpu_custom_call" | custom-call | flops 603979776 | bytes 589824 | tf_op jit(solution)/shard_map/pallas_call | solution.py:414
  100.1 0.7 fusion.2.refs_0_
  100.8 4.7 %collective-permute-done.16.refs_2_ = f32[192,256]{1,0:T(8,128)} collective-permute-done((f32[192,256]{1,0:T(8,128)}, f32[192,256]{1,0:T(8,128)}, u32[]{:S(2)}, u32[]{:S(2)}) %collective-permute-start.16) | collective-permute-done | bytes 196640 | tf_op jit(solution)/shard_map/ppermute | solution.py:311
  105.5 2.9 %shard_map.128 = bf16[16,2,4,40,128]{4,3,2,1,0:T(8,128)(2,1)} custom-call(f32[192,256]{1,0:T(8,128)} %fusion.2.refs_0_, f32[192,256]{1,0:T(8,128)} %collective-permute-done.15.refs_1_, f32[192,256]{1,0:T(8,128)} %collective-permute-done.16.refs_2_, f32[192,256]{1,0:T(8,128)} %collective-permute-done.17.refs_3_, bf16[192,256]{1,0:T(8,128)(2,1)} %get-tuple-element.34.refs_4_, ...), custom_call_target="tpu_custom_call" | custom-call | tf_op jit(solution)/shard_map/pallas_call | solution.py:445
  108.4 8.9 %all-to-all-start.4 = ((bf16[128,40,128]{2,1,0:T(8,128)(2,1)}), bf16[128,40,128]{2,1,0:T(8,128)(2,1)S(1)}, u32[]{:S(2)}, u32[]{:S(2)}) async-start(bf16[128,40,128]{2,1,0:T(8,128)(2,1)} %bitcast.44), calls=%async_computation.4 | async-start | bytes 2621440 | tf_op jit(solution)/shard_map/all_to_all | solution.py:306
  117.3 0.9 copy-done.5
  118.3 1.4 shard_map.130.active_ref
  119.7 1.3 copy-done.4
  121.1 0.1 constant_dynamic-slice_fusion
  121.2 2.7 %shard_map.129 = f32[192,256]{1,0:T(8,128)} custom-call(bf16[16,192,256]{2,1,0:T(8,128)(2,1)} %all-to-all-done.3.got_ref, f32[16,256]{1,0:T(8,128)S(1)} %pad.14.parts_ref, bf16[192,256]{1,0:T(8,128)(2,1)S(1)} %copy-done.10, bf16[208,256]{1,0:T(8,128)(2,1)S(1)} %copy-done.7), custom_call_target="tpu_custom_call" | custom-call | tf_op jit(solution)/shard_map/pallas_call | solution.py:455
  123.9 15.9 %all-to-all-done.4.got_ref = bf16[128,40,128]{2,1,0:T(8,128)(2,1)S(1)} async-done(((bf16[128,40,128]{2,1,0:T(8,128)(2,1)}), bf16[128,40,128]{2,1,0:T(8,128)(2,1)S(1)}, u32[]{:S(2)}, u32[]{:S(2)}) %all-to-all-start.4) | async-done | bytes 1310752 | tf_op jit(solution)/shard_map/all_to_all | solution.py:306
  139.7 1.1 shard_map.132
  140.8 3.8 %all-to-all-start.5 = ((bf16[128,16,128]{2,1,0:T(8,128)(2,1)}), bf16[128,16,128]{2,1,0:T(8,128)(2,1)S(1)}, u32[]{:S(2)}, u32[]{:S(2)}) async-start(bf16[128,16,128]{2,1,0:T(8,128)(2,1)} %shard_map.132), calls=%async_computation.5 | async-start | bytes 1048576 | tf_op jit(solution)/shard_map/all_to_all | solution.py:306
  144.7 0.1 convert_element_type.38
  144.8 0.7 convert_element_type.40.ids_ref
  145.5 11.2 %shard_map.131 = (f32[2048,256]{1,0:T(8,128)}, f32[2048,256]{1,0:T(8,128)}) custom-call(s32[1,2048]{1,0:T(1,128)} %convert_element_type.40.ids_ref, bf16[128,40,128]{2,1,0:T(8,128)(2,1)} %copy-done.1, f32[2048,256]{1,0:T(8,128)} %table_ref.3, f32[2048,256]{1,0:T(8,128)} %accum_ref.1, bf16[2048,512]{1,0:T(8,128)(2,1)} %copy-done.4, ...), custom_call_target="tpu_custom_call" | custom-call | flops 4294967296 | bytes 8388608 | tf_op jit(solution)/shard_map/pallas_call | solution.py:484
  156.7 2.0 %all-to-all-done.5 = bf16[128,16,128]{2,1,0:T(8,128)(2,1)S(1)} async-done(((bf16[128,16,128]{2,1,0:T(8,128)(2,1)}), bf16[128,16,128]{2,1,0:T(8,128)(2,1)S(1)}, u32[]{:S(2)}, u32[]{:S(2)}) %all-to-all-start.5) | async-done | bytes 524320 | tf_op jit(solution)/shard_map/all_to_all | solution.py:306
  158.7 1.1 fusion.4
  (55 shorter events, 0.4 us)
Async XLA Ops:
  2.3 15.5 %all-to-all-start = ((s32[32,1,128]{2,1,0:T(1,128)}), s32[32,1,128]{2,1,0:T(1,128)S(1)}, u32[]{:S(2)}, u32[]{:S(2)}) async-start(s32[32,1,128]{2,1,0:T(1,128)} %bitcast.43), calls=%async_computation | async-start | bytes 32768 | tf_op jit(solution)/shard_map/all_to_all | solution.py:306
  10.9 0.9 copy-start.8
  11.8 0.7 copy-start.11
  12.5 3.8 %copy-start.13 = (bf16[192]{0:T(256)(128)(2,1)S(1)}, bf16[192]{0:T(256)(128)(2,1)}, u32[]{:S(2)}) copy-start(bf16[192]{0:T(256)(128)(2,1)} %param.11) | copy-start | bytes 1156
  12.5 5.4 %copy-start = (f32[2048,256]{1,0:T(8,128)S(1)}, f32[2048,256]{1,0:T(8,128)}, u32[]{:S(2)}) copy-start(f32[2048,256]{1,0:T(8,128)} %table_ref.3) | copy-start | bytes 6291460
  12.5 14.4 %collective-permute-start.7 = (bf16[192,256]{1,0:T(8,128)(2,1)S(1)}, bf16[192,256]{1,0:T(8,128)(2,1)S(1)}, u32[]{:S(2)}, u32[]{:S(2)}) collective-permute-start(bf16[192,256]{1,0:T(8,128)(2,1)S(1)} %shard_map.121), channel_id=1, source_target_pairs={{0,96},{32,0},{64,32},{96,64},{1,97},{33,1},{65,33},{97,65},{2,98}... | collective-permute-start | bytes 294920 | tf_op jit(solution)/shard_map/ppermute | solution.py:311
  15.2 11.7 %collective-permute-start.8 = (bf16[192,256]{1,0:T(8,128)(2,1)S(1)}, bf16[192,256]{1,0:T(8,128)(2,1)S(1)}, u32[]{:S(2)}, u32[]{:S(2)}) collective-permute-start(bf16[192,256]{1,0:T(8,128)(2,1)S(1)} %shard_map.121), channel_id=1, source_target_pairs={{0,64},{32,96},{64,0},{96,32},{1,65},{33,97},{65,1},{97,33},{2,66}... | collective-permute-start | bytes 294920 | tf_op jit(solution)/shard_map/ppermute | solution.py:311
  15.8 11.1 %collective-permute-start.9 = (bf16[192,256]{1,0:T(8,128)(2,1)S(1)}, bf16[192,256]{1,0:T(8,128)(2,1)S(1)}, u32[]{:S(2)}, u32[]{:S(2)}) collective-permute-start(bf16[192,256]{1,0:T(8,128)(2,1)S(1)} %shard_map.121), channel_id=1, source_target_pairs={{0,32},{32,64},{64,96},{96,0},{1,33},{33,65},{65,97},{97,1},{2,34}... | collective-permute-start | bytes 294920 | tf_op jit(solution)/shard_map/ppermute | solution.py:311
  16.4 10.6 %copy-start.9 = (bf16[192,256]{1,0:T(8,128)(2,1)S(1)}, bf16[192,256]{1,0:T(8,128)(2,1)}, u32[]{:S(2)}) copy-start(bf16[192,256]{1,0:T(8,128)(2,1)} %q_ref.1) | copy-start | bytes 294916
  20.1 15.6 %all-to-all-start.1 = ((bf16[32,16,256]{2,1,0:T(8,128)(2,1)}), bf16[32,16,256]{2,1,0:T(8,128)(2,1)S(1)}, u32[]{:S(2)}, u32[]{:S(2)}) async-start(bf16[32,16,256]{2,1,0:T(8,128)(2,1)} %bitcast.5), calls=%async_computation.1 | async-start | bytes 524288 | tf_op jit(solution)/shard_map/all_to_all | solution.py:306
  27.0 16.2 %collective-permute-start.10 = (bf16[768,256]{1,0:T(8,128)(2,1)S(1)}, bf16[768,256]{1,0:T(8,128)(2,1)S(1)}, u32[]{:S(2)}, u32[]{:S(2)}) collective-permute-start(bf16[768,256]{1,0:T(8,128)(2,1)S(1)} %shard_map.122), channel_id=1, source_target_pairs={{0,3},{1,0},{2,1},{3,2},{4,7},{5,4},{6,5},{7,6},{8,11},{9,8},{10,9... | collective-permute-start | bytes 1179656 | tf_op jit(solution)/shard_map/ppermute | solution.py:311
  30.8 11.4 %collective-permute-start.11 = (bf16[768,256]{1,0:T(8,128)(2,1)S(1)}, bf16[768,256]{1,0:T(8,128)(2,1)S(1)}, u32[]{:S(2)}, u32[]{:S(2)}) collective-permute-start(bf16[768,256]{1,0:T(8,128)(2,1)S(1)} %shard_map.122), channel_id=1, source_target_pairs={{0,1},{1,2},{2,3},{3,0},{4,5},{5,6},{6,7},{7,4},{8,9},{9,10},{10,1... | collective-permute-start | bytes 1179656 | tf_op jit(solution)/shard_map/ppermute | solution.py:311
  35.7 0.7 copy-start.12
  38.8 8.2 %copy-start.6 = (bf16[208,256]{1,0:T(8,128)(2,1)S(1)}, bf16[208,256]{1,0:T(8,128)(2,1)}, u32[]{:S(2)}) copy-start(bf16[208,256]{1,0:T(8,128)(2,1)} %get-tuple-element.26.refs_0_.pay_ref) | copy-start | bytes 319492
  38.8 8.2 %collective-permute-start = (bf16[208,256]{1,0:T(8,128)(2,1)}, bf16[208,256]{1,0:T(8,128)(2,1)S(1)}, u32[]{:S(2)}, u32[]{:S(2)}) collective-permute-start(bf16[208,256]{1,0:T(8,128)(2,1)} %get-tuple-element.26.refs_0_.pay_ref), channel_id=1, source_target_pairs={{0,8},{8,16},{16,24},{24,0},{1,9},{9,17},{17,25},{25,1},{2,10},{10... | collective-permute-start | bytes 319496 | tf_op jit(solution)/shard_map/ppermute | solution.py:311
  39.0 9.6 %collective-permute-start.1 = (bf16[208,256]{1,0:T(8,128)(2,1)}, bf16[208,256]{1,0:T(8,128)(2,1)S(1)}, u32[]{:S(2)}, u32[]{:S(2)}) collective-permute-start(bf16[208,256]{1,0:T(8,128)(2,1)} %get-tuple-element.26.refs_0_.pay_ref), channel_id=1, source_target_pairs={{0,16},{8,24},{16,0},{24,8},{1,17},{9,25},{17,1},{25,9},{2,18},{10... | collective-permute-start | bytes 319496 | tf_op jit(solution)/shard_map/ppermute | solution.py:311
  40.9 7.8 %collective-permute-start.2 = (bf16[208,256]{1,0:T(8,128)(2,1)}, bf16[208,256]{1,0:T(8,128)(2,1)S(1)}, u32[]{:S(2)}, u32[]{:S(2)}) collective-permute-start(bf16[208,256]{1,0:T(8,128)(2,1)} %get-tuple-element.26.refs_0_.pay_ref), channel_id=1, source_target_pairs={{0,24},{8,0},{16,8},{24,16},{1,25},{9,1},{17,9},{25,17},{2,26},{10... | collective-permute-start | bytes 319496 | tf_op jit(solution)/shard_map/ppermute | solution.py:311
  42.2 7.0 %collective-permute-start.13 = (bf16[384,256]{1,0:T(8,128)(2,1)S(1)}, bf16[384,256]{1,0:T(8,128)(2,1)S(1)}, u32[]{:S(2)}, u32[]{:S(2)}) collective-permute-start(bf16[384,256]{1,0:T(8,128)(2,1)S(1)} %slice.61), channel_id=1, source_target_pairs={{0,1},{1,2},{2,3},{3,0},{4,5},{5,6},{6,7},{7,4},{8,9},{9,10},{10,1... | collective-permute-start | bytes 589832 | tf_op jit(solution)/shard_map/ppermute | solution.py:311
  43.2 8.0 %collective-permute-start.12 = (bf16[384,256]{1,0:T(8,128)(2,1)S(1)}, bf16[384,256]{1,0:T(8,128)(2,1)S(1)}, u32[]{:S(2)}, u32[]{:S(2)}) collective-permute-start(bf16[384,256]{1,0:T(8,128)(2,1)S(1)} %slice.60), channel_id=1, source_target_pairs={{0,3},{1,0},{2,1},{3,2},{4,7},{5,4},{6,5},{7,6},{8,11},{9,8},{10,9... | collective-permute-start | bytes 589832 | tf_op jit(solution)/shard_map/ppermute | solution.py:311
  47.0 5.0 %collective-permute-start.3 = (bf16[208,256]{1,0:T(8,128)(2,1)S(1)}, bf16[208,256]{1,0:T(8,128)(2,1)S(1)}, u32[]{:S(2)}, u32[]{:S(2)}) collective-permute-start(bf16[208,256]{1,0:T(8,128)(2,1)S(1)} %copy-done.6), channel_id=1, source_target_pairs={{0,4},{4,0},{1,5},{5,1},{2,6},{6,2},{3,7},{7,3},{8,12},{12,8},{9,1... | collective-permute-start | bytes 319496 | tf_op jit(solution)/shard_map/ppermute | solution.py:311
  48.6 3.3 %collective-permute-start.4 = (bf16[208,256]{1,0:T(8,128)(2,1)S(1)}, bf16[208,256]{1,0:T(8,128)(2,1)S(1)}, u32[]{:S(2)}, u32[]{:S(2)}) collective-permute-start(bf16[208,256]{1,0:T(8,128)(2,1)S(1)} %collective-permute-done.refs_1_), channel_id=1, source_target_pairs={{0,4},{4,0},{1,5},{5,1},{2,6},{6,2},{3,7},{7,3},{8,12},{12,8},{9,1... | collective-permute-start | bytes 319496 | tf_op jit(solution)/shard_map/ppermute | solution.py:311
  48.7 3.2 %collective-permute-start.5 = (bf16[208,256]{1,0:T(8,128)(2,1)S(1)}, bf16[208,256]{1,0:T(8,128)(2,1)S(1)}, u32[]{:S(2)}, u32[]{:S(2)}) collective-permute-start(bf16[208,256]{1,0:T(8,128)(2,1)S(1)} %collective-permute-done.1.refs_2_), channel_id=1, source_target_pairs={{0,4},{4,0},{1,5},{5,1},{2,6},{6,2},{3,7},{7,3},{8,12},{12,8},{9,1... | collective-permute-start | bytes 319496 | tf_op jit(solution)/shard_map/ppermute | solution.py:311
  49.2 3.0 %collective-permute-start.6 = (bf16[208,256]{1,0:T(8,128)(2,1)S(1)}, bf16[208,256]{1,0:T(8,128)(2,1)S(1)}, u32[]{:S(2)}, u32[]{:S(2)}) collective-permute-start(bf16[208,256]{1,0:T(8,128)(2,1)S(1)} %collective-permute-done.2.refs_3_), channel_id=1, source_target_pairs={{0,4},{4,0},{1,5},{5,1},{2,6},{6,2},{3,7},{7,3},{8,12},{12,8},{9,1... | collective-permute-start | bytes 319496 | tf_op jit(solution)/shard_map/ppermute | solution.py:311
  59.7 12.7 %all-to-all-start.2 = ((f32[16,32,128]{2,1,0:T(8,128)}), f32[16,32,128]{2,1,0:T(8,128)S(1)}, u32[]{:S(2)}, u32[]{:S(2)}) async-start(f32[16,32,128]{2,1,0:T(8,128)} %get-tuple-element.28), calls=%async_computation.2 | async-start | bytes 524288 | tf_op jit(solution)/shard_map/all_to_all | solution.py:306
  72.4 24.0 %copy-start.2 = (f32[16,32,128]{2,1,0:T(8,128)}, f32[16,32,128]{2,1,0:T(8,128)S(1)}, u32[]{:S(2)}) copy-start(f32[16,32,128]{2,1,0:T(8,128)S(1)} %all-to-all-done.2.parts_ref) | copy-start | bytes 786436
  72.4 28.4 %all-to-all-start.3 = ((bf16[16,192,256]{2,1,0:T(8,128)(2,1)}), bf16[16,192,256]{2,1,0:T(8,128)(2,1)}, u32[]{:S(2)}, u32[]{:S(2)}) async-start(bf16[16,192,256]{2,1,0:T(8,128)(2,1)} %bitcast.46), calls=%async_computation.3 | async-start | bytes 3145728 | tf_op jit(solution)/shard_map/all_to_all | solution.py:306
  83.9 7.6 %collective-permute-start.14 = (f32[4,192,256]{2,1,0:T(8,128)S(1)}, f32[4,192,256]{2,1,0:T(8,128)S(1)}, u32[]{:S(2)}, u32[]{:S(2)}) collective-permute-start(f32[4,192,256]{2,1,0:T(8,128)S(1)} %shard_map.125), channel_id=1, source_target_pairs={{0,4},{4,0},{1,5},{5,1},{2,6},{6,2},{3,7},{7,3},{8,12},{12,8},{9,1... | collective-permute-start | bytes 2359304 | tf_op jit(solution)/shard_map/ppermute | solution.py:311
  92.3 13.2 %collective-permute-start.17 = (f32[192,256]{1,0:T(8,128)}, f32[192,256]{1,0:T(8,128)}, u32[]{:S(2)}, u32[]{:S(2)}) collective-permute-start(f32[192,256]{1,0:T(8,128)} %get-tuple-element.45), channel_id=1, source_target_pairs={{0,8},{8,16},{16,24},{24,0},{1,9},{9,17},{17,25},{25,1},{2,10},{10... | collective-permute-start | bytes 589832 | tf_op jit(solution)/shard_map/ppermute | solution.py:311
  93.5 7.3 %collective-permute-start.15 = (f32[192,256]{1,0:T(8,128)}, f32[192,256]{1,0:T(8,128)}, u32[]{:S(2)}, u32[]{:S(2)}) collective-permute-start(f32[192,256]{1,0:T(8,128)} %get-tuple-element.44), channel_id=1, source_target_pairs={{0,24},{8,0},{16,8},{24,16},{1,25},{9,1},{17,9},{25,17},{2,26},{10... | collective-permute-start | bytes 589832 | tf_op jit(solution)/shard_map/ppermute | solution.py:311
  95.0 10.5 %collective-permute-start.16 = (f32[192,256]{1,0:T(8,128)}, f32[192,256]{1,0:T(8,128)}, u32[]{:S(2)}, u32[]{:S(2)}) collective-permute-start(f32[192,256]{1,0:T(8,128)} %get-tuple-element.43), channel_id=1, source_target_pairs={{0,16},{8,24},{16,0},{24,8},{1,17},{9,25},{17,1},{25,9},{2,18},{10... | collective-permute-start | bytes 589832 | tf_op jit(solution)/shard_map/ppermute | solution.py:311
  108.4 31.3 %all-to-all-start.4 = ((bf16[128,40,128]{2,1,0:T(8,128)(2,1)}), bf16[128,40,128]{2,1,0:T(8,128)(2,1)S(1)}, u32[]{:S(2)}, u32[]{:S(2)}) async-start(bf16[128,40,128]{2,1,0:T(8,128)(2,1)} %bitcast.44), calls=%async_computation.4 | async-start | bytes 2621440 | tf_op jit(solution)/shard_map/all_to_all | solution.py:306
  117.3 1.0 copy-start.5
  118.3 2.8 %slice-start = ((f32[16,32,128]{2,1,0:T(8,128)}), f32[16,24,128]{2,1,0:T(8,128)S(1)}, s32[]{:S(2)}) async-start(f32[16,32,128]{2,1,0:T(8,128)} %copy-done.2), calls=%async_computation.6 | async-start | bytes 393216 | tf_op jit(solution)/shard_map/slice | solution.py:454
  118.3 2.9 %copy-start.7 = (bf16[208,256]{1,0:T(8,128)(2,1)S(1)}, bf16[208,256]{1,0:T(8,128)(2,1)}, u32[]{:S(2)}) copy-start(bf16[208,256]{1,0:T(8,128)(2,1)} %get-tuple-element.26.refs_0_.pay_ref) | copy-start | bytes 319492
  118.3 2.9 %copy-start.10 = (bf16[192,256]{1,0:T(8,128)(2,1)S(1)}, bf16[192,256]{1,0:T(8,128)(2,1)}, u32[]{:S(2)}) copy-start(bf16[192,256]{1,0:T(8,128)(2,1)} %q_ref.1) | copy-start | bytes 294916
  119.7 1.3 copy-start.4
  123.9 20.8 %copy-start.3 = (f32[16,32,128]{2,1,0:T(8,128)S(1)}, f32[16,32,128]{2,1,0:T(8,128)}, u32[]{:S(2)}) copy-start(f32[16,32,128]{2,1,0:T(8,128)} %copy-done.2) | copy-start | bytes 786436
  139.7 5.1 %copy-start.1 = (bf16[128,40,128]{2,1,0:T(8,128)(2,1)}, bf16[128,40,128]{2,1,0:T(8,128)(2,1)S(1)}, u32[]{:S(2)}) copy-start(bf16[128,40,128]{2,1,0:T(8,128)(2,1)S(1)} %all-to-all-done.4.got_ref) | copy-start | bytes 3932164
  140.8 17.9 %all-to-all-start.5 = ((bf16[128,16,128]{2,1,0:T(8,128)(2,1)}), bf16[128,16,128]{2,1,0:T(8,128)(2,1)S(1)}, u32[]{:S(2)}, u32[]{:S(2)}) async-start(bf16[128,16,128]{2,1,0:T(8,128)(2,1)} %shard_map.132), calls=%async_computation.5 | async-start | bytes 1048576 | tf_op jit(solution)/shard_map/all_to_all | solution.py:306
